TPU v7x, 32 devices: a whole 2x2x4 slice. The times are simulated.
32 devices in a mesh: dp: 2 (over y), row: 4 (over z), col: 4 (over x, core).
Axes of the slice: x: 2, y: 2, z: 4, core: 2. Of those that a mesh axis runs over, the one named last changes fastest.
Arguments:
- image_tokens: bfloat16 [8192, 1536], P(('dp', 'col'), 'row'), may hold values from -6 to 6
- text_tokens: bfloat16 [1232, 1536], P(('dp', 'col'), 'row'), may hold values from -6 to 6
- condition: bfloat16 [8, 1536], P('dp', 'col'), may hold values from -6 to 6
- ada_w: bfloat16 [2, 1536, 6, 1536], P(None, 'col', None, 'row'), may hold values from -0.15625 to 0.15625
- ada_b: bfloat16 [2, 6, 1536], P(None, None, 'row'), may hold values from -3 to 3
- qkv_w: bfloat16 [2, 1536, 3, 1536], P(None, 'row', None, 'col'), may hold values from -0.15625 to 0.15625
- qkv_b: bfloat16 [2, 2, 1536], P(None, None, 'col'), may hold values from -3 to 3
- out_w: bfloat16 [2, 1536, 1536], P(None, 'col', 'row'), may hold values from -0.4375 to 0.4375
- out_b: bfloat16 [2, 1536], P(None, 'row'), may hold values from -3 to 3
- up_w: bfloat16 [2, 1536, 6144], P(None, 'row', 'col'), may hold values from -0.15625 to 0.15625
- up_b: bfloat16 [2, 6144], P(None, 'col'), may hold values from -3 to 3
- down_w: bfloat16 [2, 6144, 1536], P(None, 'col', 'row'), may hold values from -0.078125 to 0.078125
- down_b: bfloat16 [2, 1536], P(None, 'row'), may hold values from -3 to 3
- image_cot: bfloat16 [8192, 1536], P(('dp', 'col'), 'row'), may hold values from -6 to 6
- text_cot: bfloat16 [1232, 1536], P(('dp', 'col'), 'row'), may hold values from -6 to 6
Outputs:
- image_out: bfloat16 [8192, 1536], P(('dp', 'col'), 'row')
- text_out: bfloat16 [1232, 1536], P(('dp', 'col'), 'row')
- image_grad: float32 [8192, 1536], P(('dp', 'col'), 'row')
- text_grad: float32 [1232, 1536], P(('dp', 'col'), 'row')
- condition_grad: float32 [8, 1536], P('dp', 'col')
- grad_ada_w: float32 [2, 1536, 6, 1536], P(None, 'col', None, 'row')
- grad_ada_b: float32 [2, 6, 1536], P(None, None, 'row')
- grad_qkv_w: float32 [2, 1536, 3, 1536], P(None, 'row', None, 'col')
- grad_qkv_b: float32 [2, 2, 1536], P(None, None, 'col')
- grad_out_w: float32 [2, 1536, 1536], P(None, 'col', 'row')
- grad_out_b: float32 [2, 1536], P(None, 'row')
- grad_up_w: float32 [2, 1536, 6144], P(None, 'row', 'col')
- grad_up_b: float32 [2, 6144], P(None, 'col')
- grad_down_w: float32 [2, 6144, 1536], P(None, 'col', 'row')
- grad_down_b: float32 [2, 1536], P(None, 'row')
All inputs are finite; a program needn't handle non-finite values.
Results may differ from a plain program's by a relative error of at most 0.015.
The roundings to bfloat16 on the way count: a program that leaves them out, or rounds other values in their place, can miss the bound.
Values may be sent and summed in bfloat16 or wider, within the bound.
A program may use at most 320 MiB of HBM per device.

v0:
```python
import jax
import jax.numpy as jnp
from jax import lax
from jax.sharding import PartitionSpec as P

D = 1536
HEAD = 64
IMG = 1024
TXT = 154


EPSILON = 1e-06
HIGHEST = lax.Precision.HIGHEST


def product(left, right):
    return jnp.dot(left, right, preferred_element_type=jnp.float32)


def product_left(left, right):
    return lax.dot_general(
        left, right, (((0,), (0,)), ((), ())), preferred_element_type=jnp.float32
    )


def product_right(left, right):
    return lax.dot_general(
        left, right, (((1,), (1,)), ((), ())), preferred_element_type=jnp.float32
    )


def membership(count, length, sequences):
    first = lax.axis_index("col") * count
    owners = (first + lax.iota(jnp.int32, count)) // length
    return (owners[:, None] == lax.iota(jnp.int32, sequences)[None, :]).astype(jnp.float32)


def spread_rows(member, table):
    return jnp.dot(member, table, precision=HIGHEST)


def collect_rows(member, values):
    return lax.dot_general(member, values, (((0,), (0,)), ((), ())), precision=HIGHEST)


def row_totals(image_first, image_second, text_first, text_second):
    return lax.psum(
        (
            jnp.sum(image_first, axis=1),
            jnp.sum(image_second, axis=1),
            jnp.sum(text_first, axis=1),
            jnp.sum(text_second, axis=1),
        ),
        "row",
    )


def normalize(values, total, square):
    mean = total[:, None] / D
    spread = square[:, None] / D - mean * mean
    inverse = lax.rsqrt(spread + EPSILON)
    return ((values - mean) * inverse, inverse)


def normalize_back(grad_norm, normed, inverse, total, cross):
    return inverse * (grad_norm - total[:, None] / D - normed * cross[:, None] / D)


def gelu_value(values):
    return jax.nn.gelu(values, approximate=True)


def gelu_slope(values, grad):
    return jax.vjp(gelu_value, values)[1](grad)[0]


def silu_slope(values, grad):
    return jax.vjp(jax.nn.silu, values)[1](grad)[0]


def gather_tokens(image, text):
    return (
        lax.all_gather(image, "col", axis=0, tiled=True),
        lax.all_gather(text, "col", axis=0, tiled=True),
    )


def sum_to_rows(image, text):
    return (
        lax.psum_scatter(image, "row", scatter_dimension=0, tiled=True),
        lax.psum_scatter(text, "row", scatter_dimension=0, tiled=True),
    )


def gather_features(image, text):
    return (
        lax.all_gather(image, "row", axis=0, tiled=True),
        lax.all_gather(text, "row", axis=0, tiled=True),
    )


def sum_to_columns(image, text):
    return (
        lax.psum_scatter(image, "col", scatter_dimension=0, tiled=True),
        lax.psum_scatter(text, "col", scatter_dimension=0, tiled=True),
    )


def split_heads(values):
    return values.reshape(values.shape[0], values.shape[1] // HEAD, HEAD)


def attend_forward(query, keys, values):
    query_heads = split_heads(query)
    key_heads = split_heads(keys)
    value_heads = split_heads(values)
    scores = jnp.einsum(
        "qhd,khd->hqk", query_heads, key_heads, preferred_element_type=jnp.float32
    ) * HEAD ** (-0.5)
    peak = jnp.max(scores, axis=2, keepdims=True)
    expo = jnp.exp(scores - peak)
    total = jnp.sum(expo, axis=2, keepdims=True)
    prob = (expo / total).astype(jnp.bfloat16)
    attended = jnp.einsum("hqk,khd->qhd", prob, value_heads, preferred_element_type=jnp.float32)
    return (
        attended.reshape(query.shape[0], query.shape[1]).astype(jnp.bfloat16),
        (peak + jnp.log(total))[:, :, 0],
    )


def attend_backward(query, keys, values, logsum, grad_out):
    query_heads = split_heads(query)
    key_heads = split_heads(keys)
    value_heads = split_heads(values)
    grad_heads = split_heads(grad_out)
    scores = jnp.einsum(
        "qhd,khd->hqk", query_heads, key_heads, preferred_element_type=jnp.float32
    ) * HEAD ** (-0.5)
    prob_full = jnp.exp(scores - logsum[:, :, None])
    prob = prob_full.astype(jnp.bfloat16)
    grad_prob = jnp.einsum(
        "qhd,khd->hqk", grad_heads, value_heads, preferred_element_type=jnp.float32
    )
    delta = jnp.sum(prob_full * grad_prob, axis=2, keepdims=True)
    grad_scores = (prob_full * (grad_prob - delta)).astype(jnp.bfloat16)
    grad_query = jnp.einsum(
        "hqk,khd->qhd", grad_scores, key_heads, preferred_element_type=jnp.float32
    ) * HEAD ** (-0.5)
    grad_keys = jnp.einsum(
        "hqk,qhd->khd", grad_scores, query_heads, preferred_element_type=jnp.float32
    ) * HEAD ** (-0.5)
    grad_values = jnp.einsum("hqk,qhd->khd", prob, grad_heads, preferred_element_type=jnp.float32)
    width = query.shape[1]
    return jnp.stack(
        [
            grad_query.reshape(query.shape[0], width),
            grad_keys.reshape(keys.shape[0], width),
            grad_values.reshape(keys.shape[0], width),
        ],
        axis=1,
    )


def shards(
    image_tokens,
    text_tokens,
    condition,
    ada_w,
    ada_b,
    qkv_w,
    qkv_b,
    out_w,
    out_b,
    up_w,
    up_b,
    down_w,
    down_b,
    image_cot,
    text_cot,
):
    seqs = condition.shape[0]
    width_row = image_tokens.shape[1]
    width_col = condition.shape[1]
    image_in = image_tokens.astype(jnp.float32)
    text_in = text_tokens.astype(jnp.float32)
    cond_value = condition.astype(jnp.float32)
    silu_low = jax.nn.silu(cond_value).astype(jnp.bfloat16)
    modul_parts = jnp.stack(
        [
            product(silu_low, ada_w[0].reshape(width_col, 6 * width_row)),
            product(silu_low, ada_w[1].reshape(width_col, 6 * width_row)),
        ]
    )
    mods = lax.psum(modul_parts, "col") + ada_b.astype(jnp.float32).reshape(2, 1, 6 * width_row)
    member_image = membership(image_in.shape[0], IMG, seqs)
    member_text = membership(text_in.shape[0], TXT, seqs)
    modul_image = spread_rows(member_image, mods[0]).reshape(-1, 6, width_row)
    modul_text = spread_rows(member_text, mods[1]).reshape(-1, 6, width_row)
    totals = row_totals(image_in, image_in * image_in, text_in, text_in * text_in)
    norm_image, inverse_image = normalize(image_in, totals[0], totals[1])
    norm_text, inverse_text = normalize(text_in, totals[2], totals[3])
    mixed_image = (norm_image * (1.0 + modul_image[:, 1]) + modul_image[:, 0]).astype(jnp.bfloat16)
    mixed_text = (norm_text * (1.0 + modul_text[:, 1]) + modul_text[:, 0]).astype(jnp.bfloat16)
    full_mixed_image, full_mixed_text = gather_tokens(mixed_image, mixed_text)
    qkv_part_image, qkv_part_text = sum_to_rows(
        product(full_mixed_image, qkv_w[0].reshape(width_row, 3 * width_col)),
        product(full_mixed_text, qkv_w[1].reshape(width_row, 3 * width_col)),
    )
    bias_all = qkv_b.astype(jnp.float32)
    zero_bias = jnp.zeros((width_col,), jnp.float32)
    qkv_image = (
        qkv_part_image.reshape(-1, 3, width_col)
        + jnp.stack([bias_all[0, 0], zero_bias, bias_all[0, 1]])
    ).astype(jnp.bfloat16)
    qkv_text = (
        qkv_part_text.reshape(-1, 3, width_col)
        + jnp.stack([bias_all[1, 0], zero_bias, bias_all[1, 1]])
    ).astype(jnp.bfloat16)
    rows_image = qkv_image.shape[0]
    rows_text = qkv_text.shape[0]
    groups = rows_image // IMG
    seq_image = qkv_image.reshape(groups, IMG, 3, width_col)
    seq_text = qkv_text.reshape(groups, TXT, 3, width_col)

    def forward_group(item):
        part_image, part_text = item
        joint = jnp.concatenate([part_image, part_text], axis=0)
        attended, logsum = attend_forward(joint[:, 0], joint[:, 1], joint[:, 2])
        return (attended[:IMG], attended[IMG:], logsum)

    attn_image_parts, attn_text_parts, logsums = lax.map(forward_group, (seq_image, seq_text))
    attn_image = attn_image_parts.reshape(rows_image, width_col)
    attn_text = attn_text_parts.reshape(rows_text, width_col)
    full_attn_image, full_attn_text = gather_features(attn_image, attn_text)
    proj_image, proj_text = sum_to_columns(
        product(full_attn_image, out_w[0]), product(full_attn_text, out_w[1])
    )
    proj_image = proj_image + out_b[0].astype(jnp.float32)
    proj_text = proj_text + out_b[1].astype(jnp.float32)
    resid_image = image_in + modul_image[:, 2] * proj_image
    resid_text = text_in + modul_text[:, 2] * proj_text
    totals = row_totals(resid_image, resid_image * resid_image, resid_text, resid_text * resid_text)
    norm2_image, inverse2_image = normalize(resid_image, totals[0], totals[1])
    norm2_text, inverse2_text = normalize(resid_text, totals[2], totals[3])
    mixed2_image = (norm2_image * (1.0 + modul_image[:, 4]) + modul_image[:, 3]).astype(
        jnp.bfloat16
    )
    mixed2_text = (norm2_text * (1.0 + modul_text[:, 4]) + modul_text[:, 3]).astype(jnp.bfloat16)
    full_mixed2_image, full_mixed2_text = gather_tokens(mixed2_image, mixed2_text)
    up_part_image = product(full_mixed2_image, up_w[0])
    up_part_text = product(full_mixed2_text, up_w[1])
    up_bias = up_b.astype(jnp.float32)
    pre_image, pre_text = sum_to_rows(up_part_image, up_part_text)
    pre_image = pre_image + up_bias[0]
    pre_text = pre_text + up_bias[1]
    full_hidden_image, full_hidden_text = gather_features(
        gelu_value(pre_image).astype(jnp.bfloat16), gelu_value(pre_text).astype(jnp.bfloat16)
    )
    branch_image, branch_text = sum_to_columns(
        product(full_hidden_image, down_w[0]), product(full_hidden_text, down_w[1])
    )
    branch_image = branch_image + down_b[0].astype(jnp.float32)
    branch_text = branch_text + down_b[1].astype(jnp.float32)
    image_out = (resid_image + modul_image[:, 5] * branch_image).astype(jnp.bfloat16)
    text_out = (resid_text + modul_text[:, 5] * branch_text).astype(jnp.bfloat16)
    cot_image = image_cot.astype(jnp.float32)
    cot_text = text_cot.astype(jnp.float32)
    grad_branch_image = (modul_image[:, 5] * cot_image).astype(jnp.bfloat16)
    grad_branch_text = (modul_text[:, 5] * cot_text).astype(jnp.bfloat16)
    full_branch_image, full_branch_text = gather_tokens(grad_branch_image, grad_branch_text)
    grad_down_w = jnp.stack(
        [
            product_left(full_hidden_image, full_branch_image),
            product_left(full_hidden_text, full_branch_text),
        ]
    )
    grad_down_b = jnp.stack(
        [
            jnp.sum(full_branch_image, axis=0, dtype=jnp.float32),
            jnp.sum(full_branch_text, axis=0, dtype=jnp.float32),
        ]
    )
    grad_hidden_image, grad_hidden_text = sum_to_rows(
        product_right(full_branch_image, down_w[0]), product_right(full_branch_text, down_w[1])
    )
    grad_pre_image = gelu_slope(pre_image, grad_hidden_image).astype(jnp.bfloat16)
    grad_pre_text = gelu_slope(pre_text, grad_hidden_text).astype(jnp.bfloat16)
    full_pre_image, full_pre_text = gather_features(grad_pre_image, grad_pre_text)
    grad_up_w = jnp.stack(
        [
            product_left(full_mixed2_image, full_pre_image),
            product_left(full_mixed2_text, full_pre_text),
        ]
    )
    grad_up_b = jnp.stack(
        [
            jnp.sum(full_pre_image, axis=0, dtype=jnp.float32),
            jnp.sum(full_pre_text, axis=0, dtype=jnp.float32),
        ]
    )
    grad_mixed2_image, grad_mixed2_text = sum_to_columns(
        product_right(full_pre_image, up_w[0]), product_right(full_pre_text, up_w[1])
    )
    grad_norm2_image = grad_mixed2_image * (1.0 + modul_image[:, 4])
    grad_norm2_text = grad_mixed2_text * (1.0 + modul_text[:, 4])
    totals = row_totals(
        grad_norm2_image,
        grad_norm2_image * norm2_image,
        grad_norm2_text,
        grad_norm2_text * norm2_text,
    )
    grad_resid_image = cot_image + normalize_back(
        grad_norm2_image, norm2_image, inverse2_image, totals[0], totals[1]
    )
    grad_resid_text = cot_text + normalize_back(
        grad_norm2_text, norm2_text, inverse2_text, totals[2], totals[3]
    )
    grad_proj_image = (modul_image[:, 2] * grad_resid_image).astype(jnp.bfloat16)
    grad_proj_text = (modul_text[:, 2] * grad_resid_text).astype(jnp.bfloat16)
    full_proj_image, full_proj_text = gather_tokens(grad_proj_image, grad_proj_text)
    grad_out_w = jnp.stack(
        [
            product_left(full_attn_image, full_proj_image),
            product_left(full_attn_text, full_proj_text),
        ]
    )
    grad_out_b = jnp.stack(
        [
            jnp.sum(full_proj_image, axis=0, dtype=jnp.float32),
            jnp.sum(full_proj_text, axis=0, dtype=jnp.float32),
        ]
    )
    grad_attn_image, grad_attn_text = sum_to_rows(
        product_right(full_proj_image, out_w[0]), product_right(full_proj_text, out_w[1])
    )
    grad_attn_image = grad_attn_image.astype(jnp.bfloat16).reshape(groups, IMG, width_col)
    grad_attn_text = grad_attn_text.astype(jnp.bfloat16).reshape(groups, TXT, width_col)

    def backward_group(item):
        part_image, part_text, grad_image, grad_text, logsum = item
        joint = jnp.concatenate([part_image, part_text], axis=0)
        grad_out = jnp.concatenate([grad_image, grad_text], axis=0)
        grads = attend_backward(joint[:, 0], joint[:, 1], joint[:, 2], logsum, grad_out)
        return (grads[:IMG], grads[IMG:])

    qkv_grads_image, qkv_grads_text = lax.map(
        backward_group, (seq_image, seq_text, grad_attn_image, grad_attn_text, logsums)
    )
    grad_qkv_image = qkv_grads_image.reshape(rows_image, 3 * width_col).astype(jnp.bfloat16)
    grad_qkv_text = qkv_grads_text.reshape(rows_text, 3 * width_col).astype(jnp.bfloat16)
    full_qkv_image, full_qkv_text = gather_features(grad_qkv_image, grad_qkv_text)
    grad_qkv_w = jnp.stack(
        [
            product_left(full_mixed_image, full_qkv_image).reshape(width_row, 3, width_col),
            product_left(full_mixed_text, full_qkv_text).reshape(width_row, 3, width_col),
        ]
    )
    sums_image = jnp.sum(full_qkv_image, axis=0, dtype=jnp.float32).reshape(3, width_col)
    sums_text = jnp.sum(full_qkv_text, axis=0, dtype=jnp.float32).reshape(3, width_col)
    grad_qkv_b = jnp.stack(
        [jnp.stack([sums_image[0], sums_image[2]]), jnp.stack([sums_text[0], sums_text[2]])]
    )
    grad_mixed_image, grad_mixed_text = sum_to_columns(
        product_right(full_qkv_image, qkv_w[0].reshape(width_row, 3 * width_col)),
        product_right(full_qkv_text, qkv_w[1].reshape(width_row, 3 * width_col)),
    )
    grad_norm_image = grad_mixed_image * (1.0 + modul_image[:, 1])
    grad_norm_text = grad_mixed_text * (1.0 + modul_text[:, 1])
    totals = row_totals(
        grad_norm_image, grad_norm_image * norm_image, grad_norm_text, grad_norm_text * norm_text
    )
    image_grad = grad_resid_image + normalize_back(
        grad_norm_image, norm_image, inverse_image, totals[0], totals[1]
    )
    text_grad = grad_resid_text + normalize_back(
        grad_norm_text, norm_text, inverse_text, totals[2], totals[3]
    )
    terms_image = jnp.stack(
        [
            grad_mixed_image,
            grad_mixed_image * norm_image,
            grad_resid_image * proj_image,
            grad_mixed2_image,
            grad_mixed2_image * norm2_image,
            cot_image * branch_image,
        ],
        axis=1,
    )
    terms_text = jnp.stack(
        [
            grad_mixed_text,
            grad_mixed_text * norm_text,
            grad_resid_text * proj_text,
            grad_mixed2_text,
            grad_mixed2_text * norm2_text,
            cot_text * branch_text,
        ],
        axis=1,
    )
    modul_grads = jnp.stack(
        [
            collect_rows(member_image, terms_image.reshape(-1, 6 * width_row)),
            collect_rows(member_text, terms_text.reshape(-1, 6 * width_row)),
        ]
    )
    modul_low = lax.psum(modul_grads.astype(jnp.bfloat16), "col")
    grad_ada_b = jnp.sum(modul_low, axis=1, dtype=jnp.float32).reshape(2, 6, width_row)
    grad_ada_w = jnp.stack(
        [
            product_left(silu_low, modul_low[0]).reshape(width_col, 6, width_row),
            product_left(silu_low, modul_low[1]).reshape(width_col, 6, width_row),
        ]
    )
    silu_part = product_right(
        modul_low[0], ada_w[0].reshape(width_col, 6 * width_row)
    ) + product_right(modul_low[1], ada_w[1].reshape(width_col, 6 * width_row))
    silu_grad = lax.psum(silu_part, "row")
    condition_grad = silu_slope(cond_value, silu_grad)
    summed = (
        lax.psum(grad_ada_w.astype(jnp.bfloat16), "dp").astype(jnp.float32),
        lax.psum(grad_ada_b.astype(jnp.bfloat16), "dp").astype(jnp.float32),
        lax.psum(grad_qkv_w.astype(jnp.bfloat16), "dp").astype(jnp.float32),
        lax.psum(grad_qkv_b.astype(jnp.bfloat16), "dp").astype(jnp.float32),
        lax.psum(grad_out_w.astype(jnp.bfloat16), "dp").astype(jnp.float32),
        lax.psum(grad_out_b.astype(jnp.bfloat16), "dp").astype(jnp.float32),
        lax.psum(grad_up_w.astype(jnp.bfloat16), "dp").astype(jnp.float32),
        lax.psum(grad_up_b.astype(jnp.bfloat16), "dp").astype(jnp.float32),
        lax.psum(grad_down_w.astype(jnp.bfloat16), "dp").astype(jnp.float32),
        lax.psum(grad_down_b.astype(jnp.bfloat16), "dp").astype(jnp.float32),
    )
    return (
        image_out,
        text_out,
        image_grad,
        text_grad,
        condition_grad,
        summed[0],
        summed[1],
        summed[2],
        summed[3],
        summed[4],
        summed[5],
        summed[6],
        summed[7],
        summed[8],
        summed[9],
    )


def solution(mesh):
    placed = (
        P(("dp", "col"), "row"),
        P(("dp", "col"), "row"),
        P("dp", "col"),
        P(None, "col", None, "row"),
        P(None, None, "row"),
        P(None, "row", None, "col"),
        P(None, None, "col"),
        P(None, "col", "row"),
        P(None, "row"),
        P(None, "row", "col"),
        P(None, "col"),
        P(None, "col", "row"),
        P(None, "row"),
        P(("dp", "col"), "row"),
        P(("dp", "col"), "row"),
    )
    return jax.shard_map(
        shards,
        mesh=mesh,
        in_specs=placed,
        out_specs=(
            P(("dp", "col"), "row"),
            P(("dp", "col"), "row"),
            P(("dp", "col"), "row"),
            P(("dp", "col"), "row"),
            P("dp", "col"),
            P(None, "col", None, "row"),
            P(None, None, "row"),
            P(None, "row", None, "col"),
            P(None, None, "col"),
            P(None, "col", "row"),
            P(None, "row"),
            P(None, "row", "col"),
            P(None, "col"),
            P(None, "col", "row"),
            P(None, "row"),
        ),
        check_vma=False,
    )
```

profile of v0, /device:TPU:0, one launch (start us, length us, event | category | flops | bytes accessed | tf_op | source)
XLA Modules:
  0.0 3190.3 jit_solution(12685752954052986180)
XLA Ops:
  19.1 20.4 all-reduce.19
  39.5 9.8 all-reduce.27.cloned.1.call-done
  63.0 26.7 all-gather.20.cloned.1.call-done
  89.8 10.9 fusion.180
  104.9 7.7 all-gather
  118.2 106.3 %fusion = f32[160,1152]{1,0:T(8,128)} fusion(f32[616,1152]{1,0:T(8,128)} %fusion.181), kind=kCustom, calls=%all-reduce-scatter | all-reduce-scatter fusion | flops 737281 | bytes 3576320
  225.4 13.3 collective-permute-start
  250.7 212.4 %reduce-scatter.25.cloned.1.call-done = f32[1024,1152]{1,0:T(8,128)} async-done(((f32[4096,1152]{1,0:T(8,128)}), f32[1024,1152]{1,0:T(8,128)}) %reduce-scatter.25.cloned.1.call-update) | async-done | bytes 4718608 | tf_op jit(solution)/shard_map/reduce_scatter | solution.py:90
  463.1 6.0 copy.150
  472.2 14.2 fusion.179
  486.4 14.6 fusion.8
  501.0 14.5 fusion.28
  517.5 65.5 %all-gather.22.cloned.1.call-done = bf16[4096,384]{0,1:T(8,128)(2,1)} async-done(((bf16[1024,384]{0,1:T(8,128)(2,1)}), bf16[4096,384]{0,1:T(8,128)(2,1)}) %all-gather.22.cloned.1.call-update) | async-done | bytes 3145744 | tf_op jit(solution)/shard_map/all_gather | solution.py:97
  583.0 6.4 fusion.97
  590.5 16.3 all-gather.1
  609.3 24.0 fusion.1
  642.7 11.8 reduce-scatter.27.cloned.1.call-done
  656.9 18.5 all-reduce.18
  680.6 25.8 all-gather.24.cloned.1.call-done
  706.4 14.2 fusion.67
  720.7 16.5 all-gather.28.cloned.1.call-done
  737.2 14.4 fusion.61
  752.3 401.8 %reduce-scatter.29.cloned.1.call-done = f32[1024,1536]{1,0:T(8,128)} async-done(((f32[4096,1536]{1,0:T(8,128)}), f32[1024,1536]{1,0:T(8,128)}) %reduce-scatter.29.cloned.1.call-update) | async-done | bytes 6291472 | tf_op jit(solution)/shard_map/reduce_scatter | solution.py:90
  1154.1 418.6 %reduce-scatter.33.cloned.1.call-done = f32[1024,1536]{1,0:T(8,128)} async-done(((f32[4096,1536]{1,0:T(8,128)}), f32[1024,1536]{1,0:T(8,128)}) %reduce-scatter.33.cloned.1.call-update) | async-done | bytes 6291472 | tf_op jit(solution)/shard_map/reduce_scatter | solution.py:90
  1572.7 9.2 fusion.20
  1584.1 7.4 all-gather.4
  1593.5 8.6 all-gather.2
  1611.7 264.7 %fusion.170 = (f32[160,1536]{1,0:T(8,128)}, f32[160,1536]{1,0:T(8,128)}) fusion(f32[616,1536]{1,0:T(8,128)} %fusion.59, f32[616,1536]{1,0:T(8,128)} %fusion.53), kind=kCustom, calls=%all-reduce-scatter.9 | all-reduce-scatter fusion | flops 1966081 | bytes 9536000
  1877.3 35.9 %collective-permute-start.4 = (f32[18,1536]{1,0:T(8,128)S(1)}, f32[18,1536]{1,0:T(8,128)}, u32[]{:S(2)}, u32[]{:S(2)}) collective-permute-start(f32[18,1536]{1,0:T(8,128)S(1)} %slice.288), channel_id=1, source_target_pairs={{0,4},{4,8},{8,12},{1,5},{5,9},{9,13},{2,6},{6,10},{10,14},{3,7},{... | collective-permute-start | bytes 331784
  1914.8 9.6 collective-permute-start.2
  1924.4 6.0 concatenate.23
  1930.4 6.0 concatenate.21
  1939.8 11.2 fusion.65
  1951.1 200.1 %all-gather.26.cloned.1.call-done = bf16[4096,1536]{1,0:T(8,128)(2,1)} async-done(((bf16[1024,1536]{1,0:T(8,128)(2,1)}), bf16[4096,1536]{1,0:T(8,128)(2,1)}) %all-gather.26.cloned.1.call-update) | async-done | bytes 12582928 | tf_op jit(solution)/shard_map/all_gather | solution.py:97
  2151.2 10.1 fusion.63
  2161.8 33.3 %all-gather.38.cloned.1.call-done = bf16[4,154,1536]{2,1,0:T(8,128)(2,1)} async-done(((bf16[1,154,1536]{2,1,0:T(8,128)(2,1)}), bf16[4,154,1536]{2,1,0:T(8,128)(2,1)}) %all-gather.38.cloned.1.call-update) | async-done | bytes 1892368 | tf_op jit(solution)/shard_map/all_gather | solution.py:98
  2202.3 15.0 fusion.5
  2224.9 30.7 reduce-scatter.35.cloned.1.call-done
  2258.6 19.9 all-reduce.17
  2279.8 37.0 %reduce-scatter.31.cloned.1.call-done = f32[1024,384]{0,1:T(8,128)} async-done(((f32[4096,384]{0,1:T(8,128)}), f32[1024,384]{0,1:T(8,128)}) %reduce-scatter.31.cloned.1.call-update) | async-done | bytes 1572880 | tf_op jit(solution)/shard_map/reduce_scatter | solution.py:104
  2316.8 5.7 multiply_convert_fusion.2
  2322.5 28.6 all-gather.32.cloned.1.call-done
  2351.1 6.8 fusion.95
  2360.7 7.0 all-gather.6
  2368.3 41.3 %fusion.6 = f32[160,384]{1,0:T(8,128)S(1)} fusion(f32[616,384]{1,0:T(8,128)S(1)} %fusion.91), kind=kCustom, calls=%all-reduce-scatter.6 | all-reduce-scatter fusion | flops 245761 | bytes 1192448
  2414.7 70.0 %reduce-scatter.37.cloned.1.call-done = f32[1024,384]{1,0:T(8,128)} async-done(((f32[4096,384]{1,0:T(8,128)}), f32[1024,384]{1,0:T(8,128)}) %reduce-scatter.37.cloned.1.call-update) | async-done | bytes 1572880 | tf_op jit(solution)/shard_map/reduce_scatter | solution.py:90
  2486.5 14.5 fusion.10
  2500.9 26.7 multiply_reduce_fusion
  2527.6 30.0 multiply_convert_fusion
  2557.6 11.6 convolution_multiply_fusion.1
  2569.3 9.7 convolution_multiply_fusion.2
  2584.8 164.0 %all-gather.34.cloned.1.call-done = bf16[4096,1152]{0,1:T(8,128)(2,1)} async-done(((bf16[1024,1152]{0,1:T(8,128)(2,1)}), bf16[4096,1152]{0,1:T(8,128)(2,1)}) %all-gather.34.cloned.1.call-update) | async-done | bytes 9437200 | tf_op jit(solution)/shard_map/all_gather | solution.py:97
  2748.7 11.0 fusion.182
  2759.9 32.7 %all-gather.36.cloned.1.call-done = bf16[4,154,1536]{2,1,0:T(8,128)(2,1)} async-done(((bf16[1,154,1536]{2,1,0:T(8,128)(2,1)}), bf16[4,154,1536]{2,1,0:T(8,128)(2,1)}) %all-gather.36.cloned.1.call-update) | async-done | bytes 1892368 | tf_op jit(solution)/shard_map/all_gather | solution.py:98
  2801.3 9.3 fusion.24
  2813.5 7.0 fusion.25
  2832.3 22.4 fusion.169
  2868.0 7.8 convolution_convert_fusion.7
  2879.1 10.3 reduce-scatter.39.cloned.1.call-done
  2902.6 11.8 psum.220
  2923.5 6.9 reduce.5
  2949.9 18.7 all-reduce.16
  2975.3 9.2 all-reduce.20
  2989.0 177.7 %all-reduce.29.cloned.1.call-done = (bf16[2,384,3,384]{1,3,2,0:T(8,128)(2,1)}, bf16[2,384,6,384]{3,1,2,0:T(8,128)(2,1)}, bf16[2,384,384]{2,1,0:T(8,128)(2,1)}, b...) async-done(((bf16[2,384,3,384]{1,3,2,0:T(8,128)(2,1)}, bf16[2,384,6,384]{3,1,2,0:T(8,128)(2,1)}, bf16[2,384,384]{2,1,0:T(8,128)(2,1)}, bf16[2,384,1536]{2,1,0:T(8,128)(2,1)}, ...) | async-done | bytes 10616848 | tf_op jit(solution)/shard_map/psum | solution.py:422
  (448 shorter events, 237.0 us)
Async XLA Ops:
  7.2 42.2 %all-reduce.27.cloned.1.call-start = ((), (), s32[]{:S(2)}) async-start(), calls=%async_computation.8 | async-start | bytes 147456 | tf_op jit(solution)/shard_map/psum | solution.py:194
  15.9 23.6 copy-start.91
  17.2 72.6 %all-gather.20.cloned.1.call-start = ((), (), s32[]{:S(2)}) async-start(), calls=%async_computation.9 | async-start | bytes 3932160 | tf_op jit(solution)/shard_map/all_gather | solution.py:83
  18.8 635.7 %copy-start.3 = (bf16[1024,384]{0,1:T(8,128)(2,1)}, bf16[1024,384]{0,1:T(8,128)(2,1)S(1)}, u32[]{:S(2)}) copy-start(bf16[1024,384]{0,1:T(8,128)(2,1)S(1)} %copy.145) | copy-start | bytes 2359300
  39.5 14.7 copy-start.70
  39.5 14.7 copy-start.72
  39.5 14.7 copy-start.76
  59.2 403.9 %reduce-scatter.25.cloned.1.call-start = ((), (), s32[]{:S(2)}) async-start(), calls=%async_computation.10 | async-start | bytes 23592960 | tf_op jit(solution)/shard_map/reduce_scatter | solution.py:90
  100.8 482.2 %all-gather.22.cloned.1.call-start = ((), (), s32[]{:S(2)}) async-start(), calls=%async_computation.11 | async-start | bytes 3932160 | tf_op jit(solution)/shard_map/all_gather | solution.py:97
  103.8 14.4 copy-start.38
  103.9 14.3 copy-start.95
  103.9 14.3 copy-start.78
  103.9 14.2 copy-start.80
  104.7 536.3 %copy-start.18 = (f32[154,6,384]{2,0,1:T(8,128)}, f32[154,6,384]{2,0,1:T(8,128)S(1)}, u32[]{:S(2)}) copy-start(f32[154,6,384]{2,0,1:T(8,128)S(1)} %fusion.149) | copy-start | bytes 4257796
  118.1 120.6 %copy-start.105 = (u32[32]{0:T(128)S(1)}, u32[32]{0:T(128)}, u32[]{:S(2)}) copy-start(u32[32]{0:T(128)} %constant.143) | copy-start | bytes 388
  225.4 18.6 collective-permute-start
  472.2 28.8 copy-start.31
  500.9 14.5 copy-start.64
  516.4 66.6 %copy-start.47 = (bf16[2,384,384]{2,1,0:T(8,128)(2,1)S(1)}, bf16[2,384,384]{2,1,0:T(8,128)(2,1)}, u32[]{:S(2)}) copy-start(bf16[2,384,384]{2,1,0:T(8,128)(2,1)} %param.22) | copy-start | bytes 1769476
  517.4 137.1 %reduce-scatter.27.cloned.1.call-start = ((), (), s32[]{:S(2)}) async-start(), calls=%async_computation.12 | async-start | bytes 7864320 | tf_op jit(solution)/shard_map/reduce_scatter | solution.py:104
  589.5 116.9 %all-gather.24.cloned.1.call-start = ((), (), s32[]{:S(2)}) async-start(), calls=%async_computation.13 | async-start | bytes 3932160 | tf_op jit(solution)/shard_map/all_gather | solution.py:83
  606.8 28.6 copy-start.92
  606.8 29.2 copy-start.104
  609.3 31.7 copy-start.29
  634.1 4.6 collective-permute-start.1
  636.0 18.6 copy-start.87
  638.7 36.8 %copy-start.15 = (bf16[1024,384]{0,1:T(8,128)(2,1)}, bf16[1024,384]{0,1:T(8,128)(2,1)S(1)}, u32[]{:S(2)}) copy-start(bf16[1024,384]{0,1:T(8,128)(2,1)S(1)} %copy.158) | copy-start | bytes 2359300
  656.9 1659.8 %copy-start.1 = (f32[1024,384]{0,1:T(8,128)}, f32[1024,384]{0,1:T(8,128)S(1)}, u32[]{:S(2)}) copy-start(f32[1024,384]{0,1:T(8,128)S(1)} %get-tuple-element.195) | copy-start | bytes 4718596
  679.8 57.3 %all-gather.28.cloned.1.call-start = ((), (), s32[]{:S(2)}) async-start(), calls=%async_computation.17 | async-start | bytes 3932160 | tf_op jit(solution)/shard_map/all_gather | solution.py:83
  680.6 473.5 %reduce-scatter.29.cloned.1.call-start = ((), (), s32[]{:S(2)}) async-start(), calls=%async_computation.14 | async-start | bytes 31457280 | tf_op jit(solution)/shard_map/reduce_scatter | solution.py:90
  720.6 852.0 %reduce-scatter.33.cloned.1.call-start = ((), (), s32[]{:S(2)}) async-start(), calls=%async_computation.18 | async-start | bytes 31457280 | tf_op jit(solution)/shard_map/reduce_scatter | solution.py:90
  751.6 1188.3 %all-gather.30.cloned.1.call-start = ((), (), s32[]{:S(2)}) async-start(), calls=%async_computation.19 | async-start | bytes 15728640 | tf_op jit(solution)/shard_map/all_gather | solution.py:97
  1582.0 569.2 %all-gather.26.cloned.1.call-start = ((), (), s32[]{:S(2)}) async-start(), calls=%async_computation.15 | async-start | bytes 15728640 | tf_op jit(solution)/shard_map/all_gather | solution.py:97
  1582.7 612.4 %all-gather.38.cloned.1.call-start = ((), (), s32[]{:S(2)}) async-start(), calls=%async_computation.26 | async-start | bytes 2457600 | tf_op jit(solution)/shard_map/all_gather | solution.py:98
  1582.8 639.8 %copy-start.82 = (f32[154]{0:T(256)}, f32[154]{0:T(256)S(1)}, u32[]{:S(2)}) copy-start(f32[154]{0:T(256)S(1)} %get-tuple-element.230) | copy-start | bytes 1852
  1582.8 639.8 %copy-start.84 = (f32[154]{0:T(256)}, f32[154]{0:T(256)S(1)}, u32[]{:S(2)}) copy-start(f32[154]{0:T(256)S(1)} %get-tuple-element.231) | copy-start | bytes 1852
  1877.3 47.1 %collective-permute-start.4 = (f32[18,1536]{1,0:T(8,128)S(1)}, f32[18,1536]{1,0:T(8,128)}, u32[]{:S(2)}, u32[]{:S(2)}) collective-permute-start(f32[18,1536]{1,0:T(8,128)S(1)} %slice.288), channel_id=1, source_target_pairs={{0,4},{4,8},{8,12},{1,5},{5,9},{9,13},{2,6},{6,10},{10,14},{3,7},{... | collective-permute-start | bytes 331784
  1914.8 15.6 collective-permute-start.2
  1939.7 315.8 %reduce-scatter.35.cloned.1.call-start = ((), (), s32[]{:S(2)}) async-start(), calls=%async_computation.20 | async-start | bytes 7864320 | tf_op jit(solution)/shard_map/reduce_scatter | solution.py:104
  1951.1 365.7 %reduce-scatter.31.cloned.1.call-start = ((), (), s32[]{:S(2)}) async-start(), calls=%async_computation.16 | async-start | bytes 7864320 | tf_op jit(solution)/shard_map/reduce_scatter | solution.py:104
  2161.4 189.8 %all-gather.32.cloned.1.call-start = ((), (), s32[]{:S(2)}) async-start(), calls=%async_computation.21 | async-start | bytes 3932160 | tf_op jit(solution)/shard_map/all_gather | solution.py:83
  2198.4 21.1 copy-start.93
  2218.1 2.1 collective-permute-start.5
  2255.6 61.2 %copy-start.6 = (f32[1024,384]{0,1:T(8,128)S(1)}, f32[1024,384]{0,1:T(8,128)}, u32[]{:S(2)}) copy-start(f32[1024,384]{0,1:T(8,128)} %reduce-scatter.35.cloned.1.call-done) | copy-start | bytes 4718596
  2322.4 162.2 %reduce-scatter.37.cloned.1.call-start = ((), (), s32[]{:S(2)}) async-start(), calls=%async_computation.22 | async-start | bytes 7864320 | tf_op jit(solution)/shard_map/reduce_scatter | solution.py:90
  2357.9 390.8 %all-gather.34.cloned.1.call-start = ((), (), s32[]{:S(2)}) async-start(), calls=%async_computation.23 | async-start | bytes 11796480 | tf_op jit(solution)/shard_map/all_gather | solution.py:97
  2367.7 44.8 %copy-start.25 = (bf16[4,154,384]{2,1,0:T(8,128)(2,1)}, bf16[4,154,384]{2,1,0:T(8,128)(2,1)S(1)}, u32[]{:S(2)}) copy-start(bf16[4,154,384]{2,1,0:T(8,128)(2,1)S(1)} %all-gather.6) | copy-start | bytes 1419268
  2367.7 44.8 %copy-start.65 = (f32[6,1178]{1,0:T(8,128)S(1)}, f32[6,1178]{1,0:T(8,128)}, u32[]{:S(2)}) copy-start(f32[6,1178]{1,0:T(8,128)} %copy-done.64) | copy-start | bytes 84820
  2367.8 46.9 %copy-start.58 = (bf16[616,384]{1,0:T(8,128)(2,1)}, bf16[616,384]{1,0:T(8,128)(2,1)S(1)}, u32[]{:S(2)}) copy-start(bf16[616,384]{1,0:T(8,128)(2,1)S(1)} %reshape.241) | copy-start | bytes 1419268
  2409.7 4.4 collective-permute-start.6
  2486.4 14.5 copy-start.32
  2527.6 30.0 copy-start.12
  2581.1 211.5 %all-gather.36.cloned.1.call-start = ((), (), s32[]{:S(2)}) async-start(), calls=%async_computation.25 | async-start | bytes 2457600 | tf_op jit(solution)/shard_map/all_gather | solution.py:98
  2581.7 246.9 %all-gather.40.cloned.1.call-start = ((), (), s32[]{:S(2)}) async-start(), calls=%async_computation.27 | async-start | bytes 1843200 | tf_op jit(solution)/shard_map/all_gather | solution.py:98
  2584.7 304.6 %reduce-scatter.39.cloned.1.call-start = ((), (), s32[]{:S(2)}) async-start(), calls=%async_computation.24 | async-start | bytes 7864320 | tf_op jit(solution)/shard_map/reduce_scatter | solution.py:104
  2759.8 36.1 %copy-start.42 = (bf16[616,384]{1,0:T(8,128)(2,1)S(1)}, bf16[616,384]{1,0:T(8,128)(2,1)}, u32[]{:S(2)}) copy-start(bf16[616,384]{1,0:T(8,128)(2,1)} %reshape.233) | copy-start | bytes 1419268
  2759.8 36.1 %copy-start.54 = (bf16[616,1536]{1,0:T(8,128)(2,1)S(1)}, bf16[616,1536]{1,0:T(8,128)(2,1)}, u32[]{:S(2)}) copy-start(bf16[616,1536]{1,0:T(8,128)(2,1)} %reshape.239) | copy-start | bytes 5677060
  2759.8 406.9 %all-reduce.29.cloned.1.call-start = ((), (), s32[]{:S(2)}) async-start(), calls=%async_computation.28 | async-start | bytes 21233664 | tf_op jit(solution)/shard_map/psum | solution.py:422
  2832.3 27.8 copy-start.56
  2854.7 9.1 collective-permute-start.7
  2856.0 8.2 collective-permute-start.3
  2898.3 16.2 copy-start.75
  2972.3 15.9 copy-start.51
  2972.3 15.9 copy-start.63
  (75 other events, 260.9 us)
Sparse Core Ops, SparseCore 0:
  17.3 32.0 all-reduce.26
  59.3 30.4 all-gather.19
  100.9 362.1 reduce-scatter.24
  517.6 65.4 all-gather.21
  589.6 64.9 reduce-scatter.26
  679.9 26.3 all-gather.23
  708.6 28.5 all-gather.27
  739.7 414.3 reduce-scatter.28
  1156.4 416.1 reduce-scatter.32
  1582.0 347.9 all-gather.29
  1931.6 219.5 all-gather.25
  2153.3 41.7 all-gather.37
  2198.3 57.1 reduce-scatter.34
  2258.0 58.7 reduce-scatter.30
  2322.6 28.5 all-gather.31
  2358.1 126.5 reduce-scatter.36
  2581.2 167.4 all-gather.33
  2750.8 41.7 all-gather.35
  2794.2 34.3 all-gather.39
  2831.7 57.5 reduce-scatter.38
  2918.2 248.4 all-reduce.28
where the time goes:
time: 3200 us; the launch traced here: 3190 us
  waiting for transfers between devices  1980 us (62%)
  blocking collectives  619 us (19%)
  matrix products  244 us (8%)
  other arithmetic  145 us (5%)
  local copies, waits for them, and re-layouts  110 us (3%)
  starting transfers between devices  70.9 us (2%)
    reduce_scatter x4, waiting for transfers between devices, sum_to_rows(): lax.psum_scatter(image, 'row', scatter_dimension=0, tiled=True)  1100 us
    unnamed x6, blocking collectives  474 us
    all_gather x4, waiting for transfers between devices, gather_features(): lax.all_gather(image, 'row', axis=0, tiled=True)  430 us
    psum x1, waiting for transfers between devices, shards(): lax.psum(grad_qkv_w.astype(jnp.bfloat16), 'dp').astype(jnp.float32)  178 us
    all_gather x4, waiting for transfers between devices, gather_tokens(): lax.all_gather(image, 'col', axis=0, tiled=True)  97.6 us
    reduce_scatter x4, waiting for transfers between devices, sum_to_columns(): lax.psum_scatter(image, 'col', scatter_dimension=0, tiled=True)  89.8 us
    unnamed x263, local copies, waits for them, and re-layouts  88.2 us
    psum x4, blocking collectives, row_totals(): lax.psum((jnp.sum(image_first, axis=1), jnp.sum(image_second, axis=1), jn...  77.5 us
  transfers between devices with their start and end apart: 29, of which 23 were waited for; matrix products, arithmetic and copies ran while one was open for 22% of the time, Pallas kernels for 0%

commit v1 on v0

v1 whole, which is shorter than its diff:
```python
import functools

import jax
import jax.numpy as jnp
from jax import lax
from jax.experimental import pallas as pl
from jax.experimental.pallas import tpu as pltpu
from jax.sharding import PartitionSpec as P

D = 1536
HEAD = 64
IMG = 1024
TXT = 154
PAD = 160
SCALE = HEAD**-0.5
EPSILON = 1e-06
BF = jnp.bfloat16
F32 = jnp.float32


def product(left, right):
    return jnp.dot(left, right, preferred_element_type=F32)


def product_left(left, right):
    return lax.dot_general(left, right, (((0,), (0,)), ((), ())), preferred_element_type=F32)


def product_right(left, right):
    return lax.dot_general(left, right, (((1,), (1,)), ((), ())), preferred_element_type=F32)


def gelu_value(values):
    return jax.nn.gelu(values, approximate=True)


def gelu_slope(values, grad):
    return jax.vjp(gelu_value, values)[1](grad)[0]


def silu_slope(values, grad):
    return jax.vjp(jax.nn.silu, values)[1](grad)[0]


def gather(values, axis_name, axis=0):
    return lax.all_gather(values, axis_name, axis=axis, tiled=True)


def shifted(values, count, step):
    return lax.ppermute(values, "dp", [(i, (i + step) % count) for i in range(count)])


def partner(values, count):
    return lax.ppermute(values, "dp", [(i, i ^ 1) for i in range(count)])


def in_order(mine, other, parity, axis):
    first = jnp.where(parity == 0, mine, other)
    second = jnp.where(parity == 0, other, mine)
    return jnp.stack([first, second], axis=axis)


def sum_over_dp(values, count):
    total = values.astype(F32)
    for step in range(1, count):
        total = total + shifted(values, count, step).astype(F32)
    return total


def join_over_dp(values, count, parity):
    mine = values.astype(F32)
    other = shifted(values, count, 1).astype(F32)
    for step in range(2, count):
        moved = shifted(values, count, step).astype(F32)
        if step % 2:
            other = other + moved
        else:
            mine = mine + moved
    joined = in_order(mine, other, parity, 0)
    return joined.reshape((-1,) + values.shape[1:])


def gather_block(block, count, parity):
    half = lax.dynamic_index_in_dim(block.reshape(2, -1, block.shape[1]), parity, 0, keepdims=False)
    mine = lax.all_gather(half, "row")
    both = in_order(mine, partner(mine, count), parity, 1)
    return both.reshape(mine.shape[0], -1, mine.shape[2])


def after(value, *others):
    return lax.optimization_barrier((value, others))[0]


def norm_local(values):
    mean = jnp.mean(values, axis=1, keepdims=True)
    square = jnp.mean(values * values, axis=1, keepdims=True)
    inverse = lax.rsqrt(square - mean * mean + EPSILON)
    return (values - mean) * inverse, inverse


def norm_local_back(grad, normed, inverse):
    total = jnp.mean(grad, axis=1, keepdims=True)
    cross = jnp.mean(grad * normed, axis=1, keepdims=True)
    return inverse * (grad - total - normed * cross)


def row_stats(first, second):
    pair = jnp.stack([jnp.sum(first, axis=1), jnp.sum(second, axis=1)])
    return jnp.pad(pair, ((0, 6), (0, 0)))


def row_means(stats):
    totals = jnp.sum(stats.reshape(4, 8, -1)[:, :2], axis=0) / D
    return totals[0][:, None], totals[1][:, None]


def norm_row(values, stats):
    mean, square = row_means(stats)
    inverse = lax.rsqrt(square - mean * mean + EPSILON)
    return (values - mean) * inverse, inverse


def norm_row_back(grad, normed, inverse, stats):
    total, cross = row_means(stats)
    return inverse * (grad - total - normed * cross)


def side(values, rows):
    width = values.shape[1]
    return values.reshape(rows, -1, width).transpose(1, 0, 2).reshape(-1, rows * width)


def stack(values, rows):
    count = values.shape[0]
    return values.reshape(count, rows, -1).transpose(1, 0, 2).reshape(rows * count, -1)


LOG2 = 1.4426950408889634


def dot_nt(left, right):
    return lax.dot_general(left, right, (((1,), (1,)), ((), ())), preferred_element_type=F32)


def dot_tn(left, right):
    return lax.dot_general(left, right, (((0,), (0,)), ((), ())), preferred_element_type=F32)


def head_mask(values, head):
    lane = lax.broadcasted_iota(jnp.int32, values.shape, 1)
    return jnp.where((lane >= head * HEAD) & (lane < (head + 1) * HEAD), values, 0)


def attend_kernel(qi, ki, vi, qt, kt, vt, oi, ot, li, lt, kim, vim, ktm, vtm):
    for h in range(2):
        kim[h] = head_mask(ki[...], h)
        vim[h] = head_mask(vi[...], h)
        ktm[h] = head_mask(kt[...], h)
        vtm[h] = head_mask(vt[...], h)

    def block(query):
        total = None
        rows = []
        for h in range(2):
            si = dot_nt(query, kim[h])
            st = dot_nt(query, ktm[h])
            lane = lax.broadcasted_iota(jnp.int32, st.shape, 1)
            st = jnp.where(lane < TXT, st, -1e30)
            peak = jnp.maximum(
                jnp.max(si, axis=1, keepdims=True), jnp.max(st, axis=1, keepdims=True)
            )
            ei = jnp.exp2((si - peak) * (SCALE * LOG2))
            et = jnp.exp2((st - peak) * (SCALE * LOG2))
            norm = jnp.sum(ei, axis=1, keepdims=True) + jnp.sum(et, axis=1, keepdims=True)
            part = product(ei.astype(BF), vim[h]) + product(et.astype(BF), vtm[h])
            part = part / norm
            total = part if total is None else total + part
            rows.append(peak * (SCALE * LOG2) + jnp.log2(norm))
        lane = lax.broadcasted_iota(jnp.int32, total.shape, 1)
        stats = jnp.where(lane == 0, rows[0], jnp.where(lane == 1, rows[1], 0.0))
        return total.astype(BF), jnp.transpose(stats)[:8]

    for b in range(IMG // 256):
        at = pl.ds(b * 256, 256)
        oi[at, :], li[0, :, at] = block(qi[at, :])
    ot[...], lt[0] = block(qt[...])


def attend(qkv_i, qkv_t):
    width = qkv_i.shape[1] // 3
    pairs = width // 128

    def part(rows, which):
        return pl.BlockSpec((rows, 128), lambda j: (0, which * pairs + j))

    return pl.pallas_call(
        attend_kernel,
        grid=(pairs,),
        in_specs=[part(n, w) for n in (IMG, PAD) for w in range(3)],
        out_specs=[
            part(IMG, 0),
            part(PAD, 0),
            pl.BlockSpec((1, 8, IMG), lambda j: (j, 0, 0)),
            pl.BlockSpec((1, 8, PAD), lambda j: (j, 0, 0)),
        ],
        out_shape=[
            jax.ShapeDtypeStruct((IMG, width), BF),
            jax.ShapeDtypeStruct((PAD, width), BF),
            jax.ShapeDtypeStruct((pairs, 8, IMG), F32),
            jax.ShapeDtypeStruct((pairs, 8, PAD), F32),
        ],
        scratch_shapes=[pltpu.VMEM((2, n, 128), BF) for n in (IMG, IMG, PAD, PAD)],
        compiler_params=pltpu.CompilerParams(vmem_limit_bytes=56 * 1024 * 1024),
        cost_estimate=cost(19),
        name="attend",
    )(qkv_i, qkv_i, qkv_i, qkv_t, qkv_t, qkv_t)


def attend_back_kernel(
    qi, ki, vi, qt, kt, vt, oi, ot, gi, gt, li, lt, dqi, dki, dvi, dqt, dkt, dvt, aki, avi, akt, avt
):
    for acc in (aki, avi, akt, avt):
        acc[...] = jnp.zeros_like(acc)
    lane8 = lax.broadcasted_iota(jnp.int32, (8, 128), 1) // HEAD
    row8 = lax.broadcasted_iota(jnp.int32, (8, 128), 0)
    pick = (lane8 == row8).astype(F32)

    def block(query, out, grad, logsum):
        products = grad.astype(F32) * out.astype(F32)
        delta = lax.dot_general(
            pick, products, (((1,), (1,)), ((), ())),
            preferred_element_type=F32, precision=lax.Precision.HIGHEST,
        )
        total = None
        for h in range(2):
            qm = head_mask(query, h)
            gm = head_mask(grad, h)
            part = None
            for keys, values, ak, av, text in ((ki, vi, aki, avi, False), (kt, vt, akt, avt, True)):
                scores = dot_nt(keys[...], qm) * (SCALE * LOG2) - logsum[h : h + 1]
                prob = jnp.exp2(scores)
                if text:
                    place = lax.broadcasted_iota(jnp.int32, prob.shape, 0)
                    prob = jnp.where(place < TXT, prob, 0.0)
                grads = (prob * (dot_nt(values[...], gm) - delta[h : h + 1])).astype(BF)
                av[...] += product(prob.astype(BF), gm)
                ak[...] += product(grads, qm)
                term = dot_tn(grads, keys[...])
                part = term if part is None else part + term
            part = head_mask(part, h)
            total = part if total is None else total + part
        return (total * SCALE).astype(BF)

    for b in range(IMG // 256):
        at = pl.ds(b * 256, 256)
        dqi[at, :] = block(qi[at, :], oi[at, :], gi[at, :], li[0, :, at])
    dqt[...] = block(qt[...], ot[...], gt[...], lt[0])
    dki[...] = (aki[...] * SCALE).astype(BF)
    dvi[...] = avi[...].astype(BF)
    dkt[...] = (akt[...] * SCALE).astype(BF)
    dvt[...] = avt[...].astype(BF)


def attend_back(qkv_i, qkv_t, out_i, out_t, grad_i, grad_t, log_i, log_t):
    width = qkv_i.shape[1] // 3
    pairs = width // 128

    def part(rows, which):
        return pl.BlockSpec((rows, 128), lambda j: (0, which * pairs + j))

    results = pl.pallas_call(
        attend_back_kernel,
        grid=(pairs,),
        in_specs=[part(n, w) for n in (IMG, PAD) for w in range(3)]
        + [part(n, 0) for n in (IMG, PAD, IMG, PAD)]
        + [pl.BlockSpec((1, 8, n), lambda j: (j, 0, 0)) for n in (IMG, PAD)],
        out_specs=[part(n, 0) for n in (IMG, PAD) for w in range(3)],
        out_shape=[jax.ShapeDtypeStruct((n, width), BF) for n in (IMG, PAD) for w in range(3)],
        scratch_shapes=[pltpu.VMEM((n, 128), F32) for n in (IMG, IMG, PAD, PAD)],
        compiler_params=pltpu.CompilerParams(vmem_limit_bytes=56 * 1024 * 1024),
        cost_estimate=cost(32),
        name="attend_back",
    )(qkv_i, qkv_i, qkv_i, qkv_t, qkv_t, qkv_t, out_i, out_t, grad_i, grad_t, log_i, log_t)
    return jnp.concatenate(results[:3], axis=1), jnp.concatenate(results[3:], axis=1)


MESH = pl.DeviceIdType.MESH


def cost(micros):
    return pl.CostEstimate(flops=0, bytes_accessed=micros * 3_500_000, transcendentals=0)


def span(start, size):
    unit = 16 if size % 16 == 0 else 8
    return pl.ds(pl.multiple_of(start, unit), size)


class AllGatherCol:
    def __init__(self, value, pieces=1):
        self.ins = [value]
        n, w = value.shape
        self.n, self.pieces, self.step = n, pieces, n // pieces
        self.outs = [jax.ShapeDtypeStruct((4 * n, w), value.dtype)]
        self.scratch = [pltpu.SemaphoreType.DMA((3 * pieces,)) for _ in range(2)]

    def peers(self, me):
        return [(me[0], me[1], me[2] ^ 1), (me[0], me[1], me[2] ^ 2)]

    greets = awaits = peers

    def move(self, refs, me, which, i):
        (value,), (out,), (send, recv) = refs
        core, across = self.peers(me)
        owner = me[2] ^ 2 if which == 2 else me[2]
        slot = out.at[span(owner * self.n + i * self.step, self.step)]
        source = slot if which == 2 else value.at[pl.ds(i * self.step, self.step)]
        k = which * self.pieces + i
        return pltpu.make_async_remote_copy(
            source, slot, send.at[k], recv.at[k],
            device_id=across if which == 0 else core, device_id_type=MESH,
        )

    def start(self, refs, me):
        for which in range(2):
            for i in range(self.pieces):
                self.move(refs, me, which, i).start()
        (value,), (out,), _ = refs
        out[span(me[2] * self.n, self.n)] = value[...]

    def middle(self, refs, me):
        for i in range(self.pieces):
            self.move(refs, me, 0, i).wait_recv()
            self.move(refs, me, 2, i).start()

    def finish(self, refs, me):
        for which in range(3):
            for i in range(self.pieces):
                move = self.move(refs, me, which, i)
                move.wait_send()
                if which:
                    move.wait_recv()


class ReduceScatterCol:
    def __init__(self, value, pieces=1):
        self.ins = [value]
        n, w = value.shape[0] // 4, value.shape[1]
        self.n, self.pieces, self.step = n, pieces, n // pieces
        self.outs = [jax.ShapeDtypeStruct((n, w), F32)]
        self.scratch = [pltpu.VMEM((n, w), BF) for _ in range(4)]
        self.scratch += [pltpu.SemaphoreType.DMA((3 * pieces,)) for _ in range(2)]

    peers = AllGatherCol.peers
    greets = awaits = peers

    def move(self, refs, me, which, i):
        (part,), _, (first, second, third, total, send, recv) = refs
        core, across = self.peers(me)
        at = pl.ds(i * self.step, self.step)
        if which == 2:
            source, target = total.at[at], third.at[at]
        else:
            owner = me[2] ^ 3 if which == 0 else me[2] ^ 1
            source = part.at[span(owner * self.n + i * self.step, self.step)]
            target = (first, second)[which].at[at]
        k = which * self.pieces + i
        return pltpu.make_async_remote_copy(
            source, target, send.at[k], recv.at[k],
            device_id=across if which == 2 else core, device_id_type=MESH,
        )

    def start(self, refs, me):
        for which in range(2):
            for i in range(self.pieces):
                self.move(refs, me, which, i).start()

    def middle(self, refs, me):
        (part,), _, (first, second, third, total, send, recv) = refs
        for i in range(self.pieces):
            self.move(refs, me, 0, i).wait_recv()
            at = pl.ds(i * self.step, self.step)
            mine = part[span((me[2] ^ 2) * self.n + i * self.step, self.step)]
            total[at] = (mine.astype(F32) + first[at].astype(F32)).astype(BF)
            self.move(refs, me, 2, i).start()

    def finish(self, refs, me):
        (part,), (out,), (first, second, third, total, send, recv) = refs
        for i in range(self.pieces):
            for which in (1, 2):
                self.move(refs, me, which, i).wait_recv()
            at = pl.ds(i * self.step, self.step)
            mine = part[span(me[2] * self.n + i * self.step, self.step)].astype(F32)
            out[at] = mine + second[at].astype(F32) + third[at].astype(F32)
        for which in range(3):
            for i in range(self.pieces):
                self.move(refs, me, which, i).wait_send()


class AllGatherRow:
    axis = 1

    def __init__(self, value, size=4):
        self.ins = [value]
        n, w = value.shape
        self.n, self.size = n, size
        self.outs = [jax.ShapeDtypeStruct((size * n, w), value.dtype)]
        self.scratch = [pltpu.SemaphoreType.DMA((size - 1,)) for _ in range(2)]

    def peers(self, me):
        found = []
        for k in range(1, self.size):
            device = list(me)
            device[self.axis] = lax.rem(me[self.axis] + k, self.size)
            found.append(tuple(device))
        return found

    greets = awaits = peers

    def move(self, refs, me, k):
        (value,), (out,), (send, recv) = refs
        return pltpu.make_async_remote_copy(
            value, out.at[span(me[self.axis] * self.n, self.n)], send.at[k], recv.at[k],
            device_id=self.peers(me)[k], device_id_type=MESH,
        )

    def start(self, refs, me):
        for k in range(self.size - 1):
            self.move(refs, me, k).start()
        (value,), (out,), _ = refs
        out[span(me[self.axis] * self.n, self.n)] = value[...]

    def middle(self, refs, me):
        pass

    def finish(self, refs, me):
        for k in range(self.size - 1):
            self.move(refs, me, k).wait()


class AllGatherDp(AllGatherRow):
    axis = 0


class ReduceScatterRow:
    def __init__(self, value):
        self.ins = [value]
        n, w = value.shape[0] // 4, value.shape[1]
        self.n = n
        self.outs = [jax.ShapeDtypeStruct((n, w), F32)]
        self.scratch = [pltpu.VMEM((3, n, w), BF)]
        self.scratch += [pltpu.SemaphoreType.DMA((3,)) for _ in range(2)]

    axis, size = 1, 4
    peers = AllGatherRow.peers
    greets = awaits = peers

    def move(self, refs, me, k):
        (part,), _, (held, send, recv) = refs
        target = self.peers(me)[k]
        return pltpu.make_async_remote_copy(
            part.at[span(target[1] * self.n, self.n)], held.at[k], send.at[k], recv.at[k],
            device_id=target, device_id_type=MESH,
        )

    def start(self, refs, me):
        for k in (1, 0, 2):
            self.move(refs, me, k).start()

    def middle(self, refs, me):
        pass

    def finish(self, refs, me):
        (part,), (out,), (held, send, recv) = refs
        for k in range(3):
            self.move(refs, me, k).wait()
        total = part[span(me[1] * self.n, self.n)].astype(F32)
        for k in range(3):
            total = total + held[k].astype(F32)
        out[...] = total


class ToSequence:
    def __init__(self, value):
        self.ins = [value]
        self.n, self.w = value.shape[0] // 4, value.shape[1]
        self.outs = [jax.ShapeDtypeStruct((self.n, 4 * self.w), value.dtype)]
        self.scratch = [pltpu.SemaphoreType.DMA((4,)) for _ in range(2)]

    def targets(self, me):
        return [(me[0], me[2], k) for k in range(4)]

    def sources(self, me):
        return [(me[0], k, me[1]) for k in range(4)]

    def greets(self, me):
        return [
            (device, jnp.logical_not((device[1] == me[1]) & (device[2] == me[2])))
            for device in self.sources(me)
        ]

    def awaits(self, me):
        return self.targets(me)

    def remote(self, me, device):
        return jnp.logical_not((device[1] == me[1]) & (device[2] == me[2]))

    def place(self, refs, me, k):
        (value,), (out,), _ = refs
        source = value.at[pl.ds(k * self.n, self.n)]
        return source, out.at[:, pl.ds(pl.multiple_of(me[1] * self.w, 128), self.w)]

    def outgoing(self, refs, me, k):
        send, recv = refs[2]
        source, target = self.place(refs, me, k)
        return pltpu.make_async_remote_copy(
            source, target, send.at[k], recv.at[me[1]],
            device_id=self.targets(me)[k], device_id_type=MESH,
        )

    def incoming(self, refs, me, k):
        send, recv = refs[2]
        (value,), (out,), _ = refs
        landing = out.at[:, pl.ds(k * self.w, self.w)]
        return pltpu.make_async_remote_copy(
            value.at[pl.ds(0, self.n)], landing, send.at[k], recv.at[k],
            device_id=self.targets(me)[k], device_id_type=MESH,
        )

    def copy_own(self, refs, me):
        (value,), (out,), _ = refs
        at = pl.ds(pl.multiple_of(me[1] * self.w, 128), self.w)
        out[:, at] = value[span(me[2] * self.n, self.n)]

    def start(self, refs, me):
        for k in range(4):
            @pl.when(self.remote(me, self.targets(me)[k]))
            def _():
                self.outgoing(refs, me, k).start()

        @pl.when(me[1] == me[2])
        def _():
            self.copy_own(refs, me)

    def middle(self, refs, me):
        pass

    def finish(self, refs, me):
        for k in range(4):
            @pl.when(self.remote(me, self.targets(me)[k]))
            def _():
                self.outgoing(refs, me, k).wait_send()

            @pl.when(self.remote(me, self.sources(me)[k]))
            def _():
                self.incoming(refs, me, k).wait_recv()


class FromSequence(ToSequence):
    def __init__(self, value):
        self.ins = [value]
        self.n, self.w = value.shape[0], value.shape[1] // 4
        self.outs = [jax.ShapeDtypeStruct((4 * self.n, self.w), value.dtype)]
        self.scratch = [pltpu.SemaphoreType.DMA((4,)) for _ in range(2)]

    def targets(self, me):
        return [(me[0], k, me[1]) for k in range(4)]

    def sources(self, me):
        return [(me[0], me[2], k) for k in range(4)]

    def outgoing(self, refs, me, k):
        (value,), (out,), (send, recv) = refs
        return pltpu.make_async_remote_copy(
            value.at[:, pl.ds(k * self.w, self.w)],
            out.at[span(me[2] * self.n, self.n)],
            send.at[k], recv.at[me[2]],
            device_id=self.targets(me)[k], device_id_type=MESH,
        )

    def incoming(self, refs, me, k):
        (value,), (out,), (send, recv) = refs
        return pltpu.make_async_remote_copy(
            value.at[:, pl.ds(0, self.w)],
            out.at[pl.ds(k * self.n, self.n)],
            send.at[k], recv.at[k],
            device_id=self.targets(me)[k], device_id_type=MESH,
        )

    def copy_own(self, refs, me):
        (value,), (out,), _ = refs
        at = pl.ds(pl.multiple_of(me[1] * self.w, 128), self.w)
        out[span(me[2] * self.n, self.n)] = value[:, at]


def exchange_kernel(ops, *refs):
    me = tuple(lax.axis_index(name) for name in ("dp", "row", "col"))
    refs = list(refs)
    parts = []
    for kind in ("ins", "outs", "scratch"):
        taken = []
        for op in ops:
            count = len(getattr(op, kind))
            taken.append(refs[:count])
            refs = refs[count:]
        parts.append(taken)
    parts = list(zip(*parts))
    barrier = pltpu.get_barrier_semaphore()
    count = 0
    for op in ops:
        for item in op.greets(me):
            device, wanted = item if len(item) == 2 else (item, None)
            if wanted is None:
                pl.semaphore_signal(barrier, 1, device_id=device, device_id_type=MESH)
            else:
                @pl.when(wanted)
                def _():
                    pl.semaphore_signal(barrier, 1, device_id=device, device_id_type=MESH)
        if isinstance(op, ToSequence):
            count = count + 4 - (me[1] == me[2]).astype(jnp.int32)
        else:
            count = count + len(op.awaits(me))
    pl.semaphore_wait(barrier, count)
    for op, part in zip(ops, parts):
        op.start(part, me)
    for op, part in zip(ops, parts):
        op.middle(part, me)
    for op, part in zip(ops, parts):
        op.finish(part, me)


def exchange(number, micros, *ops):
    ins = [value for op in ops for value in op.ins]
    outs = [shape for op in ops for shape in op.outs]
    results = pl.pallas_call(
        functools.partial(exchange_kernel, ops),
        in_specs=[pl.BlockSpec(memory_space=pltpu.VMEM)] * len(ins),
        out_specs=[pl.BlockSpec(memory_space=pltpu.VMEM)] * len(outs),
        out_shape=outs,
        scratch_shapes=[shape for op in ops for shape in op.scratch],
        compiler_params=pltpu.CompilerParams(
            collective_id=number, has_side_effects=True, vmem_limit_bytes=60 * 1024 * 1024
        ),
        cost_estimate=cost(micros),
        name="exchange" + str(number),
    )(*ins)
    return results if len(results) > 1 else results[0]


def pad_text(values):
    return jnp.pad(values, ((0, PAD - TXT), (0, 0)))


def shards(
    dps,
    rows,
    cols,
    image_tokens,
    text_tokens,
    condition,
    ada_w,
    ada_b,
    qkv_w,
    qkv_b,
    out_w,
    out_b,
    up_w,
    up_b,
    down_w,
    down_b,
    image_cot,
    text_cot,
):
    row = lax.axis_index("row")
    col = lax.axis_index("col")
    seqs = condition.shape[0]
    wr = image_tokens.shape[1]
    wc = condition.shape[1]
    wf = up_w.shape[2]

    parity = lax.rem(lax.axis_index("dp"), 2)
    first_0 = gather_block(
        jnp.concatenate([qkv_w[0].reshape(wr, 3 * wc), out_w[0]], axis=1), dps, parity
    )
    qkv_0 = first_0[:, :, : 3 * wc].reshape(rows * wr, 3 * wc)
    out_0 = first_0[:, :, 3 * wc :].transpose(1, 0, 2).reshape(wc, rows * wr)
    qkv_1 = qkv_w[1].reshape(wr, 3 * wc)
    share = wf // rows
    up_bias_1 = lax.dynamic_slice_in_dim(up_b[1], row * share, share).astype(F32)

    cond_value = condition.astype(F32)
    silu_low = jax.nn.silu(cond_value).astype(BF)
    modul_parts = jnp.concatenate(
        [product(silu_low, ada_w[s].reshape(wc, 6 * wr)) for s in range(2)]
    )
    modul_all = exchange(1, 7, AllGatherCol(modul_parts)).reshape(cols, 2, seqs, 6, wr)
    mods = jnp.sum(modul_all, axis=0) + ada_b.astype(F32)[:, None]
    bias_rows = jnp.broadcast_to(
        jnp.stack([out_b[0], down_b[0]]).astype(F32)[None], (seqs, 2, wr)
    )
    sent = jnp.concatenate([mods[0], bias_rows], axis=1).reshape(seqs * 8, wr)
    x1 = pad_text(text_tokens.astype(F32))
    cot1 = pad_text(text_cot.astype(F32))
    x0, mods_row, stats = exchange(
        2,
        30,
        ToSequence(image_tokens),
        AllGatherRow(sent),
        AllGatherRow(row_stats(x1, x1 * x1)),
    )
    mod_0 = lax.dynamic_index_in_dim(
        mods_row.reshape(rows, seqs, 8, wr), row, 1, keepdims=False
    ).transpose(1, 0, 2).reshape(8, rows * wr)
    mod_1 = lax.dynamic_index_in_dim(mods[1], col, 0, keepdims=False)
    up_0 = gather_block(up_w[0], dps, parity).reshape(rows * wr, wf)

    x0 = x0.astype(F32)
    norm1_0, inv1_0 = norm_local(x0)
    mixed1_0 = (norm1_0 * (1.0 + mod_0[1]) + mod_0[0]).astype(BF)
    norm1_1, inv1_1 = norm_row(x1, stats)
    mixed1_1 = (norm1_1 * (1.0 + mod_1[1]) + mod_1[0]).astype(BF)
    full1_1, full1_0, cot0 = exchange(
        3, 27, AllGatherCol(mixed1_1), AllGatherCol(mixed1_0, 4), ToSequence(image_cot)
    )
    down_0 = gather_block(down_w[0], dps, parity)
    down_0 = down_0.transpose(1, 0, 2).reshape(wf, rows * wr)
    cot0 = cot0.astype(F32)
    qkv_bias = jnp.stack(
        [qkv_b[:, 0], jnp.zeros_like(qkv_b[:, 0]), qkv_b[:, 1]], axis=1
    ).astype(F32).reshape(2, 3 * wc)
    qkv_t, wide_g1, branch_g0 = exchange(
        4,
        45,
        ReduceScatterRow(product(full1_1, qkv_1).astype(BF)),
        AllGatherRow((mod_1[5] * cot1).astype(BF)),
        AllGatherCol((mod_0[5] * cot0).astype(BF), 4),
    )
    text_w = jnp.stack([up_w[1].T.reshape(rows, 2, -1, wr), down_w[1].reshape(rows, 2, -1, wr)])
    text_w = lax.dynamic_index_in_dim(after(text_w, qkv_t), parity, 2, keepdims=False)
    text_w = lax.all_to_all(text_w, "row", 1, 1)
    text_w = in_order(text_w, partner(text_w, dps), parity, 2).reshape(2, rows, -1, wr)
    up_1, down_1 = text_w.transpose(0, 2, 1, 3).reshape(2, -1, rows * wr)
    qkv_txt = (qkv_t + qkv_bias[1]).astype(BF)
    qkv_img = (product(full1_0, qkv_0) + qkv_bias[0]).astype(BF)
    attn_0, attn_text, log_0, log_1 = attend(qkv_img, qkv_txt)
    attn_1, branch_g1 = exchange(
        6, 14, AllGatherRow(attn_text), AllGatherCol(side(wide_g1, rows), 2)
    )

    proj_1, proj_0 = exchange(
        7,
        25,
        ReduceScatterCol(product(attn_1, out_w[1]).astype(BF)),
        ReduceScatterCol(product(attn_0, out_0).astype(BF), 4),
    )
    proj_0 = proj_0 + mod_0[6]
    resid_0 = x0 + mod_0[2] * proj_0
    norm2_0, inv2_0 = norm_local(resid_0)
    mixed2_0 = (norm2_0 * (1.0 + mod_0[4]) + mod_0[3]).astype(BF)
    proj_1 = proj_1 + out_b[1].astype(F32)
    resid_1 = x1 + mod_1[2] * proj_1
    stats, full2_0 = exchange(
        8, 22, AllGatherRow(row_stats(resid_1, resid_1 * resid_1)), AllGatherCol(mixed2_0, 4)
    )
    norm2_1, inv2_1 = norm_row(resid_1, stats)
    mixed2_1 = (norm2_1 * (1.0 + mod_1[4]) + mod_1[3]).astype(BF)
    wide2_1 = exchange(9, 13, AllGatherRow(mixed2_1))
    full2_1 = exchange(10, 13, AllGatherCol(side(wide2_1, rows), 2))

    def halves(values, which):
        cut = values.reshape(values.shape[0], -1, 2, values.shape[1] // 2 // rows)
        return lax.dynamic_index_in_dim(cut, which, 2, keepdims=False).reshape(
            values.shape[0], -1
        )

    def half(values, which):
        cut = values.shape[1] // 2
        return lax.dynamic_slice_in_dim(values, which * cut, cut, 1)

    def by_row(left, right):
        wide = product_left(right, left).reshape(rows, wr, left.shape[1])
        return wide.transpose(0, 2, 1)

    pre_0 = product(full2_0, up_0) + up_b[0].astype(F32)
    hidden_0 = gelu_value(pre_0).astype(BF)
    pre_g0 = gelu_slope(pre_0, product_right(branch_g0, down_0)).astype(BF)
    pre_1 = product_right(full2_1, up_1) + up_bias_1
    hidden_1 = gelu_value(pre_1).astype(BF)
    pre_g1 = gelu_slope(pre_1, product_right(branch_g1, down_1)).astype(BF)

    def add_partner(other, mine):
        return (mine + partner(other, dps).astype(F32)).astype(BF)

    def reduce_block(both):
        return lax.psum_scatter(both, "row", scatter_dimension=0)

    down_o = by_row(half(hidden_0, 1 - parity), branch_g0).astype(BF)
    up_o = product_left(halves(full2_0, 1 - parity), pre_g0).reshape(rows, -1, wf).astype(BF)
    mixed2_g0, wide2_g1 = exchange(
        11,
        35,
        ReduceScatterCol(after(product_right(pre_g0, up_0).astype(BF), down_o, up_o), 4),
        ReduceScatterCol(product(pre_g1, up_1).astype(BF), 2),
    )
    down_b0 = add_partner(down_o, by_row(half(hidden_0, parity), branch_g0))
    up_b0 = add_partner(
        up_o, product_left(halves(full2_0, parity), pre_g0).reshape(rows, -1, wf)
    )
    def text_part(which):
        parts = [
            product_left(half(pre_g1, which), full2_1),
            product_left(half(hidden_1, which), branch_g1),
        ]
        return jnp.stack(parts).astype(BF)

    text_o = text_part(1 - parity)
    text_m = text_part(parity)

    resid_g0 = cot0 + norm_local_back(mixed2_g0 * (1.0 + mod_0[4]), norm2_0, inv2_0)
    down_h0 = reduce_block(down_b0)
    mixed2_g1, proj_g0 = exchange(
        12,
        22,
        ReduceScatterRow(stack(wide2_g1.astype(BF), rows)),
        AllGatherCol((mod_0[2] * resid_g0).astype(BF), 4),
    )
    up_h0 = reduce_block(up_b0)
    norm2_g1 = mixed2_g1 * (1.0 + mod_1[4])
    stats, wide_1 = exchange(
        13,
        16,
        AllGatherRow(row_stats(norm2_g1, norm2_g1 * norm2_1)),
        ReduceScatterCol(after(product(hidden_1, down_1).astype(BF), down_b0), 2),
    )
    resid_g1 = cot1 + norm_row_back(norm2_g1, norm2_1, inv2_1, stats)
    proj_g1 = exchange(14, 7, AllGatherCol((mod_1[2] * resid_g1).astype(BF)))
    attn_g0 = product_right(proj_g0, out_0).astype(BF)
    attn_g1, branch_0 = exchange(
        15,
        22,
        ReduceScatterRow(product_right(proj_g1, out_w[1]).astype(BF)),
        ReduceScatterCol(product(hidden_0, down_0).astype(BF), 4),
    )
    attn_g1 = attn_g1.astype(BF)
    branch_0 = branch_0 + mod_0[7]
    out_g1 = product_left(attn_1, proj_g1)
    out_o = by_row(half(attn_0, 1 - parity), proj_g0).astype(BF)
    qkv_grad_0, qkv_grad_t = attend_back(
        qkv_img, qkv_txt, attn_0, attn_text, after(attn_g0, out_o, text_o, up_b0), attn_g1, log_0, log_1
    )
    out_b0 = add_partner(out_o, by_row(half(attn_0, parity), proj_g0))
    out_h0 = reduce_block(out_b0)
    text_b = (text_m + partner(text_o, dps).astype(F32)).astype(BF)
    text_b = text_b.reshape(2, share // 2, rows, wr).transpose(0, 2, 1, 3)
    text_h = lax.all_to_all(text_b, "row", 1, 1)
    qkv_o = product_left(halves(full1_0, 1 - parity), qkv_grad_0)
    qkv_o = qkv_o.reshape(rows, -1, 3 * wc).astype(BF)

    def column_sums(values):
        return jnp.sum(values, axis=0, dtype=F32)

    first = (row == 0).astype(F32)
    place = (lax.iota(jnp.int32, rows) == row).astype(F32)[:, None]
    qkv_s0 = column_sums(qkv_grad_0)
    qkv_s1 = column_sums(qkv_grad_t)
    vectors = jnp.concatenate(
        [
            column_sums(branch_g0),
            column_sums(proj_g0),
            column_sums(branch_g1) * first,
            (place * column_sums(proj_g1)[None]).reshape(-1),
            column_sums(pre_g0),
            (place * column_sums(pre_g1)[None]).reshape(-1),
            qkv_s0[:wc],
            qkv_s0[2 * wc :],
            qkv_s1[:wc],
            qkv_s1[2 * wc :],
        ]
    ).reshape(-1, wc)
    pad_rows = -vectors.shape[0] % 8
    qkv_grad_1, mixed1_g0, vectors = exchange(
        16,
        35,
        AllGatherRow(qkv_grad_t),
        ReduceScatterCol(after(product_right(qkv_grad_0, qkv_0).astype(BF), qkv_o), 4),
        AllGatherRow(jnp.pad(vectors, ((0, pad_rows), (0, 0)))),
    )
    qkv_b0 = add_partner(
        qkv_o, product_left(halves(full1_0, parity), qkv_grad_0).reshape(rows, -1, 3 * wc)
    )
    qkv_g1 = product_left(full1_1, qkv_grad_1)
    image_grad = resid_g0 + norm_local_back(mixed1_g0 * (1.0 + mod_0[1]), norm1_0, inv1_0)
    mixed1_g1, branch_1, vectors, image_grad, image_out = exchange(
        17,
        37,
        ReduceScatterCol(product_right(qkv_grad_1, qkv_1).astype(BF)),
        ReduceScatterRow(stack(after(wide_1, out_b0, down_h0).astype(BF), rows)),
        AllGatherDp(jnp.sum(vectors.reshape(rows, -1, wc), axis=0), dps),
        FromSequence(image_grad.astype(BF)),
        FromSequence((resid_0 + mod_0[5] * branch_0).astype(BF)),
    )
    vectors = jnp.sum(vectors.reshape(dps, -1, wc), axis=0).reshape(-1)
    qkv_h0 = reduce_block(qkv_b0)
    branch_1 = branch_1 + down_b[1].astype(F32)
    text_out = (resid_1 + mod_1[5] * branch_1).astype(BF)[:TXT]
    norm1_g1 = mixed1_g1 * (1.0 + mod_1[1])

    sums_0 = jnp.stack(
        [
            jnp.sum(t, axis=0)
            for t in (
                mixed1_g0,
                mixed1_g0 * norm1_0,
                resid_g0 * proj_0,
                mixed2_g0,
                mixed2_g0 * norm2_0,
                cot0 * branch_0,
            )
        ]
    )
    sums_1 = jnp.stack(
        [
            jnp.sum(t, axis=0)
            for t in (
                mixed1_g1,
                mixed1_g1 * norm1_1,
                resid_g1 * proj_1,
                mixed2_g1,
                mixed2_g1 * norm2_1,
                cot1 * branch_1,
            )
        ]
    )
    stats, cols_0, cols_1 = exchange(
        18,
        10,
        AllGatherRow(row_stats(norm1_g1, norm1_g1 * norm1_1)),
        AllGatherCol(jnp.pad(sums_0, ((0, 2), (0, 0)))),
        AllGatherCol(jnp.pad(sums_1, ((0, 2), (0, 0)))),
    )
    image_grad = image_grad.astype(F32)
    text_grad = resid_g1 + norm_row_back(norm1_g1, norm1_1, inv1_1, stats)
    rows_0 = exchange(19, 8, AllGatherRow(jnp.sum(cols_0.reshape(cols, 8, rows * wr), axis=0)))
    rows_0 = lax.dynamic_index_in_dim(
        rows_0.reshape(seqs, 8, rows, wr)[:, :6], row, 2, keepdims=False
    )
    mods_low = jnp.stack([rows_0, cols_1.reshape(seqs, 8, wr)[:, :6]]).astype(BF)
    mods_low = mods_low.reshape(2, seqs, 6 * wr)
    silu_part = product_right(mods_low[0], ada_w[0].reshape(wc, 6 * wr)) + product_right(
        mods_low[1], ada_w[1].reshape(wc, 6 * wr)
    )
    mods_all, silu_all, silu_part = exchange(
        20,
        9,
        AllGatherDp(mods_low.reshape(2 * seqs, 6 * wr).astype(F32), dps),
        AllGatherDp(jnp.pad(silu_low.astype(F32), ((0, 8 - seqs), (0, 0))), dps),
        AllGatherRow(jnp.pad(silu_part, ((0, 8 - seqs), (0, 0)))),
    )
    mods_all = mods_all.reshape(dps, 2, seqs, 6 * wr).transpose(1, 0, 2, 3)
    mods_all = mods_all.reshape(2, dps * seqs, 6 * wr).astype(BF)
    silu_all = silu_all.reshape(dps, 8, wc)[:, :seqs].reshape(dps * seqs, wc).astype(BF)
    ada_gw = jnp.stack(
        [product_left(silu_all, mods_all[s]).reshape(wc, 6, wr) for s in range(2)]
    )
    ada_gb = jnp.sum(mods_all, axis=1, dtype=F32).reshape(2, 6, wr)
    silu_sum = jnp.sum(silu_part.reshape(rows, 8, wc), axis=0)[:seqs]
    condition_grad = silu_slope(cond_value, silu_sum)
    row_sums = lax.dynamic_index_in_dim(
        vectors[: 4 * rows * wr].reshape(2, 2, rows, wr), row, 2, keepdims=False
    )
    rest = vectors[4 * rows * wr : 4 * rows * wr + 2 * wf + 4 * wc]
    up_gb = rest[: 2 * wf].reshape(2, wf)
    qkv_gb = rest[2 * wf :].reshape(2, 2, wc)

    def finish(half_sum, second_part):
        first_part = join_over_dp(half_sum, dps, parity)
        return jnp.stack([first_part, sum_over_dp(second_part.astype(BF), dps)])

    text_h = text_h.transpose(2, 0, 1, 3)
    text_g = join_over_dp(text_h[None], dps, parity)
    text_g = text_g.reshape(2, share // 2, 2, rows, wr).transpose(2, 3, 0, 1, 4).reshape(2, wf, wr)
    up_g = jnp.stack([join_over_dp(up_h0, dps, parity), text_g[0].T])
    down_g = jnp.stack([join_over_dp(down_h0, dps, parity), text_g[1]])

    return (
        image_out,
        text_out,
        image_grad,
        text_grad[:TXT],
        condition_grad,
        ada_gw,
        ada_gb,
        finish(qkv_h0, qkv_g1).reshape(2, wr, 3, wc),
        qkv_gb,
        finish(out_h0, out_g1),
        row_sums[:, 1],
        up_g,
        up_gb,
        down_g,
        row_sums[:, 0],
    )


def solution(mesh):
    placed = (
        P(("dp", "col"), "row"),
        P(("dp", "col"), "row"),
        P("dp", "col"),
        P(None, "col", None, "row"),
        P(None, None, "row"),
        P(None, "row", None, "col"),
        P(None, None, "col"),
        P(None, "col", "row"),
        P(None, "row"),
        P(None, "row", "col"),
        P(None, "col"),
        P(None, "col", "row"),
        P(None, "row"),
        P(("dp", "col"), "row"),
        P(("dp", "col"), "row"),
    )
    sizes = [mesh.shape[name] for name in ("dp", "row", "col")]
    return jax.shard_map(
        functools.partial(shards, *sizes),
        mesh=mesh,
        in_specs=placed,
        out_specs=(
            P(("dp", "col"), "row"),
            P(("dp", "col"), "row"),
            P(("dp", "col"), "row"),
            P(("dp", "col"), "row"),
            P("dp", "col"),
            P(None, "col", None, "row"),
            P(None, None, "row"),
            P(None, "row", None, "col"),
            P(None, None, "col"),
            P(None, "col", "row"),
            P(None, "row"),
            P(None, "row", "col"),
            P(None, "col"),
            P(None, "col", "row"),
            P(None, "row"),
        ),
        check_vma=False,
    )
```

time: 3200 us -> 1160 us (0.36)
  waiting for transfers between devices: 1980 us -> 108 us
  blocking collectives: 619 us -> 0 us
  Pallas kernels: 0 us -> 612 us
  matrix products: 244 us -> 139 us
  starting transfers between devices: 70.9 us -> 28.7 us
  other arithmetic: 145 us -> 108 us
    reduce_scatter x8 -> x4, waiting for transfers between devices: 1190 us -> 5.88 us  [reduce_block(): return lax.psum_scatter(both, 'row', scatter_dimension=0)]
    pallas_call x0 -> x21, Pallas kernels: none -> 612 us  [the longest x19 561 us: exchange(): pl.pallas_call(functools.partial(exchange_kernel, ops), in_specs=[pl.Bloc...]
    all_gather x11 -> x3, waiting for transfers between devices: 596 us -> 0.02 us  [gather_block(): mine = lax.all_gather(half, 'row')]
    unnamed x6 -> x0, blocking collectives: 474 us -> none
    psum x2 -> x0, waiting for transfers between devices: 187 us -> none  [the longest x1 178 us: shards(): lax.psum(grad_qkv_w.astype(jnp.bfloat16), 'dp').astype(jnp.float32)]
    dot_general x20 -> x10, matrix products: 155 us -> 44.5 us  [product(): return jnp.dot(left, right, preferred_element_type=F32)]
    psum x6 -> x0, blocking collectives: 98.6 us -> none  [the longest x4 77.5 us: row_totals(): lax.psum((jnp.sum(image_first, axis=1), jnp.sum(image_second, axis=1), jn...]
    unnamed x8 -> x0, starting transfers between devices: 69.5 us -> none
  transfers between devices with their start and end apart: 29 -> 25, of which waited for: 23 -> 7; matrix products, arithmetic and copies ran while one was open for 22% -> 27% of each run, Pallas kernels for 0% -> 53%
where the time goes in v1:
time: 1160 us; the launch traced here: 1150 us
  Pallas kernels  612 us (53%)
  matrix products  139 us (12%)
  local copies, waits for them, and re-layouts  138 us (12%)
  other arithmetic  108 us (9%)
  waiting for transfers between devices  108 us (9%)
  starting transfers between devices  28.7 us (2%)
  between operations  15.9 us (1%)
    pallas_call x19, Pallas kernels, exchange(): pl.pallas_call(functools.partial(exchange_kernel, ops), in_specs=[pl.Bloc...  561 us
    dot_general x16, matrix products, product_left(): lax.dot_general(left, right, (((0,), (0,)), ((), ())), preferred_element_...  47.4 us
    dot_general x10, matrix products, product_right(): lax.dot_general(left, right, (((1,), (1,)), ((), ())), preferred_element_...  46.7 us
    dot_general x10, matrix products, product(): return jnp.dot(left, right, preferred_element_type=F32)  44.5 us
    all_to_all x1, waiting for transfers between devices, shards(): text_w = lax.all_to_all(text_w, 'row', 1, 1)  42.2 us
    unnamed x218, local copies, waits for them, and re-layouts  39.8 us
    pallas_call x1, Pallas kernels, attend_back(): pl.pallas_call(attend_back_kernel, grid=(pairs,), in_specs=[part(n, w) fo...  32.2 us
    ppermute x7, waiting for transfers between devices, shifted(): lax.ppermute(values, 'dp', [(i, (i + step) % count) for i in range(count)])  31.5 us
  transfers between devices with their start and end apart: 25, of which 7 were waited for; matrix products, arithmetic and copies ran while one was open for 27% of the time, Pallas kernels for 53%

profile of v1, /device:TPU:0, one launch (start us, length us, event | category | flops | bytes accessed | tf_op | source)
XLA Modules:
  0.0 1149.2 jit_solution(18129689171163132006)
XLA Ops:
  17.2 3.6 fusion.150
  20.8 3.9 copy.148
  31.8 8.5 exchange1.1
  42.9 63.0 %exchange2.1 = (bf16[256,1536]{1,0:T(8,128)(2,1)}, f32[128,384]{1,0:T(8,128)}, f32[32,160]{1,0:T(8,128)}) custom-call(bf16[1024,384]{1,0:T(8,128)(2,1)} %refs_0_.1, f32[32,384]{1,0:T(8,128)} %maximum_bitcast_fusion.1.refs_1_, f32[8,160]{1,0:T(8,128)} %fusion.105.refs_2_), custom_call_target="tpu_custom_call" | custom-call | bytes 105000000 | tf_op jit(solution)/shard_map/exchange2/pallas_call | solution.py:635
  113.9 42.9 %exchange3.1 = (bf16[640,384]{1,0:T(8,128)(2,1)}, bf16[1024,1536]{1,0:T(8,128)(2,1)}, bf16[256,1536]{1,0:T(8,128)(2,1)}) custom-call(bf16[160,384]{1,0:T(8,128)(2,1)} %get-tuple-element.294.refs_0_, bf16[256,1536]{1,0:T(8,128)(2,1)} %fusion.35.refs_1_, bf16[1024,384]{1,0:T(8,128)(2,1)} %refs_2_.1), custom_call_target="tpu_custom_call" | custom-call | bytes 94500000 | tf_op jit(solution)/shard_map/exchange3/pallas_call | solution.py:635
  156.9 3.2 convolution_convert_fusion.7.refs_0_
  161.2 67.6 %exchange4.1 = (f32[160,1152]{1,0:T(8,128)}, bf16[640,384]{1,0:T(8,128)(2,1)}, bf16[1024,1536]{1,0:T(8,128)(2,1)}) custom-call(bf16[640,1152]{1,0:T(8,128)(2,1)} %convolution_convert_fusion.7.refs_0_, bf16[160,384]{1,0:T(8,128)(2,1)} %get-tuple-element.293.refs_1_, bf16[256,1536]{1,0:T(8,128)(2,1)} %fusion.27.refs_2_), custom_call_target="tpu_custom_call" | custom-call | bytes 157500000 | tf_op jit(solution)/shard_map/exchange4/pallas_call | solution.py:635
  228.8 3.0 fusion.153
  233.3 7.6 all-to-all-start
  248.4 42.2 %all-to-all-done = bf16[2,4,192,384]{3,2,0,1:T(8,128)(2,1)S(1)} async-done(((bf16[2,4,192,384]{3,2,0,1:T(8,128)(2,1)}), bf16[2,4,192,384]{3,2,0,1:T(8,128)(2,1)S(1)}, u32[]{:S(2)}, u32[]{:S(2)}) %all-to-all-start) | async-done | bytes 1179680 | tf_op jit(solution)/shard_map/all_to_all | solution.py:740
  296.0 5.1 copy.170
  304.9 19.3 %collective-permute-done.3 = bf16[2,4,192,384]{3,2,1,0:T(8,128)(2,1)} collective-permute-done((bf16[2,4,192,384]{3,2,1,0:T(8,128)(2,1)}, bf16[2,4,192,384]{3,2,1,0:T(8,128)(2,1)}, u32[]{:S(2)}, u32[]{:S(2)}) %collective-permute-start.3) | collective-permute-done | bytes 1179680 | tf_op jit(solution)/shard_map/ppermute | solution.py:54
  340.0 8.6 add_convert_fusion.2.qi.ki.vi
  348.6 18.9 %attend.1 = (bf16[1024,384]{1,0:T(8,128)(2,1)}, bf16[160,384]{1,0:T(8,128)(2,1)}, f32[3,8,1024]{2,1,0:T(8,128)}, f32[3,8,160]{2,1,0:T(8,128)}) custom-call(bf16[1024,1152]{1,0:T(8,128)(2,1)} %add_convert_fusion.2.qi.ki.vi, bf16[1024,1152]{1,0:T(8,128)(2,1)} %add_convert_fusion.2.qi.ki.vi, bf16[1024,1152]{1,0:T(8,128)(2,1)} %add_convert_fusion.2.qi.ki.vi, ...), custom_call_target="tpu_custom_call" | custom-call | bytes 66500000 | tf_op jit(solution)/shard_map/attend/pallas_call | solution.py:196
  367.5 18.7 %exchange6.1 = (bf16[640,384]{1,0:T(8,128)(2,1)}, bf16[640,1536]{1,0:T(8,128)(2,1)}) custom-call(bf16[160,384]{1,0:T(8,128)(2,1)} %get-tuple-element.76.refs_0_.ot, bf16[160,1536]{1,0:T(8,128)(2,1)} %bitcast.407), custom_call_target="tpu_custom_call" | custom-call | bytes 49000000 | tf_op jit(solution)/shard_map/exchange6/pallas_call | solution.py:635
  388.4 5.0 convolution_convert_fusion.2.refs_1_
  393.4 27.5 %exchange7.1 = (f32[160,384]{1,0:T(8,128)}, f32[256,1536]{1,0:T(8,128)}) custom-call(bf16[640,384]{1,0:T(8,128)(2,1)} %convolution_convert_fusion.18.refs_0_, bf16[1024,1536]{1,0:T(8,128)(2,1)} %convolution_convert_fusion.2.refs_1_), custom_call_target="tpu_custom_call" | custom-call | bytes 87500000 | tf_op jit(solution)/shard_map/exchange7/pallas_call | solution.py:635
  429.5 24.2 %exchange8.1 = (f32[32,160]{1,0:T(8,128)}, bf16[1024,1536]{1,0:T(8,128)(2,1)}) custom-call(f32[8,160]{1,0:T(8,128)} %fusion.106.refs_0_, bf16[256,1536]{1,0:T(8,128)(2,1)} %add_convert_fusion.6.refs_1_), custom_call_target="tpu_custom_call" | custom-call | bytes 77000000 | tf_op jit(solution)/shard_map/exchange8/pallas_call | solution.py:635
  453.8 4.6 copy.158
  458.4 9.8 fusion.163
  473.1 6.6 copy.154
  479.7 13.0 %convert_reduce_fusion = (f32[1536]{0:T(1024)}, bf16[1024,1536]{1,0:T(8,128)(2,1)S(1)}, bf16[1024,1536]{1,0:T(8,128)(2,1)S(1)}) fusion(f32[1024,1536]{1,0:T(8,128)} %fusion.163, f32[1536]{0:T(1024)S(1)} %convert_reduce_fusion.11, bf16[1024,1536]{1,0:T(8,128)(2,1)} %get-tuple-element.77, bf16[1536,1536]{0,1:T(8,128)(2,1)} %bitcast.389), kind=kOutput, calls=%fused_computation.10 | convolution fusion | flops 4871158272 | bytes 20459520 | tf_op jit(solution)/shard_map/dot_general | solution.py:30
  492.7 11.1 convolution_convert_fusion.1.refs_0_
  503.8 6.4 convolution_convert_fusion.refs_1_
  510.2 4.0 convolution_convert_fusion.5
  514.2 4.2 convolution_convert_fusion.4
  522.1 14.0 %exchange9.1 = bf16[640,384]{1,0:T(8,128)(2,1)} custom-call(bf16[160,384]{1,0:T(8,128)(2,1)} %add_convert_fusion.8.refs_0_), custom_call_target="tpu_custom_call" | custom-call | bytes 45500000 | tf_op jit(solution)/shard_map/exchange9/pallas_call | solution.py:635
  538.3 16.8 %exchange10.1 = bf16[640,1536]{1,0:T(8,128)(2,1)} custom-call(bf16[160,1536]{1,0:T(8,128)(2,1)} %bitcast.406), custom_call_target="tpu_custom_call" | custom-call | bytes 45500000 | tf_op jit(solution)/shard_map/exchange10/pallas_call | solution.py:635
  555.1 3.1 fusion.164
  564.0 36.2 %exchange11.1 = (f32[256,1536]{1,0:T(8,128)}, f32[160,1536]{1,0:T(8,128)}) custom-call(bf16[1024,1536]{1,0:T(8,128)(2,1)} %convolution_convert_fusion.1.refs_0_, bf16[640,1536]{1,0:T(8,128)(2,1)} %convolution_convert_fusion.9.refs_1_), custom_call_target="tpu_custom_call" | custom-call | bytes 122500000 | tf_op jit(solution)/shard_map/exchange11/pallas_call | solution.py:635
  607.2 25.4 %exchange12.1 = (f32[160,384]{1,0:T(8,128)}, bf16[1024,1536]{1,0:T(8,128)(2,1)}) custom-call(bf16[640,384]{1,0:T(8,128)(2,1)} %bitcast.408, bf16[256,1536]{1,0:T(8,128)(2,1)} %multiply_convert_fusion.1.refs_1_), custom_call_target="tpu_custom_call" | custom-call | bytes 77000000 | tf_op jit(solution)/shard_map/exchange12/pallas_call | solution.py:635
  632.7 3.0 convolution_convert_fusion.11
  646.2 2.8 convolution_convert_fusion.16.gi
  649.0 6.9 collective-permute-done.6
  656.9 3.3 fusion.14
  666.5 5.8 fusion.49
  672.3 5.8 reduce-scatter.9.cloned.1.call-done
  684.0 3.5 all-to-all-start.1
  689.5 7.2 add_convert_fusion.1
  696.7 5.0 add_convert_fusion
  701.8 28.0 %exchange13.1 = (f32[32,160]{1,0:T(8,128)}, f32[160,1536]{1,0:T(8,128)}) custom-call(f32[8,160]{1,0:T(8,128)} %fusion.107.refs_0_, bf16[640,1536]{1,0:T(8,128)(2,1)} %convolution_convert_fusion.8.refs_1_), custom_call_target="tpu_custom_call" | custom-call | bytes 56000000 | tf_op jit(solution)/shard_map/exchange13/pallas_call | solution.py:635
  734.0 8.8 exchange14.1
  745.1 28.1 %exchange15.1 = (f32[160,384]{1,0:T(8,128)}, f32[256,1536]{1,0:T(8,128)}) custom-call(bf16[640,384]{1,0:T(8,128)(2,1)} %convolution_convert_fusion.17.refs_0_, bf16[1024,1536]{1,0:T(8,128)(2,1)} %convolution_convert_fusion.refs_1_), custom_call_target="tpu_custom_call" | custom-call | bytes 77000000 | tf_op jit(solution)/shard_map/exchange15/pallas_call | solution.py:635
  774.8 32.2 %attend_back.1 = (bf16[1024,384]{1,0:T(8,128)(2,1)}, bf16[1024,384]{1,0:T(8,128)(2,1)}, bf16[1024,384]{1,0:T(8,128)(2,1)}, bf16[160,384]{1,0:T(8,128)(2,1)}, bf1...) custom-call(bf16[1024,1152]{1,0:T(8,128)(2,1)} %add_convert_fusion.2.qi.ki.vi, ...), custom_call_target="tpu_custom_call" | custom-call | bytes 112000000 | tf_op jit(solution)/shard_map/attend_back/pallas_call | solution.py:271
  810.0 3.4 convolution_convert_fusion.6
  814.9 6.0 convolution_convert_fusion.3.refs_1_
  840.0 42.4 %exchange16.1 = (bf16[640,1152]{1,0:T(8,128)(2,1)}, f32[256,1536]{1,0:T(8,128)}, f32[128,384]{1,0:T(8,128)}) custom-call(bf16[160,1152]{1,0:T(8,128)(2,1)} %copy-done.37, bf16[1024,1536]{1,0:T(8,128)(2,1)} %convolution_convert_fusion.3.refs_1_, f32[32,384]{1,0:T(8,128)} %pad.54.refs_2_), custom_call_target="tpu_custom_call" | custom-call | bytes 122500000 | tf_op jit(solution)/shard_map/exchange16/pallas_call | solution.py:635
  884.2 3.0 fusion.28
  894.1 3.4 convolution_convert_fusion.10
  905.9 20.8 %collective-permute-done.11 = bf16[384,384]{1,0:T(8,128)(2,1)} collective-permute-done((bf16[384,384]{1,0:T(8,128)(2,1)S(1)}, bf16[384,384]{1,0:T(8,128)(2,1)}, u32[]{:S(2)}, u32[]{:S(2)}) %collective-permute-start.11) | collective-permute-done | bytes 294944 | tf_op jit(solution)/shard_map/ppermute | solution.py:50
  928.9 2.8 convert_add_fusion.2
  934.5 4.0 copy.177
  938.5 10.7 collective-permute-done.14
  951.4 2.9 fusion.149
  955.7 4.9 add_convert_fusion.3
  962.7 65.8 %exchange17.1 = (f32[160,384]{1,0:T(8,128)}, f32[160,384]{1,0:T(8,128)}, f32[64,384]{1,0:T(8,128)}, bf16[1024,384]{1,0:T(8,128)(2,1)}, bf16[1024,384]{1,0:T(8,128)(2,1)}) custom-call(bf16[640,384]{1,0:T(8,128)(2,1)} %convolution_convert_fusion.19.refs_0_, bf16[640,384]{1,0:T(8,128)(2,1)} %bitcast.405, f32[32,384]{1,0:T(8,128)} %reduce_sum.438.refs_2_, ...), custom_call_target="tpu_custom_call" | custom-call | bytes 129500000 | tf_op jit(solution)/shard_map/exchange17/pallas_call | solution.py:635
  1032.0 20.7 %exchange18.1 = (f32[32,160]{1,0:T(8,128)}, f32[32,1536]{1,0:T(8,128)}, f32[32,384]{1,0:T(8,128)}) custom-call(f32[8,160]{1,0:T(8,128)} %select_maximum_fusion.refs_0_, f32[8,1536]{1,0:T(8,128)} %pad.56.refs_1_, f32[8,384]{1,0:T(8,128)} %pad.57.refs_2_), custom_call_target="tpu_custom_call" | custom-call | bytes 35000000 | tf_op jit(solution)/shard_map/exchange18/pallas_call | solution.py:635
  1055.1 9.1 exchange19.1
  1071.2 13.5 %exchange20.1 = (f32[16,2304]{1,0:T(8,128)}, f32[16,384]{1,0:T(8,128)}, f32[32,384]{1,0:T(8,128)}) custom-call(f32[8,2304]{1,0:T(8,128)} %bitcast.429, f32[8,384]{1,0:T(8,128)} %pad_convert_fusion.refs_1_, f32[8,384]{1,0:T(8,128)} %pad.60.refs_2_), custom_call_target="tpu_custom_call" | custom-call | bytes 31500000 | tf_op jit(solution)/shard_map/exchange20/pallas_call | solution.py:635
  1100.1 6.5 pad_maximum_fusion
  1110.6 4.9 pad_maximum_fusion.5
  1117.0 6.0 copy.184
  1125.0 4.9 pad_maximum_fusion.6
  1132.4 4.0 stack.278
  (485 shorter events, 224.9 us)
Async XLA Ops:
  7.2 238.4 %all-gather.4.cloned.1.call-start = ((), (), s32[]{:S(2)}) async-start(), calls=%async_computation.6 | async-start | bytes 2949120 | tf_op jit(solution)/shard_map/all_gather | solution.py:85
  13.5 317.7 %all-gather.8.cloned.1.call-start = ((), (), s32[]{:S(2)}) async-start(), calls=%async_computation.8 | async-start | bytes 2949120 | tf_op jit(solution)/shard_map/all_gather | solution.py:85
  27.0 14.4 %copy-start.84 = (bf16[2,6,384]{2,0,1:T(2,128)(2,1)S(1)}, bf16[2,6,384]{2,0,1:T(2,128)(2,1)}, u32[]{:S(2)}) copy-start(bf16[2,6,384]{2,0,1:T(2,128)(2,1)} %param.19) | copy-start | bytes 27652
  29.0 12.5 %copy-start.38 = (bf16[154,384]{1,0:T(8,128)(2,1)S(1)}, bf16[154,384]{1,0:T(8,128)(2,1)}, u32[]{:S(2)}) copy-start(bf16[154,384]{1,0:T(8,128)(2,1)} %param.16) | copy-start | bytes 354820
  29.0 12.6 %copy-start.86 = (bf16[2,384]{1,0:T(2,128)(2,1)S(1)}, bf16[2,384]{1,0:T(2,128)(2,1)}, u32[]{:S(2)}) copy-start(bf16[2,384]{1,0:T(2,128)(2,1)} %param.23) | copy-start | bytes 4612
  29.0 12.6 %copy-start.87 = (bf16[2,384]{1,0:T(2,128)(2,1)S(1)}, bf16[2,384]{1,0:T(2,128)(2,1)}, u32[]{:S(2)}) copy-start(bf16[2,384]{1,0:T(2,128)(2,1)} %param.27) | copy-start | bytes 4612
  40.3 69.7 %copy-start.17 = (bf16[1,384,1536]{2,1,0:T(8,128)(2,1)S(1)}, bf16[1,384,1536]{2,1,0:T(8,128)(2,1)}, u32[]{:S(2)}) copy-start(bf16[1,384,1536]{2,1,0:T(8,128)(2,1)} %get-tuple-element.251) | copy-start | bytes 3538948
  110.0 50.2 %copy-start.64 = (f32[1536]{0:T(1024)}, f32[1536]{0:T(1024)S(1)}, u32[]{:S(2)}) copy-start(f32[1536]{0:T(1024)S(1)} %mul.479) | copy-start | bytes 18436
  111.4 45.5 %copy-start.24 = (bf16[1,384,3,384]{1,3,2,0:T(8,128)(2,1)S(1)}, bf16[1,384,3,384]{1,3,2,0:T(8,128)(2,1)}, u32[]{:S(2)}) copy-start(bf16[1,384,3,384]{1,3,2,0:T(8,128)(2,1)} %copy.188) | copy-start | bytes 2654212
  111.4 48.7 %copy-start.70 = (f32[384]{0:T(512)}, f32[384]{0:T(512)S(1)}, u32[]{:S(2)}) copy-start(f32[384]{0:T(512)S(1)} %get-tuple-element.217) | copy-start | bytes 4612
  111.5 48.7 %copy-start.72 = (f32[384]{0:T(512)}, f32[384]{0:T(512)S(1)}, u32[]{:S(2)}) copy-start(f32[384]{0:T(512)S(1)} %get-tuple-element.219) | copy-start | bytes 4612
  111.8 48.3 %copy-start.76 = (f32[1,160]{1,0:T(1,128)}, f32[1,160]{1,0:T(1,128)S(1)}, u32[]{:S(2)}) copy-start(f32[1,160]{1,0:T(1,128)S(1)} %get-tuple-element.285) | copy-start | bytes 1924
  111.9 48.3 %copy-start.74 = (f32[160]{0:T(256)}, f32[160]{0:T(256)S(1)}, u32[]{:S(2)}) copy-start(f32[160]{0:T(256)S(1)} %add_rsqrt_fusion.3) | copy-start | bytes 1924
  111.9 48.2 %copy-start.79 = (f32[256]{0:T(256)}, f32[256]{0:T(256)S(1)}, u32[]{:S(2)}) copy-start(f32[256]{0:T(256)S(1)} %get-tuple-element.289) | copy-start | bytes 3076
  111.9 48.2 %copy-start.81 = (f32[256]{0:T(256)}, f32[256]{0:T(256)S(1)}, u32[]{:S(2)}) copy-start(f32[256]{0:T(256)S(1)} %get-tuple-element.290) | copy-start | bytes 3076
  233.3 9.7 copy-start.83
  233.3 57.3 %all-to-all-start = ((bf16[2,4,192,384]{3,2,0,1:T(8,128)(2,1)}), bf16[2,4,192,384]{3,2,0,1:T(8,128)(2,1)S(1)}, u32[]{:S(2)}, u32[]{:S(2)}) async-start(bf16[2,4,192,384]{3,2,0,1:T(8,128)(2,1)} %copy.160), calls=%async_computation | async-start | bytes 2359296 | tf_op jit(solution)/shard_map/all_to_all | solution.py:740
  241.0 91.7 %all-gather.6.cloned.1.call-start = ((), (), s32[]{:S(2)}) async-start(), calls=%async_computation.7 | async-start | bytes 2949120 | tf_op jit(solution)/shard_map/all_gather | solution.py:85
  242.9 435.2 %reduce-scatter.9.cloned.1.call-start = ((), (), s32[]{:S(2)}) async-start(), calls=%async_computation.11 | async-start | bytes 737280 | tf_op jit(solution)/shard_map/reduce_scatter | solution.py:795
  245.5 50.4 %copy-start.68 = (bf16[2,1536]{1,0:T(2,128)(2,1)S(1)}, bf16[2,1536]{1,0:T(2,128)(2,1)}, u32[]{:S(2)}) copy-start(bf16[2,1536]{1,0:T(2,128)(2,1)} %param.25) | copy-start | bytes 18436
  245.6 87.6 %collective-permute-start = (bf16[4,192,1536]{2,1,0:T(8,128)(2,1)}, bf16[4,192,1536]{2,1,0:T(8,128)(2,1)}, u32[]{:S(2)}, u32[]{:S(2)}) collective-permute-start(bf16[4,192,1536]{2,1,0:T(8,128)(2,1)} %all-gather.4.cloned.1.call-done), channel_id=1, source_target_pairs={{0,16},{16,0},{1,17},{17,1},{2,18},{18,2},{3,19},{19,3},{4,20},{20... | collective-permute-start | bytes 7077896 | tf_op jit(solution)/shard_map/ppermute | solution.py:54
  291.8 32.5 %collective-permute-start.3 = (bf16[2,4,192,384]{3,2,1,0:T(8,128)(2,1)}, bf16[2,4,192,384]{3,2,1,0:T(8,128)(2,1)}, u32[]{:S(2)}, u32[]{:S(2)}) collective-permute-start(bf16[2,4,192,384]{3,2,1,0:T(8,128)(2,1)} %copy.162), channel_id=1, source_target_pairs={{0,16},{16,0},{1,17},{17,1},{2,18},{18,2},{3,19},{19,3},{4,20},{20... | collective-permute-start | bytes 3538952 | tf_op jit(solution)/shard_map/ppermute | solution.py:54
  331.1 89.7 %collective-permute-start.2 = (bf16[4,192,1536]{2,1,0:T(8,128)(2,1)}, bf16[4,192,1536]{2,1,0:T(8,128)(2,1)}, u32[]{:S(2)}, u32[]{:S(2)}) collective-permute-start(bf16[4,192,1536]{2,1,0:T(8,128)(2,1)} %all-gather.8.cloned.1.call-done), channel_id=1, source_target_pairs={{0,16},{16,0},{1,17},{17,1},{2,18},{18,2},{3,19},{19,3},{4,20},{20... | collective-permute-start | bytes 7077896 | tf_op jit(solution)/shard_map/ppermute | solution.py:54
  332.6 135.6 %collective-permute-start.1 = (bf16[4,768,384]{2,1,0:T(8,128)(2,1)}, bf16[4,768,384]{2,1,0:T(8,128)(2,1)}, u32[]{:S(2)}, u32[]{:S(2)}) collective-permute-start(bf16[4,768,384]{2,1,0:T(8,128)(2,1)} %all-gather.6.cloned.1.call-done), channel_id=1, source_target_pairs={{0,16},{16,0},{1,17},{17,1},{2,18},{18,2},{3,19},{19,3},{4,20},{20... | collective-permute-start | bytes 7077896 | tf_op jit(solution)/shard_map/ppermute | solution.py:54
  348.6 37.6 %copy-start.40 = (bf16[2,384,384]{2,1,0:T(8,128)(2,1)S(1)}, bf16[2,384,384]{2,1,0:T(8,128)(2,1)}, u32[]{:S(2)}) copy-start(bf16[2,384,384]{2,1,0:T(8,128)(2,1)} %param.22) | copy-start | bytes 1769476
  424.7 238.0 %copy-start.14 = (f32[160,384]{1,0:T(8,128)}, f32[160,384]{1,0:T(8,128)S(1)}, u32[]{:S(2)}) copy-start(f32[160,384]{1,0:T(8,128)S(1)} %get-tuple-element.233) | copy-start | bytes 737284
  458.4 9.8 copy-start.33
  492.7 17.5 %copy-start.95 = (bf16[1024,1536]{1,0:T(8,128)(2,1)}, bf16[1024,1536]{1,0:T(8,128)(2,1)S(1)}, u32[]{:S(2)}) copy-start(bf16[1024,1536]{1,0:T(8,128)(2,1)S(1)} %get-tuple-element.234) | copy-start | bytes 9437188
  492.7 21.5 %copy-start.96 = (bf16[1024,1536]{1,0:T(8,128)(2,1)}, bf16[1024,1536]{1,0:T(8,128)(2,1)S(1)}, u32[]{:S(2)}) copy-start(bf16[1024,1536]{1,0:T(8,128)(2,1)S(1)} %get-tuple-element.231) | copy-start | bytes 9437188
  492.7 11.1 copy-start.16
  518.4 171.1 %collective-permute-start.4 = (bf16[4,192,1536]{2,1,0:T(8,128)(2,1)}, bf16[4,192,1536]{2,1,0:T(8,128)(2,1)}, u32[]{:S(2)}, u32[]{:S(2)}) collective-permute-start(bf16[4,192,1536]{2,1,0:T(8,128)(2,1)} %convolution_convert_fusion.4), channel_id=1, source_target_pairs={{0,16},{16,0},{1,17},{17,1},{2,18},{18,2},{3,19},{19,3},{4,20},{20... | collective-permute-start | bytes 7077896 | tf_op jit(solution)/shard_map/ppermute | solution.py:54
  519.9 176.7 %collective-permute-start.5 = (bf16[4,768,384]{1,2,0:T(8,128)(2,1)}, bf16[4,768,384]{1,2,0:T(8,128)(2,1)}, u32[]{:S(2)}, u32[]{:S(2)}) collective-permute-start(bf16[4,768,384]{1,2,0:T(8,128)(2,1)} %bitcast.39), channel_id=1, source_target_pairs={{0,16},{16,0},{1,17},{17,1},{2,18},{18,2},{3,19},{19,3},{4,20},{20... | collective-permute-start | bytes 7077896 | tf_op jit(solution)/shard_map/ppermute | solution.py:54
  521.3 141.4 %copy-start.78 = (f32[160]{0:T(256)}, f32[160]{0:T(256)S(1)}, u32[]{:S(2)}) copy-start(f32[160]{0:T(256)S(1)} %add_rsqrt_fusion) | copy-start | bytes 1924
  560.7 84.8 %copy-start.54 = (bf16[640,384]{0,1:T(8,128)(2,1)}, bf16[640,384]{0,1:T(8,128)(2,1)S(1)}, u32[]{:S(2)}) copy-start(bf16[640,384]{0,1:T(8,128)(2,1)S(1)} %get-tuple-element.263) | copy-start | bytes 1474564
  639.7 16.2 %collective-permute-start.6 = (bf16[4,192,384]{2,1,0:T(8,128)(2,1)S(1)}, bf16[4,192,384]{2,1,0:T(8,128)(2,1)S(1)}, u32[]{:S(2)}, u32[]{:S(2)}) collective-permute-start(bf16[4,192,384]{2,1,0:T(8,128)(2,1)S(1)} %bitcast.422), channel_id=1, source_target_pairs={{0,16},{16,0},{1,17},{17,1},{2,18},{18,2},{3,19},{19,3},{4,20},{20... | collective-permute-start | bytes 1769480 | tf_op jit(solution)/shard_map/ppermute | solution.py:54
  642.4 38.9 %collective-permute-start.13 = (bf16[2,192,1536]{2,1,0:T(8,128)(2,1)}, bf16[2,192,1536]{2,1,0:T(8,128)(2,1)}, u32[]{:S(2)}, u32[]{:S(2)}) collective-permute-start(bf16[2,192,1536]{2,1,0:T(8,128)(2,1)} %pad_maximum_fusion.12), channel_id=1, source_target_pairs={{0,16},{16,0},{1,17},{17,1},{2,18},{18,2},{3,19},{19,3},{4,20},{20... | collective-permute-start | bytes 3538952 | tf_op jit(solution)/shard_map/ppermute | solution.py:54
  666.5 14.8 %copy-start.31 = (bf16[1,192,1536]{2,1,0:T(8,128)(2,1)S(1)}, bf16[1,192,1536]{2,1,0:T(8,128)(2,1)}, u32[]{:S(2)}) copy-start(bf16[1,192,1536]{2,1,0:T(8,128)(2,1)} %fusion.14) | copy-start | bytes 1769476
  678.1 9.5 collective-permute-start.10
  684.0 218.4 %all-to-all-start.1 = ((bf16[2,4,192,384]{3,2,0,1:T(8,128)(2,1)}), bf16[2,4,192,384]{3,2,0,1:T(8,128)(2,1)S(1)}, u32[]{:S(2)}, u32[]{:S(2)}) async-start(bf16[2,4,192,384]{3,2,0,1:T(8,128)(2,1)} %bitcast.391), calls=%async_computation.5 | async-start | bytes 2359296 | tf_op jit(solution)/shard_map/all_to_all | solution.py:855
  687.5 273.1 %reduce-scatter.5.cloned.1.call-start = ((), (), s32[]{:S(2)}) async-start(), calls=%async_computation.9 | async-start | bytes 2949120 | tf_op jit(solution)/shard_map/reduce_scatter | solution.py:795
  701.7 384.8 %reduce-scatter.11.cloned.1.call-start = ((), (), s32[]{:S(2)}) async-start(), calls=%async_computation.12 | async-start | bytes 2949120 | tf_op jit(solution)/shard_map/reduce_scatter | solution.py:795
  813.4 140.9 %collective-permute-start.7 = (bf16[4,192,1152]{2,1,0:T(8,128)(2,1)}, bf16[4,192,1152]{2,1,0:T(8,128)(2,1)}, u32[]{:S(2)}, u32[]{:S(2)}) collective-permute-start(bf16[4,192,1152]{2,1,0:T(8,128)(2,1)} %convolution_convert_fusion.6), channel_id=1, source_target_pairs={{0,16},{16,0},{1,17},{17,1},{2,18},{18,2},{3,19},{19,3},{4,20},{20... | collective-permute-start | bytes 5308424 | tf_op jit(solution)/shard_map/ppermute | solution.py:54
  840.0 44.1 %copy-start.65 = (f32[1536]{0:T(1024)S(1)}, f32[1536]{0:T(1024)}, u32[]{:S(2)}) copy-start(f32[1536]{0:T(1024)} %copy-done.64) | copy-start | bytes 18436
  884.1 222.5 %reduce-scatter.7.cloned.1.call-start = ((), (), s32[]{:S(2)}) async-start(), calls=%async_computation.10 | async-start | bytes 2211840 | tf_op jit(solution)/shard_map/reduce_scatter | solution.py:795
  897.4 31.5 %collective-permute-start.9 = (bf16[384,1152]{1,0:T(8,128)(2,1)}, bf16[384,1152]{1,0:T(8,128)(2,1)}, u32[]{:S(2)}, u32[]{:S(2)}) collective-permute-start(bf16[384,1152]{1,0:T(8,128)(2,1)} %convolution_convert_fusion.10), channel_id=1, source_target_pairs={{0,16},{16,0},{1,17},{17,1},{2,18},{18,2},{3,19},{19,3},{4,20},{20... | collective-permute-start | bytes 2654216 | tf_op jit(solution)/shard_map/ppermute | solution.py:50
  900.7 25.9 %collective-permute-start.11 = (bf16[384,384]{1,0:T(8,128)(2,1)S(1)}, bf16[384,384]{1,0:T(8,128)(2,1)}, u32[]{:S(2)}, u32[]{:S(2)}) collective-permute-start(bf16[384,384]{1,0:T(8,128)(2,1)S(1)} %convolution_convert_fusion.20), channel_id=1, source_target_pairs={{0,16},{16,0},{1,17},{17,1},{2,18},{18,2},{3,19},{19,3},{4,20},{20... | collective-permute-start | bytes 884744 | tf_op jit(solution)/shard_map/ppermute | solution.py:50
  903.5 24.3 %copy-start.32 = (f32[2,192,384]{2,1,0:T(8,128)S(1)}, f32[2,192,384]{2,1,0:T(8,128)}, u32[]{:S(2)}) copy-start(f32[2,192,384]{2,1,0:T(8,128)} %pad_maximum_fusion.14) | copy-start | bytes 1769476
  903.5 45.7 %collective-permute-start.14 = (bf16[1,192,2,4,384]{4,1,3,2,0:T(8,128)(2,1)}, bf16[1,192,2,4,384]{4,1,3,2,0:T(8,128)(2,1)}, u32[]{:S(2)}, u32[]{:S(2)}) collective-permute-start(bf16[1,192,2,4,384]{4,1,3,2,0:T(8,128)(2,1)} %bitcast.358), channel_id=1, source_target_pairs={{0,16},{16,0},{1,17},{17,1},{2,18},{18,2},{3,19},{19,3},{4,20},{20... | collective-permute-start | bytes 3538952 | tf_op jit(solution)/shard_map/ppermute | solution.py:50
  961.8 66.7 %copy-start.39 = (bf16[154,384]{1,0:T(8,128)(2,1)S(1)}, bf16[154,384]{1,0:T(8,128)(2,1)}, u32[]{:S(2)}) copy-start(bf16[154,384]{1,0:T(8,128)(2,1)} %param.16) | copy-start | bytes 354820
  961.8 66.7 %copy-start.73 = (f32[384]{0:T(512)S(1)}, f32[384]{0:T(512)}, u32[]{:S(2)}) copy-start(f32[384]{0:T(512)} %copy-done.72) | copy-start | bytes 4612
  961.8 66.7 %copy-start.75 = (f32[160]{0:T(256)S(1)}, f32[160]{0:T(256)}, u32[]{:S(2)}) copy-start(f32[160]{0:T(256)} %copy-done.74) | copy-start | bytes 1924
  961.8 66.8 %copy-start.77 = (f32[1,160]{1,0:T(1,128)S(1)}, f32[1,160]{1,0:T(1,128)}, u32[]{:S(2)}) copy-start(f32[1,160]{1,0:T(1,128)} %copy-done.76) | copy-start | bytes 1924
  961.9 67.9 %copy-start.45 = (bf16[154,384]{1,0:T(8,128)(2,1)S(1)}, bf16[154,384]{1,0:T(8,128)(2,1)}, u32[]{:S(2)}) copy-start(bf16[154,384]{1,0:T(8,128)(2,1)} %param.29) | copy-start | bytes 354820
  961.9 67.9 %copy-start.85 = (f32[384]{0:T(512)S(1)}, f32[384]{0:T(512)}, u32[]{:S(2)}) copy-start(f32[384]{0:T(512)} %convert_reduce_fusion.12) | copy-start | bytes 4612
  961.9 68.9 %copy-start.88 = (f32[1,384]{1,0:T(1,128)S(1)}, f32[1,384]{1,0:T(1,128)}, u32[]{:S(2)}) copy-start(f32[1,384]{1,0:T(1,128)} %stack.267) | copy-start | bytes 4612
  961.9 68.9 %copy-start.89 = (f32[1,384]{1,0:T(1,128)S(1)}, f32[1,384]{1,0:T(1,128)}, u32[]{:S(2)}) copy-start(f32[1,384]{1,0:T(1,128)} %stack.268) | copy-start | bytes 4612
  1028.5 38.7 %copy-start.63 = (f32[64,384]{1,0:T(8,128)S(1)}, f32[64,384]{1,0:T(8,128)}, u32[]{:S(2)}) copy-start(f32[64,384]{1,0:T(8,128)} %get-tuple-element.120) | copy-start | bytes 294916
  1067.3 28.3 %copy-start.60 = (f32[32,384]{1,0:T(8,128)}, f32[32,384]{1,0:T(8,128)S(1)}, u32[]{:S(2)}) copy-start(f32[32,384]{1,0:T(8,128)S(1)} %reduce_sum.459) | copy-start | bytes 147460
  1067.3 48.1 %collective-permute-start.15 = (bf16[768,384]{0,1:T(8,128)(2,1)}, bf16[768,384]{0,1:T(8,128)(2,1)}, u32[]{:S(2)}, u32[]{:S(2)}) collective-permute-start(bf16[768,384]{0,1:T(8,128)(2,1)} %bitcast.85), channel_id=1, source_target_pairs={{0,16},{16,0},{1,17},{17,1},{2,18},{18,2},{3,19},{19,3},{4,20},{20... | collective-permute-start | bytes 1769480 | tf_op jit(solution)/shard_map/ppermute | solution.py:50
  1070.5 21.3 %copy-start.67 = (bf16[4,384]{1,0:T(4,128)(2,1)S(1)}, bf16[4,384]{1,0:T(4,128)(2,1)}, u32[]{:S(2)}) copy-start(bf16[4,384]{1,0:T(4,128)(2,1)} %param.17) | copy-start | bytes 9220
  1070.5 21.9 %copy-start.15 = (f32[160,384]{1,0:T(8,128)S(1)}, f32[160,384]{1,0:T(8,128)}, u32[]{:S(2)}) copy-start(f32[160,384]{1,0:T(8,128)} %copy-done.14) | copy-start | bytes 737284
  1070.5 21.9 %copy-start.71 = (f32[384]{0:T(512)S(1)}, f32[384]{0:T(512)}, u32[]{:S(2)}) copy-start(f32[384]{0:T(512)} %copy-done.70) | copy-start | bytes 4612
  1086.5 21.6 %collective-permute-start.12 = (bf16[192,1536]{1,0:T(8,128)(2,1)}, bf16[192,1536]{1,0:T(8,128)(2,1)S(1)}, u32[]{:S(2)}, u32[]{:S(2)}) collective-permute-start(bf16[192,1536]{1,0:T(8,128)(2,1)} %bitcast.424), channel_id=1, source_target_pairs={{0,16},{16,0},{1,17},{17,1},{2,18},{18,2},{3,19},{19,3},{4,20},{20... | collective-permute-start | bytes 1769480 | tf_op jit(solution)/shard_map/ppermute | solution.py:50
  1106.6 23.3 %collective-permute-start.8 = (bf16[192,1152]{1,0:T(8,128)(2,1)}, bf16[192,1152]{1,0:T(8,128)(2,1)}, u32[]{:S(2)}, u32[]{:S(2)}) collective-permute-start(bf16[192,1152]{1,0:T(8,128)(2,1)} %bitcast.427), channel_id=1, source_target_pairs={{0,16},{16,0},{1,17},{17,1},{2,18},{18,2},{3,19},{19,3},{4,20},{20... | collective-permute-start | bytes 1327112 | tf_op jit(solution)/shard_map/ppermute | solution.py:50
  (61 other events, 225.7 us)
Sparse Core Ops, SparseCore 0:
  13.6 81.2 all-gather.3
  97.0 77.9 all-gather.7
  243.9 64.3 all-gather.5
  657.0 21.0 reduce-scatter.8
  701.9 53.8 reduce-scatter.4
  884.2 46.2 reduce-scatter.10
  960.7 65.0 reduce-scatter.6

commit v2 on v1

--- a/solution.py
+++ b/solution.py
@@ -46,45 +46,36 @@
     return lax.all_gather(values, axis_name, axis=axis, tiled=True)
 
 
-def shifted(values, count, step):
-    return lax.ppermute(values, "dp", [(i, (i + step) % count) for i in range(count)])
-
-
-def partner(values, count):
-    return lax.ppermute(values, "dp", [(i, i ^ 1) for i in range(count)])
-
-
-def in_order(mine, other, parity, axis):
-    first = jnp.where(parity == 0, mine, other)
-    second = jnp.where(parity == 0, other, mine)
-    return jnp.stack([first, second], axis=axis)
-
-
-def sum_over_dp(values, count):
-    total = values.astype(F32)
-    for step in range(1, count):
-        total = total + shifted(values, count, step).astype(F32)
-    return total
-
-
-def join_over_dp(values, count, parity):
-    mine = values.astype(F32)
-    other = shifted(values, count, 1).astype(F32)
-    for step in range(2, count):
-        moved = shifted(values, count, step).astype(F32)
-        if step % 2:
-            other = other + moved
-        else:
-            mine = mine + moved
-    joined = in_order(mine, other, parity, 0)
-    return joined.reshape((-1,) + values.shape[1:])
-
-
-def gather_block(block, count, parity):
-    half = lax.dynamic_index_in_dim(block.reshape(2, -1, block.shape[1]), parity, 0, keepdims=False)
-    mine = lax.all_gather(half, "row")
-    both = in_order(mine, partner(mine, count), parity, 1)
-    return both.reshape(mine.shape[0], -1, mine.shape[2])
+def sum_pair(mine_first, dps):
+    if dps == 2:
+        return SumPair(mine_first.reshape(-1, mine_first.shape[2])), lambda values: values[0]
+    total = lax.psum(mine_first, "dp")
+    half = lax.dynamic_index_in_dim(total, lax.rem(lax.axis_index("dp"), 2), 0, False)
+    return Body(lambda: None, [], []), lambda values: half
+
+
+class Weight:
+    def __init__(self, block, axis):
+        self.block, self.axis = block, axis
+        self.parity = lax.rem(lax.axis_index("dp"), 2)
+
+    def cut(self, which):
+        return lax.dynamic_slice_in_dim(self.block, which * 384, 384, self.axis)
+
+    def gather(self, i, *earlier):
+        mine = after(self.cut(2 * self.parity + i), *earlier)
+        return lax.all_gather(mine, "row", tiled=True)
+
+    def other(self, i):
+        return self.cut(2 * (1 - self.parity) + i)
+
+    def swap(self, i, gathered):
+        return SwapBlocks(gathered, self.other(i))
+
+
+def reduce_row(values):
+    values = values.reshape(4, -1, values.shape[1])
+    return lax.psum_scatter(values, "row", scatter_dimension=0)
 
 
 def after(value, *others):
@@ -151,140 +142,129 @@
     return jnp.where((lane >= head * HEAD) & (lane < (head + 1) * HEAD), values, 0)
 
 
-def attend_kernel(qi, ki, vi, qt, kt, vt, oi, ot, li, lt, kim, vim, ktm, vtm):
-    for h in range(2):
-        kim[h] = head_mask(ki[...], h)
-        vim[h] = head_mask(vi[...], h)
-        ktm[h] = head_mask(kt[...], h)
-        vtm[h] = head_mask(vt[...], h)
-
-    def block(query):
-        total = None
-        rows = []
+def attend_body(pairs, full_i, full_t, oi, ot, li, lt, kim, vim, ktm, vtm):
+    def pair(p, carry):
+        at_q, at_k, at_v = (lanes((which * pairs + p) * 128, 128) for which in range(3))
         for h in range(2):
-            si = dot_nt(query, kim[h])
-            st = dot_nt(query, ktm[h])
-            lane = lax.broadcasted_iota(jnp.int32, st.shape, 1)
-            st = jnp.where(lane < TXT, st, -1e30)
-            peak = jnp.maximum(
-                jnp.max(si, axis=1, keepdims=True), jnp.max(st, axis=1, keepdims=True)
-            )
-            ei = jnp.exp2((si - peak) * (SCALE * LOG2))
-            et = jnp.exp2((st - peak) * (SCALE * LOG2))
-            norm = jnp.sum(ei, axis=1, keepdims=True) + jnp.sum(et, axis=1, keepdims=True)
-            part = product(ei.astype(BF), vim[h]) + product(et.astype(BF), vtm[h])
-            part = part / norm
-            total = part if total is None else total + part
-            rows.append(peak * (SCALE * LOG2) + jnp.log2(norm))
-        lane = lax.broadcasted_iota(jnp.int32, total.shape, 1)
-        stats = jnp.where(lane == 0, rows[0], jnp.where(lane == 1, rows[1], 0.0))
-        return total.astype(BF), jnp.transpose(stats)[:8]
-
-    for b in range(IMG // 256):
-        at = pl.ds(b * 256, 256)
-        oi[at, :], li[0, :, at] = block(qi[at, :])
-    ot[...], lt[0] = block(qt[...])
+            kim[h] = head_mask(full_i[:, at_k], h)
+            vim[h] = head_mask(full_i[:, at_v], h)
+            ktm[h] = head_mask(full_t[:, at_k], h)
+            vtm[h] = head_mask(full_t[:, at_v], h)
+
+        def block(query):
+            total = None
+            rows = []
+            for h in range(2):
+                si = dot_nt(query, kim[h])
+                st = dot_nt(query, ktm[h])
+                lane = lax.broadcasted_iota(jnp.int32, st.shape, 1)
+                st = jnp.where(lane < TXT, st, -1e30)
+                peak = jnp.maximum(
+                    jnp.max(si, axis=1, keepdims=True), jnp.max(st, axis=1, keepdims=True)
+                )
+                ei = jnp.exp2((si - peak) * (SCALE * LOG2))
+                et = jnp.exp2((st - peak) * (SCALE * LOG2))
+                norm = jnp.sum(ei, axis=1, keepdims=True) + jnp.sum(et, axis=1, keepdims=True)
+                part = product(ei.astype(BF), vim[h]) + product(et.astype(BF), vtm[h])
+                part = part / norm
+                total = part if total is None else total + part
+                rows.append(peak * (SCALE * LOG2) + jnp.log2(norm))
+            lane = lax.broadcasted_iota(jnp.int32, total.shape, 1)
+            stats = jnp.where(lane == 0, rows[0], jnp.where(lane == 1, rows[1], 0.0))
+            return total.astype(BF), jnp.transpose(stats)[:8]
+
+        for b in range(IMG // 256):
+            at = pl.ds(b * 256, 256)
+            oi[at, at_q], li[p, :, at] = block(full_i[at, at_q])
+        ot[:, at_q], lt[p] = block(full_t[:, at_q])
+        return carry
+
+    lax.fori_loop(0, pairs, pair, 0)
 
 
 def attend(qkv_i, qkv_t):
     width = qkv_i.shape[1] // 3
     pairs = width // 128
-
-    def part(rows, which):
-        return pl.BlockSpec((rows, 128), lambda j: (0, which * pairs + j))
-
-    return pl.pallas_call(
-        attend_kernel,
-        grid=(pairs,),
-        in_specs=[part(n, w) for n in (IMG, PAD) for w in range(3)],
-        out_specs=[
-            part(IMG, 0),
-            part(PAD, 0),
-            pl.BlockSpec((1, 8, IMG), lambda j: (j, 0, 0)),
-            pl.BlockSpec((1, 8, PAD), lambda j: (j, 0, 0)),
-        ],
-        out_shape=[
+    return Body(
+        functools.partial(attend_body, pairs),
+        [qkv_i, qkv_t],
+        [
             jax.ShapeDtypeStruct((IMG, width), BF),
             jax.ShapeDtypeStruct((PAD, width), BF),
             jax.ShapeDtypeStruct((pairs, 8, IMG), F32),
             jax.ShapeDtypeStruct((pairs, 8, PAD), F32),
         ],
-        scratch_shapes=[pltpu.VMEM((2, n, 128), BF) for n in (IMG, IMG, PAD, PAD)],
-        compiler_params=pltpu.CompilerParams(vmem_limit_bytes=56 * 1024 * 1024),
-        cost_estimate=cost(19),
-        name="attend",
-    )(qkv_i, qkv_i, qkv_i, qkv_t, qkv_t, qkv_t)
-
-
-def attend_back_kernel(
-    qi, ki, vi, qt, kt, vt, oi, ot, gi, gt, li, lt, dqi, dki, dvi, dqt, dkt, dvt, aki, avi, akt, avt
+        [pltpu.VMEM((2, n, 128), BF) for n in (IMG, IMG, PAD, PAD)],
+    )
+
+
+def attend_back_body(
+    pairs, full_i, full_t, oi, ot, gi, gt, li, lt, di, dt, aki, avi, akt, avt
 ):
-    for acc in (aki, avi, akt, avt):
-        acc[...] = jnp.zeros_like(acc)
     lane8 = lax.broadcasted_iota(jnp.int32, (8, 128), 1) // HEAD
     row8 = lax.broadcasted_iota(jnp.int32, (8, 128), 0)
     pick = (lane8 == row8).astype(F32)
 
-    def block(query, out, grad, logsum):
-        products = grad.astype(F32) * out.astype(F32)
-        delta = lax.dot_general(
-            pick, products, (((1,), (1,)), ((), ())),
-            preferred_element_type=F32, precision=lax.Precision.HIGHEST,
-        )
-        total = None
-        for h in range(2):
-            qm = head_mask(query, h)
-            gm = head_mask(grad, h)
-            part = None
-            for keys, values, ak, av, text in ((ki, vi, aki, avi, False), (kt, vt, akt, avt, True)):
-                scores = dot_nt(keys[...], qm) * (SCALE * LOG2) - logsum[h : h + 1]
-                prob = jnp.exp2(scores)
-                if text:
-                    place = lax.broadcasted_iota(jnp.int32, prob.shape, 0)
-                    prob = jnp.where(place < TXT, prob, 0.0)
-                grads = (prob * (dot_nt(values[...], gm) - delta[h : h + 1])).astype(BF)
-                av[...] += product(prob.astype(BF), gm)
-                ak[...] += product(grads, qm)
-                term = dot_tn(grads, keys[...])
-                part = term if part is None else part + term
-            part = head_mask(part, h)
-            total = part if total is None else total + part
-        return (total * SCALE).astype(BF)
-
-    for b in range(IMG // 256):
-        at = pl.ds(b * 256, 256)
-        dqi[at, :] = block(qi[at, :], oi[at, :], gi[at, :], li[0, :, at])
-    dqt[...] = block(qt[...], ot[...], gt[...], lt[0])
-    dki[...] = (aki[...] * SCALE).astype(BF)
-    dvi[...] = avi[...].astype(BF)
-    dkt[...] = (akt[...] * SCALE).astype(BF)
-    dvt[...] = avt[...].astype(BF)
+    def pair(p, carry):
+        at_q, at_k, at_v = (lanes((which * pairs + p) * 128, 128) for which in range(3))
+        for acc in (aki, avi, akt, avt):
+            acc[...] = jnp.zeros_like(acc)
+
+        def block(query, out, grad, logsum):
+            products = grad.astype(F32) * out.astype(F32)
+            delta = lax.dot_general(
+                pick, products, (((1,), (1,)), ((), ())),
+                preferred_element_type=F32, precision=lax.Precision.HIGHEST,
+            )
+            total = None
+            for h in range(2):
+                qm = head_mask(query, h)
+                gm = head_mask(grad, h)
+                part = None
+                for full, ak, av, text in ((full_i, aki, avi, False), (full_t, akt, avt, True)):
+                    keys, values = full[:, at_k], full[:, at_v]
+                    scores = dot_nt(keys, qm) * (SCALE * LOG2) - logsum[h : h + 1]
+                    prob = jnp.exp2(scores)
+                    if text:
+                        place = lax.broadcasted_iota(jnp.int32, prob.shape, 0)
+                        prob = jnp.where(place < TXT, prob, 0.0)
+                    grads = (prob * (dot_nt(values, gm) - delta[h : h + 1])).astype(BF)
+                    av[...] += product(prob.astype(BF), gm)
+                    ak[...] += product(grads, qm)
+                    term = dot_tn(grads, keys)
+                    part = term if part is None else part + term
+                part = head_mask(part, h)
+                total = part if total is None else total + part
+            return (total * SCALE).astype(BF)
+
+        for b in range(IMG // 256):
+            at = pl.ds(b * 256, 256)
+            di[at, at_q] = block(full_i[at, at_q], oi[at, at_q], gi[at, at_q], li[p, :, at])
+        dt[:, at_q] = block(full_t[:, at_q], ot[:, at_q], gt[:, at_q], lt[p])
+        di[:, at_k] = (aki[...] * SCALE).astype(BF)
+        di[:, at_v] = avi[...].astype(BF)
+        dt[:, at_k] = (akt[...] * SCALE).astype(BF)
+        dt[:, at_v] = avt[...].astype(BF)
+        return carry
+
+    lax.fori_loop(0, pairs, pair, 0)
 
 
 def attend_back(qkv_i, qkv_t, out_i, out_t, grad_i, grad_t, log_i, log_t):
-    width = qkv_i.shape[1] // 3
-    pairs = width // 128
-
-    def part(rows, which):
-        return pl.BlockSpec((rows, 128), lambda j: (0, which * pairs + j))
-
-    results = pl.pallas_call(
-        attend_back_kernel,
-        grid=(pairs,),
-        in_specs=[part(n, w) for n in (IMG, PAD) for w in range(3)]
-        + [part(n, 0) for n in (IMG, PAD, IMG, PAD)]
-        + [pl.BlockSpec((1, 8, n), lambda j: (j, 0, 0)) for n in (IMG, PAD)],
-        out_specs=[part(n, 0) for n in (IMG, PAD) for w in range(3)],
-        out_shape=[jax.ShapeDtypeStruct((n, width), BF) for n in (IMG, PAD) for w in range(3)],
-        scratch_shapes=[pltpu.VMEM((n, 128), F32) for n in (IMG, IMG, PAD, PAD)],
-        compiler_params=pltpu.CompilerParams(vmem_limit_bytes=56 * 1024 * 1024),
-        cost_estimate=cost(32),
-        name="attend_back",
-    )(qkv_i, qkv_i, qkv_i, qkv_t, qkv_t, qkv_t, out_i, out_t, grad_i, grad_t, log_i, log_t)
-    return jnp.concatenate(results[:3], axis=1), jnp.concatenate(results[3:], axis=1)
+    pairs = qkv_i.shape[1] // 384
+    return Body(
+        functools.partial(attend_back_body, pairs),
+        [qkv_i, qkv_t, out_i, out_t, grad_i, grad_t, log_i, log_t],
+        [jax.ShapeDtypeStruct(v.shape, BF) for v in (qkv_i, qkv_t)],
+        [pltpu.VMEM((n, 128), F32) for n in (IMG, IMG, PAD, PAD)],
+    )
 
 
 MESH = pl.DeviceIdType.MESH
+
+
+def lanes(start, size):
+    return pl.ds(pl.multiple_of(start, 128), size)
 
 
 def cost(micros):
@@ -333,12 +313,18 @@
             self.move(refs, me, 0, i).wait_recv()
             self.move(refs, me, 2, i).start()
 
-    def finish(self, refs, me):
+    def wait_core(self, refs, me):
+        for i in range(self.pieces):
+            self.move(refs, me, 1, i).wait_recv()
+
+    def finish(self, refs, me, core=True):
+        if core:
+            self.wait_core(refs, me)
         for which in range(3):
             for i in range(self.pieces):
                 move = self.move(refs, me, which, i)
                 move.wait_send()
-                if which:
+                if which == 2:
                     move.wait_recv()
 
 
@@ -442,6 +428,103 @@
     axis = 0
 
 
+class AllToAllRow(AllGatherRow):
+    def __init__(self, value):
+        self.ins = [value]
+        self.n, self.size = value.shape[0] // 4, 4
+        self.outs = [jax.ShapeDtypeStruct(value.shape, value.dtype)]
+        self.scratch = [pltpu.SemaphoreType.DMA((3,)) for _ in range(2)]
+
+    def move(self, refs, me, k):
+        (value,), (out,), (send, recv) = refs
+        target = self.peers(me)[k]
+        return pltpu.make_async_remote_copy(
+            value.at[span(target[1] * self.n, self.n)],
+            out.at[span(me[1] * self.n, self.n)],
+            send.at[k], recv.at[k],
+            device_id=target, device_id_type=MESH,
+        )
+
+    def start(self, refs, me):
+        for k in range(3):
+            self.move(refs, me, k).start()
+        (value,), (out,), _ = refs
+        at = span(me[1] * self.n, self.n)
+        out[at] = value[at]
+
+
+class SwapBlocks:
+    def __init__(self, value, own):
+        self.ins = [value, own]
+        self.n = own.shape[0]
+        self.outs = [jax.ShapeDtypeStruct((2 * value.shape[0], value.shape[1]), value.dtype)]
+        self.scratch = [pltpu.SemaphoreType.DMA((3,)) for _ in range(2)]
+
+    def peers(self, me):
+        return [(me[0] ^ 1, me[1], me[2])]
+
+    greets = awaits = peers
+
+    def move(self, refs, me, k):
+        (value, own), (out,), (send, recv) = refs
+        block = lax.rem(me[1] + k + 1, 4)
+        place = (lax.rem(me[0], 2) * 4 + block) * self.n
+        return pltpu.make_async_remote_copy(
+            value.at[span(block * self.n, self.n)], out.at[span(place, self.n)],
+            send.at[k], recv.at[k],
+            device_id=self.peers(me)[0], device_id_type=MESH,
+        )
+
+    def start(self, refs, me):
+        for k in range(3):
+            self.move(refs, me, k).start()
+        (value, own), (out,), _ = refs
+        parity = lax.rem(me[0], 2)
+        out[span(parity * 4 * self.n, 4 * self.n)] = value[...]
+        out[span(((1 - parity) * 4 + me[1]) * self.n, self.n)] = own[...]
+
+    def middle(self, refs, me):
+        pass
+
+    def finish(self, refs, me):
+        for k in range(3):
+            self.move(refs, me, k).wait()
+
+
+class SumPair:
+    def __init__(self, value):
+        self.ins = [value]
+        n, w = value.shape[0] // 2, value.shape[1]
+        self.n = n
+        self.outs = [jax.ShapeDtypeStruct((n, w), BF)]
+        self.scratch = [pltpu.VMEM((n, w), BF)]
+        self.scratch += [pltpu.SemaphoreType.DMA((1,)) for _ in range(2)]
+
+    def peers(self, me):
+        return [(1 - me[0], me[1], me[2])]
+
+    greets = awaits = peers
+
+    def move(self, refs, me):
+        (part,), _, (held, send, recv) = refs
+        return pltpu.make_async_remote_copy(
+            part.at[span((1 - me[0]) * self.n, self.n)], held, send.at[0], recv.at[0],
+            device_id=self.peers(me)[0], device_id_type=MESH,
+        )
+
+    def start(self, refs, me):
+        self.move(refs, me).start()
+
+    def middle(self, refs, me):
+        pass
+
+    def finish(self, refs, me):
+        (part,), (out,), (held, send, recv) = refs
+        self.move(refs, me).wait()
+        mine = part[span(me[0] * self.n, self.n)].astype(F32)
+        out[...] = (mine + held[...].astype(F32)).astype(BF)
+
+
 class ReduceScatterRow:
     def __init__(self, value):
         self.ins = [value]
@@ -591,6 +674,11 @@
         (value,), (out,), _ = refs
         at = pl.ds(pl.multiple_of(me[1] * self.w, 128), self.w)
         out[span(me[2] * self.n, self.n)] = value[:, at]
+
+
+class Body:
+    def __init__(self, work, ins, outs, scratch=()):
+        self.work, self.ins, self.outs, self.scratch = work, list(ins), list(outs), list(scratch)
 
 
 def exchange_kernel(ops, *refs):
@@ -605,9 +693,10 @@
             refs = refs[count:]
         parts.append(taken)
     parts = list(zip(*parts))
+    moving = [(op, part) for op, part in zip(ops, parts) if not isinstance(op, Body)]
     barrier = pltpu.get_barrier_semaphore()
     count = 0
-    for op in ops:
+    for op, _ in moving:
         for item in op.greets(me):
             device, wanted = item if len(item) == 2 else (item, None)
             if wanted is None:
@@ -621,15 +710,18 @@
         else:
             count = count + len(op.awaits(me))
     pl.semaphore_wait(barrier, count)
-    for op, part in zip(ops, parts):
+    for op, part in moving:
         op.start(part, me)
     for op, part in zip(ops, parts):
+        if isinstance(op, Body):
+            op.work(*part[0], *part[1], *part[2])
+    for op, part in moving:
         op.middle(part, me)
-    for op, part in zip(ops, parts):
+    for op, part in moving:
         op.finish(part, me)
 
 
-def exchange(number, micros, *ops):
+def exchange(number, micros, *ops, name="exchange"):
     ins = [value for op in ops for value in op.ins]
     outs = [shape for op in ops for shape in op.outs]
     results = pl.pallas_call(
@@ -642,9 +734,636 @@
             collective_id=number, has_side_effects=True, vmem_limit_bytes=60 * 1024 * 1024
         ),
         cost_estimate=cost(micros),
-        name="exchange" + str(number),
+        name=name + str(number),
     )(*ins)
-    return results if len(results) > 1 else results[0]
+    return results
+
+
+def gelu_pair(values):
+    inner = 0.7978845608028654 * (values + 0.044715 * values * values * values)
+    bend = jnp.tanh(inner)
+    half = 0.5 * (1.0 + bend)
+    slope = half + values * (0.5 * (1.0 - bend * bend)) * (
+        0.7978845608028654 * (1.0 + 0.134145 * values * values)
+    )
+    return values * half, slope
+
+
+def block_copies(target, parts, sems, first, by_rows):
+    copies = []
+    for i, part in enumerate(parts):
+        for k in range(2):
+            for r in range(4):
+                source = part.at[pl.ds((k * 4 + r) * 384, 384)]
+                along, cross = pl.ds(r * 384, 384), pl.ds((2 * k + i) * 384, 384)
+                place = target.at[cross, along] if by_rows else target.at[along, cross]
+                copies.append(pltpu.make_async_copy(source, place, sems.at[first]))
+                first += 1
+    return copies
+
+
+def input_kernel(x, part_a, part_b, bias, qkv, qkv_w, out_w, weight, sems):
+    copies = block_copies(weight, (part_a, part_b), sems, 0, False)
+    for copy in copies:
+        copy.start()
+    for copy in copies:
+        copy.wait()
+    width = qkv.shape[1]
+    back = [pltpu.make_async_copy(weight.at[:, pl.ds(0, width)], qkv_w, sems.at[0])]
+    for r in range(4):
+        back.append(
+            pltpu.make_async_copy(
+                weight.at[pl.ds(r * 384, 384), pl.ds(width, 384)],
+                out_w.at[:, pl.ds(r * 384, 384)],
+                sems.at[1 + r],
+            )
+        )
+    for copy in back:
+        copy.start()
+
+    def step(i, _):
+        at = lanes(i * 384, 384)
+        qkv[:, at] = (product(x[...], weight[:, at]) + bias[:, at]).astype(BF)
+        return _
+
+    lax.fori_loop(0, width // 384, step, 0)
+    for copy in back:
+        copy.wait()
+
+
+def input_product(x, parts, bias):
+    rows, depth = x.shape
+    width = 3 * 384
+    return pl.pallas_call(
+        input_kernel,
+        in_specs=[
+            pl.BlockSpec(memory_space=pltpu.VMEM),
+            *[pl.BlockSpec(memory_space=pl.ANY)] * 2,
+            pl.BlockSpec(memory_space=pltpu.VMEM),
+        ],
+        out_specs=[
+            pl.BlockSpec(memory_space=pltpu.VMEM),
+            pl.BlockSpec(memory_space=pl.ANY),
+            pl.BlockSpec(memory_space=pl.ANY),
+        ],
+        out_shape=[
+            jax.ShapeDtypeStruct((rows, width), BF),
+            jax.ShapeDtypeStruct((depth, width), BF),
+            jax.ShapeDtypeStruct((384, depth), BF),
+        ],
+        scratch_shapes=[pltpu.VMEM((depth, 1536), BF), pltpu.SemaphoreType.DMA((16,))],
+        compiler_params=pltpu.CompilerParams(vmem_limit_bytes=56 * 1024 * 1024),
+        cost_estimate=cost(8),
+        name="input_product",
+    )(x, *parts, bias)
+
+
+def feed_kernel(ops, me, refs):
+    gather_0, sums_t, gather_r, gather_t, scatter_0, scatter_t, scatter_b, *swaps = ops
+    ins, outs, scratch = refs
+    (mixed_0, resid_t, mod_t, grad_0, grad_t, bias_0, bias_t) = ins[:7]
+    (down_a, own_a, down_b, own_b, up_a, up_b, text_p) = ins[7:]
+    (mixed_g0, wide_g1, stats_out, sum_0, sum_t, branch_0) = outs[:6]
+    (gup, gdown, gtext, branch_t) = outs[6:]
+    (full_0, up, down, hidden, pre_g, part_0, stage, text_w) = scratch[:8]
+    (stats_in, mixed_t, wide_t, side_t, full_t, hidden_t, pre_gt, part_t) = scratch[8:16]
+    (w_sems, s_sems, part_b, down_all) = scratch[16:20]
+    rest = scratch[20:]
+    dp, row, col = me
+    refs_g0 = ((mixed_0,), (full_0,), rest[0:2])
+    refs_st = ((stats_in,), (stats_out,), rest[2:4])
+    refs_gr = ((mixed_t,), (wide_t,), rest[4:6])
+    refs_gt = ((side_t,), (full_t,), rest[6:8])
+    refs_s0 = ((part_0,), (mixed_g0,), rest[8:14])
+    refs_s1 = ((part_t,), (wide_g1,), rest[14:20])
+    refs_sb = ((part_b,), (branch_0,), rest[20:26])
+    refs_sd = [
+        ((down_a, own_a), (down_all.at[0],), rest[26:28]),
+        ((down_b, own_b), (down_all.at[1],), rest[28:30]),
+    ]
+
+    for i, swap in enumerate(swaps):
+        swap.start(refs_sd[i], me)
+    copies = block_copies(up, (up_a, up_b), w_sems, 0, False)
+    parity = lax.rem(dp, 2)
+    for k in range(2):
+        for r in range(4):
+            for w in range(2):
+                at = text_w.at[w, pl.ds(k * 192, 192), pl.ds(r * 384, 384)]
+                source = text_p.at[pl.ds((k * 4 + r) * 384 + w * 192, 192)]
+                copies.append(pltpu.make_async_copy(source, at, w_sems.at[16 + 8 * k + 2 * r + w]))
+    for copy in copies:
+        copy.start()
+    gather_0.start(refs_g0, me)
+
+    resid = resid_t[...]
+    lane = lax.broadcasted_iota(jnp.int32, (PAD, 128), 1)
+    pair = jnp.where(
+        lane == 0,
+        jnp.sum(resid, axis=1, keepdims=True),
+        jnp.where(lane == 1, jnp.sum(resid * resid, axis=1, keepdims=True), 0.0),
+    )
+    stats_in[...] = jnp.transpose(pair)[:8]
+    sums_t.start(refs_st, me)
+    sums_t.finish(refs_st, me)
+    total = stats_out[0:8] + stats_out[8:16] + stats_out[16:24] + stats_out[24:32]
+    total = jnp.transpose(jnp.concatenate([total, jnp.zeros((120, PAD), F32)], axis=0)) / D
+    mean, square = total[:, 0:1], total[:, 1:2]
+    normed = (resid - mean) * lax.rsqrt(square - mean * mean + EPSILON)
+    mixed_t[...] = (normed * mod_t[1:2] + mod_t[0:1]).astype(BF)
+    gather_r.start(refs_gr, me)
+    for copy in copies:
+        copy.wait()
+    for i, swap in enumerate(swaps):
+        swap.finish(refs_sd[i], me)
+        for k in range(2):
+            for r in range(4):
+                place = down.at[pl.ds((2 * k + i) * 384, 384), pl.ds(r * 384, 384)]
+                place[...] = down_all[i, pl.ds((k * 4 + r) * 384, 384), :]
+    sum_0[...] = jnp.zeros_like(sum_0)
+    sum_t[...] = jnp.zeros_like(sum_t)
+
+    def quarter(i, carry):
+        @pl.when(i == 2)
+        def _():
+            gather_r.finish(refs_gr, me)
+            for r in range(4):
+                side_t[:, pl.ds(r * 384, 384)] = wide_t[pl.ds(r * PAD, PAD), :]
+            gather_0.middle(refs_g0, me)
+            gather_0.finish(refs_g0, me, False)
+            gather_t.start(refs_gt, me)
+
+        @pl.when(i == 1)
+        def _():
+            gather_0.wait_core(refs_g0, me)
+
+        at = span((col ^ (i ^ (i // 2))) * 256, 256)
+
+        def tile(j, carry):
+            cut = lanes(j * 512, 512)
+            pre = product(full_0[at, :], up[:, cut]) + bias_0[:, cut]
+            value, slope = gelu_pair(pre)
+            hidden[at, cut] = value.astype(BF)
+            back = product_right(grad_0[at, :], down[cut, :])
+            grad = (back * slope).astype(BF)
+            pre_g[at, cut] = grad
+            sum_0[:, cut] += jnp.sum(grad.astype(F32), axis=0, keepdims=True)
+            return carry
+
+        lax.fori_loop(0, 3, tile, 0)
+
+        def tile_back(j, carry):
+            cut = lanes(j * 512, 512)
+            part_0[at, cut] = product_right(pre_g[at, :], up[cut, :]).astype(BF)
+            return carry
+
+        lax.fori_loop(0, 3, tile_back, 0)
+        return carry
+
+    lax.fori_loop(0, 4, quarter, 0)
+    scatter_0.start(refs_s0, me)
+    scatter_0.middle(refs_s0, me)
+    gather_t.middle(refs_gt, me)
+    gather_t.finish(refs_gt, me)
+
+    def text_quarter(i, carry):
+        at = span(i * PAD, PAD)
+        pre = product_right(full_t[at, :], text_w[0]) + bias_t[...]
+        value, slope = gelu_pair(pre)
+        hidden_t[at, :] = value.astype(BF)
+        grad = (product_right(grad_t[at, :], text_w[1]) * slope).astype(BF)
+        pre_gt[at, :] = grad
+        sum_t[...] += jnp.sum(grad.astype(F32), axis=0, keepdims=True)
+        part_t[at, :] = product(grad, text_w[0]).astype(BF)
+        return carry
+
+    lax.fori_loop(0, 4, text_quarter, 0)
+    scatter_t.start(refs_s1, me)
+    scatter_t.middle(refs_s1, me)
+
+    def branch_quarter(i, carry):
+        at = span(i * 256, 256)
+        for j in range(3):
+            cut = pl.ds(j * 512, 512)
+            part_b[at, cut] = product(hidden[at, :], down[:, cut]).astype(BF)
+        return carry
+
+    lax.fori_loop(0, 4, branch_quarter, 0)
+    scatter_b.start(refs_sb, me)
+    scatter_b.middle(refs_sb, me)
+
+    def put(slot, moves):
+        for k, (source, target) in enumerate(moves):
+            pltpu.make_async_copy(source, target, s_sems.at[slot, k]).start()
+
+    def done(slot, moves):
+        for k, (source, target) in enumerate(moves):
+            pltpu.make_async_copy(source, target, s_sems.at[slot, k]).wait()
+
+    def staged(count, value_of, moves_of):
+        def step(i, carry):
+            slot = lax.rem(i, 2)
+
+            @pl.when(i >= 2)
+            def _():
+                done(slot, moves_of(i - 2, stage.at[slot]))
+
+            value_of(i, stage.at[slot])
+            put(slot, moves_of(i, stage.at[slot]))
+            return carry
+
+        lax.fori_loop(0, count, step, 0)
+        for i in (count - 2, count - 1):
+            done(i % 2, moves_of(i, stage.at[i % 2]))
+
+    def value_of(i, place):
+        cut = lanes(i * 384, 384)
+        for j in range(3):
+            at = pl.ds(j * 512, 512)
+            place[:, at] = product_left(hidden[:, cut], grad_0[:, at]).astype(BF)
+
+    def moves_of(i, place):
+        return [
+            (
+                place.at[:, pl.ds(r * 384, 384)],
+                gdown.at[lax.rem(i, 2), i // 2, r],
+            )
+            for r in range(4)
+        ]
+
+    staged(4, value_of, moves_of)
+
+    def value_of(i, place):
+        for j in range(3):
+            at = pl.ds(j * 512, 512)
+            left = full_0[:, lanes(i * 384, 384)]
+            place[:, at] = product_left(left, pre_g[:, at]).astype(BF)
+
+    def moves_of(i, place):
+        return [
+            (place.at[:, pl.ds((2 * k + q) * 384, 384)], gup.at[q, k, i])
+            for k in range(2)
+            for q in range(2)
+        ]
+
+    staged(4, value_of, moves_of)
+
+    def value_of(i, place):
+        @pl.when(i == 0)
+        def _():
+            for j in range(3):
+                at = pl.ds(j * 512, 512)
+                place[:, at] = product_left(pre_gt[...], full_t[:, at]).astype(BF)
+
+        @pl.when(i == 1)
+        def _():
+            for j in range(3):
+                at = pl.ds(j * 512, 512)
+                place[:, at] = product_left(hidden_t[...], grad_t[:, at]).astype(BF)
+
+    def moves_of(i, place):
+        return [
+            (place.at[pl.ds(k * 192, 192)], gtext.at[i, k]) for k in range(2)
+        ]
+
+    staged(2, value_of, moves_of)
+
+    def value_of(i, place):
+        at = span(i * PAD, PAD)
+        place[pl.ds(0, PAD)] = product(hidden_t[at, :], text_w[1]).astype(BF)
+
+    def moves_of(i, place):
+        return [(place.at[pl.ds(0, PAD)], branch_t.at[span(i * PAD, PAD)])]
+
+    staged(4, value_of, moves_of)
+    scatter_0.finish(refs_s0, me)
+    scatter_t.finish(refs_s1, me)
+    scatter_b.finish(refs_sb, me)
+
+
+def feed(number, mixed_0, resid_t, mod_t, grad_0, grad_t, bias_0, bias_t, *weights):
+    def shape(*dims, dtype=BF):
+        return jax.ShapeDtypeStruct(dims, dtype)
+
+    ops = (
+        AllGatherCol(mixed_0, 4),
+        AllGatherRow(shape(8, PAD, dtype=F32)),
+        AllGatherRow(shape(PAD, 384)),
+        AllGatherCol(shape(PAD, 1536), 2),
+        ReduceScatterCol(shape(1024, 1536), 4),
+        ReduceScatterCol(shape(640, 1536), 2),
+        ReduceScatterCol(shape(1024, 1536), 4),
+        SwapBlocks(weights[0], weights[1]),
+        SwapBlocks(weights[2], weights[3]),
+    )
+
+    def kernel(*refs):
+        me = tuple(lax.axis_index(name) for name in ("dp", "row", "col"))
+        barrier = pltpu.get_barrier_semaphore()
+        peers = ops[0].peers(me) + ops[1].peers(me) + ops[-1].peers(me)
+        for device in peers:
+            pl.semaphore_signal(barrier, 1, device_id=device, device_id_type=MESH)
+        pl.semaphore_wait(barrier, len(peers))
+        feed_kernel(ops, me, (refs[:14], refs[14:24], refs[24:]))
+
+    outs = [
+        shape(256, 1536, dtype=F32),
+        shape(PAD, 1536, dtype=F32),
+        shape(32, PAD, dtype=F32),
+        shape(1, 1536, dtype=F32),
+        shape(1, 384, dtype=F32),
+        shape(256, 1536, dtype=F32),
+        shape(2, 2, 4, 384, 384),
+        shape(2, 2, 4, 384, 384),
+        shape(2, 2, 192, 1536),
+        shape(640, 1536),
+    ]
+    vmem, hbm = pl.BlockSpec(memory_space=pltpu.VMEM), pl.BlockSpec(memory_space=pl.ANY)
+    return pl.pallas_call(
+        kernel,
+        in_specs=[vmem] * 11 + [hbm] * 3,
+        out_specs=[vmem] * 6 + [hbm] * 4,
+        out_shape=outs,
+        scratch_shapes=[
+            pltpu.VMEM((1024, 1536), BF),
+            pltpu.VMEM((1536, 1536), BF),
+            pltpu.VMEM((1536, 1536), BF),
+            pltpu.VMEM((1024, 1536), BF),
+            pltpu.VMEM((1024, 1536), BF),
+            pltpu.VMEM((1024, 1536), BF),
+            pltpu.VMEM((2, 384, 1536), BF),
+            pltpu.VMEM((2, 384, 1536), BF),
+            pltpu.VMEM((8, PAD), F32),
+            pltpu.VMEM((PAD, 384), BF),
+            pltpu.VMEM((640, 384), BF),
+            pltpu.VMEM((PAD, 1536), BF),
+            pltpu.VMEM((640, 1536), BF),
+            pltpu.VMEM((640, 384), BF),
+            pltpu.VMEM((640, 384), BF),
+            pltpu.VMEM((640, 1536), BF),
+            pltpu.SemaphoreType.DMA((40,)),
+            pltpu.SemaphoreType.DMA((2, 4)),
+            pltpu.VMEM((1024, 1536), BF),
+            pltpu.VMEM((2, 3072, 384), BF),
+        ]
+        + [item for op in ops for item in op.scratch],
+        compiler_params=pltpu.CompilerParams(
+            collective_id=number, has_side_effects=True, vmem_limit_bytes=62 * 1024 * 1024
+        ),
+        cost_estimate=cost(90),
+        name="feed",
+    )(mixed_0, resid_t, mod_t, grad_0, grad_t, bias_0, bias_t, *weights)
+
+
+class SumPairFar(SumPair):
+    def __init__(self, value):
+        super().__init__(value)
+        self.scratch.append(pltpu.SemaphoreType.DMA((1,)))
+
+    def move(self, refs, me):
+        return SumPair.move(self, (refs[0], refs[1], refs[2][:3]), me)
+
+    def finish(self, refs, me):
+        (part,), (out,), (held, send, recv, local) = refs
+        mine = pltpu.make_async_copy(part.at[span(me[0] * self.n, self.n)], out, local.at[0])
+        mine.start()
+        mine.wait()
+        self.move(refs, me).wait()
+        out[...] = (out[...].astype(F32) + held[...].astype(F32)).astype(BF)
+
+
+def columns(rows):
+    return jnp.transpose(jnp.concatenate([rows, jnp.zeros((120, PAD), F32)], axis=0))
+
+
+def row_total(gathered):
+    return gathered[0:8] + gathered[8:16] + gathered[16:24] + gathered[24:32]
+
+
+def back_kernel(plan, me, refs):
+    ins, outs, scratch = refs
+    named, sums, pairs = plan
+    (gmixed_0, cot_0, resid_0, mod_0, stacked_t, cot_t, resid_t, stats_2, mod_t) = ins[:9]
+    (out_0, out_1, image_seq, qkv_i, qkv_t, attn_i, attn_t, log_i, log_t) = ins[9:18]
+    text_in, far = ins[18], ins[19:]
+    (gresid_0, proj_0, gmixed_t, gresid_t, proj_t, image_out, dqkv_i, dqkv_t, text_out) = outs[:9]
+    far_out = outs[9:]
+    (own_0, own_t, stats_in, stats_all, part_t, gattn_t32, gattn_i, gattn_t) = scratch[:8]
+    (text_sum, text_stack, aki, avi, akt, avt) = scratch[8:14]
+    rest = list(scratch[14:])
+
+    def take(op):
+        count = len(op.scratch)
+        found = rest[:count]
+        del rest[:count]
+        return found
+
+    io = {
+        "reduce_t": ((stacked_t,), (gmixed_t,)),
+        "gather_0": ((own_0,), (proj_0,)),
+        "stats": ((stats_in,), (stats_all,)),
+        "gather_t": ((own_t,), (proj_t,)),
+        "reduce_a": ((part_t,), (gattn_t32,)),
+        "image": ((image_seq,), (image_out,)),
+        "text": ((text_stack,), (text_out,)),
+    }
+    refs_of = {key: (*io[key], take(op)) for key, op in named.items()}
+    sum_refs = [((text_in,), (text_sum,), take(op)) for op in sums]
+    far_refs = [((far[i],), (far_out[i],), take(op)) for i, op in enumerate(pairs)]
+
+    def do(key, step):
+        getattr(named[key], step)(refs_of[key], me)
+
+    do("reduce_t", "start")
+    for op, part in zip(sums, sum_refs):
+        op.start(part, me)
+
+    def norm_rows(i, carry):
+        at = pl.ds(pl.multiple_of(i * 64, 64), 64)
+        resid = resid_0[at, :]
+        mean = jnp.mean(resid, axis=1, keepdims=True)
+        square = jnp.mean(resid * resid, axis=1, keepdims=True)
+        inverse = lax.rsqrt(square - mean * mean + EPSILON)
+        normed = (resid - mean) * inverse
+        grad = gmixed_0[at, :] * (1.0 + mod_0[4:5])
+        total = jnp.mean(grad, axis=1, keepdims=True)
+        cross = jnp.mean(grad * normed, axis=1, keepdims=True)
+        result = cot_0[at, :].astype(F32) + inverse * (grad - total - normed * cross)
+        gresid_0[at, :] = result
+        own_0[at, :] = (result * mod_0[2:3]).astype(BF)
+        return carry
+
+    lax.fori_loop(0, 4, norm_rows, 0)
+    do("gather_0", "start")
+    do("reduce_t", "finish")
+
+    before = columns(row_total(stats_2)) / D
+    mean, square = before[:, 0:1], before[:, 1:2]
+    inverse = lax.rsqrt(square - mean * mean + EPSILON)
+    normed = (resid_t[...] - mean) * inverse
+    grad = gmixed_t[...] * (1.0 + mod_t[4:5])
+    lane = lax.broadcasted_iota(jnp.int32, (PAD, 128), 1)
+    pair = jnp.where(
+        lane == 0,
+        jnp.sum(grad, axis=1, keepdims=True),
+        jnp.where(lane == 1, jnp.sum(grad * normed, axis=1, keepdims=True), 0.0),
+    )
+    stats_in[...] = jnp.transpose(pair)[:8]
+    do("stats", "start")
+    do("stats", "finish")
+    after_sums = columns(row_total(stats_all)) / D
+    total, cross = after_sums[:, 0:1], after_sums[:, 1:2]
+    result = cot_t[...] + inverse * (grad - total - normed * cross)
+    gresid_t[...] = result
+    own_t[...] = (result * mod_t[2:3]).astype(BF)
+    do("gather_t", "start")
+    do("image", "start")
+    do("gather_t", "middle")
+    do("gather_t", "finish")
+    for i in range(4):
+        at = pl.ds(i * PAD, PAD)
+        part_t[at, :] = product_right(proj_t[at, :], out_1[...]).astype(BF)
+    do("reduce_a", "start")
+    do("gather_0", "middle")
+    for op, part in zip(sums, sum_refs):
+        op.finish(part, me)
+    for op, part in zip(pairs, far_refs):
+        op.start(part, me)
+    text = text_sum if sums else text_in
+    for r in range(4):
+        text_stack[pl.ds(r * 384, 384), :] = text[:, pl.ds(r * 384, 384)]
+    do("text", "start")
+    do("gather_0", "finish")
+
+    def rows_back(i, carry):
+        at = span(i * 256, 256)
+        gattn_i[at, :] = product_right(proj_0[at, :], out_0[...]).astype(BF)
+        return carry
+
+    lax.fori_loop(0, 4, rows_back, 0)
+    do("reduce_a", "finish")
+    gattn_t[...] = gattn_t32[...].astype(BF)
+    attend_back_body(
+        qkv_i.shape[1] // 384,
+        qkv_i, qkv_t, attn_i, attn_t, gattn_i, gattn_t, log_i, log_t,
+        dqkv_i, dqkv_t, aki, avi, akt, avt,
+    )
+    do("text", "finish")
+    do("image", "finish")
+    for op, part in zip(pairs, far_refs):
+        op.finish(part, me)
+
+
+def back(number, dps, values, text, fars):
+    def shape(*dims, dtype=BF):
+        return jax.ShapeDtypeStruct(dims, dtype)
+
+    named = {
+        "reduce_t": ReduceScatterRow(shape(640, 384)),
+        "gather_0": AllGatherCol(shape(256, 1536), 4),
+        "stats": AllGatherRow(shape(8, PAD, dtype=F32)),
+        "gather_t": AllGatherCol(shape(PAD, 384)),
+        "reduce_a": ReduceScatterRow(shape(640, 384)),
+        "image": FromSequence(shape(256, 1536)),
+        "text": AllToAllRow(shape(1536, 384)),
+    }
+    sums = [SumPair(text)] if dps == 2 else []
+    pairs = [SumPairFar(far) for far in fars]
+    ops = list(named.values()) + sums + pairs
+    count = 19 + len(fars)
+    out_shapes = [
+        shape(256, 1536, dtype=F32),
+        shape(1024, 1536),
+        shape(PAD, 384, dtype=F32),
+        shape(PAD, 384, dtype=F32),
+        shape(640, 384),
+        shape(1024, 384),
+        shape(1024, 1152),
+        shape(PAD, 1152),
+        shape(1536, 384),
+    ] + [op.outs[0] for op in pairs]
+
+    def kernel(*refs):
+        me = tuple(lax.axis_index(name) for name in ("dp", "row", "col"))
+        barrier = pltpu.get_barrier_semaphore()
+        peers = named["gather_0"].peers(me) + named["stats"].peers(me)
+        if dps == 2:
+            peers = peers + sums[0].peers(me)
+        for device in peers:
+            pl.semaphore_signal(barrier, 1, device_id=device, device_id_type=MESH)
+        image = named["image"]
+        for device, wanted in image.greets(me):
+            @pl.when(wanted)
+            def _():
+                pl.semaphore_signal(barrier, 1, device_id=device, device_id_type=MESH)
+        pl.semaphore_wait(barrier, len(peers) + 4 - (me[1] == me[2]).astype(jnp.int32))
+        outs = count + len(out_shapes)
+        back_kernel((named, sums, pairs), me, (refs[:count], refs[count:outs], refs[outs:]))
+
+    vmem, hbm = pl.BlockSpec(memory_space=pltpu.VMEM), pl.BlockSpec(memory_space=pl.ANY)
+    return pl.pallas_call(
+        kernel,
+        in_specs=[vmem] * 19 + [hbm] * len(fars),
+        out_specs=[vmem] * len(out_shapes),
+        out_shape=out_shapes,
+        scratch_shapes=[
+            pltpu.VMEM((256, 1536), BF),
+            pltpu.VMEM((PAD, 384), BF),
+            pltpu.VMEM((8, PAD), F32),
+            pltpu.VMEM((32, PAD), F32),
+            pltpu.VMEM((640, 384), BF),
+            pltpu.VMEM((PAD, 384), F32),
+            pltpu.VMEM((1024, 384), BF),
+            pltpu.VMEM((PAD, 384), BF),
+            pltpu.VMEM((384, 1536), BF),
+            pltpu.VMEM((1536, 384), BF),
+        ]
+        + [pltpu.VMEM((n, 128), F32) for n in (IMG, IMG, PAD, PAD)]
+        + [item for op in ops for item in op.scratch],
+        compiler_params=pltpu.CompilerParams(
+            collective_id=number, has_side_effects=True, vmem_limit_bytes=62 * 1024 * 1024
+        ),
+        cost_estimate=cost(130),
+        name="back",
+    )(*values, text, *fars)
+
+
+def finish_feed_kernel(up_parts, down_parts, text, up, down):
+    for k in range(4):
+        at = slice(k * 384, (k + 1) * 384)
+        up[0, :, at] = up_parts[at].astype(F32)
+        down[0, at] = down_parts[at].astype(F32)
+    for r in range(4):
+        starts = [k * 1536 + r * 384 for k in range(2)]
+        both = [text[start : start + 192].astype(F32) for start in starts]
+        up[1, :, r * 384 : (r + 1) * 384] = jnp.transpose(jnp.concatenate(both, axis=0))
+        for k in range(2):
+            place = r * 384 + k * 192
+            down[1, place : place + 192] = text[starts[k] + 192 : starts[k] + 384].astype(F32)
+
+
+def finish_rest_kernel(dps, parts, qkv_parts, out_parts, qkv, out):
+    for k in range(3):
+        at = slice(k * 384, (k + 1) * 384)
+        qkv[0, :, at] = parts[at].astype(F32)
+    out[0] = parts[1152:1536].astype(F32)
+    for target, terms in ((qkv, qkv_parts), (out, out_parts)):
+        total = terms[0:384].astype(F32)
+        for d in range(1, dps):
+            total = total + terms[d * 384 : (d + 1) * 384].astype(F32)
+        target[1] = total
+
+
+def finish(kernel, name, shapes, *values):
+    return pl.pallas_call(
+        kernel,
+        in_specs=[pl.BlockSpec(memory_space=pltpu.VMEM)] * len(values),
+        out_specs=[pl.BlockSpec(memory_space=pltpu.VMEM)] * len(shapes),
+        out_shape=[jax.ShapeDtypeStruct(shape, F32) for shape in shapes],
+        compiler_params=pltpu.CompilerParams(vmem_limit_bytes=56 * 1024 * 1024),
+        cost_estimate=cost(6),
+        name=name,
+    )(*values)
 
 
 def pad_text(values):
@@ -678,12 +1397,9 @@
     wc = condition.shape[1]
     wf = up_w.shape[2]
 
+    first_w = Weight(jnp.concatenate([qkv_w[0].reshape(wr, 3 * wc), out_w[0]], axis=1), 1)
+    first_a = first_w.gather(0)
     parity = lax.rem(lax.axis_index("dp"), 2)
-    first_0 = gather_block(
-        jnp.concatenate([qkv_w[0].reshape(wr, 3 * wc), out_w[0]], axis=1), dps, parity
-    )
-    qkv_0 = first_0[:, :, : 3 * wc].reshape(rows * wr, 3 * wc)
-    out_0 = first_0[:, :, 3 * wc :].transpose(1, 0, 2).reshape(wc, rows * wr)
     qkv_1 = qkv_w[1].reshape(wr, 3 * wc)
     share = wf // rows
     up_bias_1 = lax.dynamic_slice_in_dim(up_b[1], row * share, share).astype(F32)
@@ -693,7 +1409,7 @@
     modul_parts = jnp.concatenate(
         [product(silu_low, ada_w[s].reshape(wc, 6 * wr)) for s in range(2)]
     )
-    modul_all = exchange(1, 7, AllGatherCol(modul_parts)).reshape(cols, 2, seqs, 6, wr)
+    modul_all = exchange(1, 7, AllGatherCol(modul_parts))[0].reshape(cols, 2, seqs, 6, wr)
     mods = jnp.sum(modul_all, axis=0) + ada_b.astype(F32)[:, None]
     bias_rows = jnp.broadcast_to(
         jnp.stack([out_b[0], down_b[0]]).astype(F32)[None], (seqs, 2, wr)
@@ -712,7 +1428,7 @@
         mods_row.reshape(rows, seqs, 8, wr), row, 1, keepdims=False
     ).transpose(1, 0, 2).reshape(8, rows * wr)
     mod_1 = lax.dynamic_index_in_dim(mods[1], col, 0, keepdims=False)
-    up_0 = gather_block(up_w[0], dps, parity).reshape(rows * wr, wf)
+    first_b = first_w.gather(1, x0)
 
     x0 = x0.astype(F32)
     norm1_0, inv1_0 = norm_local(x0)
@@ -720,36 +1436,56 @@
     norm1_1, inv1_1 = norm_row(x1, stats)
     mixed1_1 = (norm1_1 * (1.0 + mod_1[1]) + mod_1[0]).astype(BF)
     full1_1, full1_0, cot0 = exchange(
-        3, 27, AllGatherCol(mixed1_1), AllGatherCol(mixed1_0, 4), ToSequence(image_cot)
-    )
-    down_0 = gather_block(down_w[0], dps, parity)
-    down_0 = down_0.transpose(1, 0, 2).reshape(wf, rows * wr)
+        3,
+        27,
+        AllGatherCol(mixed1_1),
+        AllGatherCol(mixed1_0, 4),
+        ToSequence(image_cot),
+    )
     cot0 = cot0.astype(F32)
     qkv_bias = jnp.stack(
         [qkv_b[:, 0], jnp.zeros_like(qkv_b[:, 0]), qkv_b[:, 1]], axis=1
     ).astype(F32).reshape(2, 3 * wc)
-    qkv_t, wide_g1, branch_g0 = exchange(
+    first_a, first_b, qkv_t, wide_g1, branch_g0 = exchange(
         4,
         45,
+        first_w.swap(0, first_a),
+        first_w.swap(1, first_b),
         ReduceScatterRow(product(full1_1, qkv_1).astype(BF)),
         AllGatherRow((mod_1[5] * cot1).astype(BF)),
         AllGatherCol((mod_0[5] * cot0).astype(BF), 4),
     )
+    up_0, down_0 = Weight(up_w[0], 1), Weight(down_w[0], 0)
+    up_a, up_b0 = up_0.gather(0, qkv_t), up_0.gather(1, qkv_t)
+    down_a, down_b0 = down_0.gather(0, qkv_t), down_0.gather(1, qkv_t)
+    qkv_txt = (qkv_t + qkv_bias[1]).astype(BF)
+    qkv_img, qkv_0, out_0 = input_product(full1_0, [first_a, first_b], qkv_bias[:1])
     text_w = jnp.stack([up_w[1].T.reshape(rows, 2, -1, wr), down_w[1].reshape(rows, 2, -1, wr)])
-    text_w = lax.dynamic_index_in_dim(after(text_w, qkv_t), parity, 2, keepdims=False)
-    text_w = lax.all_to_all(text_w, "row", 1, 1)
-    text_w = in_order(text_w, partner(text_w, dps), parity, 2).reshape(2, rows, -1, wr)
-    up_1, down_1 = text_w.transpose(0, 2, 1, 3).reshape(2, -1, rows * wr)
-    qkv_txt = (qkv_t + qkv_bias[1]).astype(BF)
-    qkv_img = (product(full1_0, qkv_0) + qkv_bias[0]).astype(BF)
-    attn_0, attn_text, log_0, log_1 = attend(qkv_img, qkv_txt)
-    attn_1, branch_g1 = exchange(
-        6, 14, AllGatherRow(attn_text), AllGatherCol(side(wide_g1, rows), 2)
-    )
-
-    proj_1, proj_0 = exchange(
+    text_w, text_own = (
+        lax.dynamic_index_in_dim(text_w, half, 2, keepdims=False).transpose(1, 0, 2, 3)
+        for half in (parity, 1 - parity)
+    )
+    text_own = lax.dynamic_index_in_dim(text_own, row, 0, False).reshape(-1, wr)
+    attn_0, attn_text, log_0, log_1, text_w = exchange(
+        5,
+        26,
+        attend(qkv_img, qkv_txt),
+        AllToAllRow(text_w.reshape(-1, wr)),
+        name="attend",
+    )
+    up_a, attn_1, branch_g1 = exchange(
+        6,
+        20,
+        up_0.swap(0, up_a),
+        AllGatherRow(attn_text),
+        AllGatherCol(side(wide_g1, rows), 2),
+    )
+
+    up_b0, text_w, proj_1, proj_0 = exchange(
         7,
-        25,
+        32,
+        up_0.swap(1, up_b0),
+        SwapBlocks(text_w, text_own),
         ReduceScatterCol(product(attn_1, out_w[1]).astype(BF)),
         ReduceScatterCol(product(attn_0, out_0).astype(BF), 4),
     )
@@ -759,102 +1495,89 @@
     mixed2_0 = (norm2_0 * (1.0 + mod_0[4]) + mod_0[3]).astype(BF)
     proj_1 = proj_1 + out_b[1].astype(F32)
     resid_1 = x1 + mod_1[2] * proj_1
-    stats, full2_0 = exchange(
-        8, 22, AllGatherRow(row_stats(resid_1, resid_1 * resid_1)), AllGatherCol(mixed2_0, 4)
-    )
-    norm2_1, inv2_1 = norm_row(resid_1, stats)
-    mixed2_1 = (norm2_1 * (1.0 + mod_1[4]) + mod_1[3]).astype(BF)
-    wide2_1 = exchange(9, 13, AllGatherRow(mixed2_1))
-    full2_1 = exchange(10, 13, AllGatherCol(side(wide2_1, rows), 2))
-
-    def halves(values, which):
-        cut = values.reshape(values.shape[0], -1, 2, values.shape[1] // 2 // rows)
-        return lax.dynamic_index_in_dim(cut, which, 2, keepdims=False).reshape(
-            values.shape[0], -1
-        )
-
-    def half(values, which):
-        cut = values.shape[1] // 2
-        return lax.dynamic_slice_in_dim(values, which * cut, cut, 1)
-
     def by_row(left, right):
         wide = product_left(right, left).reshape(rows, wr, left.shape[1])
         return wide.transpose(0, 2, 1)
 
-    pre_0 = product(full2_0, up_0) + up_b[0].astype(F32)
-    hidden_0 = gelu_value(pre_0).astype(BF)
-    pre_g0 = gelu_slope(pre_0, product_right(branch_g0, down_0)).astype(BF)
-    pre_1 = product_right(full2_1, up_1) + up_bias_1
-    hidden_1 = gelu_value(pre_1).astype(BF)
-    pre_g1 = gelu_slope(pre_1, product_right(branch_g1, down_1)).astype(BF)
-
-    def add_partner(other, mine):
-        return (mine + partner(other, dps).astype(F32)).astype(BF)
-
-    def reduce_block(both):
-        return lax.psum_scatter(both, "row", scatter_dimension=0)
-
-    down_o = by_row(half(hidden_0, 1 - parity), branch_g0).astype(BF)
-    up_o = product_left(halves(full2_0, 1 - parity), pre_g0).reshape(rows, -1, wf).astype(BF)
-    mixed2_g0, wide2_g1 = exchange(
+    results = feed(
+        8,
+        mixed2_0,
+        resid_1,
+        jnp.pad(jnp.stack([mod_1[3], 1.0 + mod_1[4]]), ((0, 6), (0, 0))),
+        branch_g0,
+        branch_g1,
+        up_b[:1].astype(F32),
+        up_bias_1[None],
+        down_a,
+        down_0.other(0),
+        down_b0,
+        down_0.other(1),
+        up_a,
+        up_b0,
+        text_w,
+    )
+    mixed2_g0, wide2_g1, stats, pre_s0, pre_s1, branch_0 = results[:6]
+    up_p, down_p, text_p, branch_p1 = results[6:]
+    branch_0 = branch_0 + mod_0[7]
+    norm2_1, inv2_1 = norm_row(resid_1, stats)
+    fars = [part.reshape(-1, wr) for part in (down_p[0], down_p[1], up_p[0], up_p[1])]
+    text_p = text_p.transpose(1, 0, 2, 3).reshape(-1, rows * wr)
+    parity_now = lax.rem(lax.axis_index("dp"), 2)
+    if dps != 2:
+        halves = [
+            lax.dynamic_slice_in_dim(
+                lax.psum(part, "dp"), parity_now * (part.shape[0] // 2), part.shape[0] // 2
+            )
+            for part in fars + [text_p]
+        ]
+        fars, text_p = [], halves[4]
+    (
+        resid_g0,
+        proj_g0,
+        mixed2_g1,
+        resid_g1,
+        proj_g1,
+        image_out,
+        qkv_grad_0,
+        qkv_grad_t,
+        text_h,
+        *sums,
+    ) = back(
         11,
-        35,
-        ReduceScatterCol(after(product_right(pre_g0, up_0).astype(BF), down_o, up_o), 4),
-        ReduceScatterCol(product(pre_g1, up_1).astype(BF), 2),
-    )
-    down_b0 = add_partner(down_o, by_row(half(hidden_0, parity), branch_g0))
-    up_b0 = add_partner(
-        up_o, product_left(halves(full2_0, parity), pre_g0).reshape(rows, -1, wf)
-    )
-    def text_part(which):
-        parts = [
-            product_left(half(pre_g1, which), full2_1),
-            product_left(half(hidden_1, which), branch_g1),
-        ]
-        return jnp.stack(parts).astype(BF)
-
-    text_o = text_part(1 - parity)
-    text_m = text_part(parity)
-
-    resid_g0 = cot0 + norm_local_back(mixed2_g0 * (1.0 + mod_0[4]), norm2_0, inv2_0)
-    down_h0 = reduce_block(down_b0)
-    mixed2_g1, proj_g0 = exchange(
-        12,
-        22,
-        ReduceScatterRow(stack(wide2_g1.astype(BF), rows)),
-        AllGatherCol((mod_0[2] * resid_g0).astype(BF), 4),
-    )
-    up_h0 = reduce_block(up_b0)
-    norm2_g1 = mixed2_g1 * (1.0 + mod_1[4])
-    stats, wide_1 = exchange(
-        13,
-        16,
-        AllGatherRow(row_stats(norm2_g1, norm2_g1 * norm2_1)),
-        ReduceScatterCol(after(product(hidden_1, down_1).astype(BF), down_b0), 2),
-    )
-    resid_g1 = cot1 + norm_row_back(norm2_g1, norm2_1, inv2_1, stats)
-    proj_g1 = exchange(14, 7, AllGatherCol((mod_1[2] * resid_g1).astype(BF)))
-    attn_g0 = product_right(proj_g0, out_0).astype(BF)
-    attn_g1, branch_0 = exchange(
-        15,
-        22,
-        ReduceScatterRow(product_right(proj_g1, out_w[1]).astype(BF)),
-        ReduceScatterCol(product(hidden_0, down_0).astype(BF), 4),
-    )
-    attn_g1 = attn_g1.astype(BF)
-    branch_0 = branch_0 + mod_0[7]
+        dps,
+        [
+            mixed2_g0,
+            cot0.astype(BF),
+            resid_0,
+            mod_0,
+            stack(wide2_g1.astype(BF), rows),
+            cot1,
+            resid_1,
+            stats,
+            jnp.pad(mod_1, ((0, 2), (0, 0))),
+            out_0,
+            out_w[1],
+            (resid_0 + mod_0[5] * branch_0).astype(BF),
+            qkv_img,
+            qkv_txt,
+            attn_0,
+            attn_text,
+            log_0,
+            log_1,
+        ],
+        text_p,
+        fars,
+    )
+    down_ha, down_hb, up_ha, up_hb = [
+        reduce_row(part) for part in (sums if dps == 2 else halves[:4])
+    ]
     out_g1 = product_left(attn_1, proj_g1)
-    out_o = by_row(half(attn_0, 1 - parity), proj_g0).astype(BF)
-    qkv_grad_0, qkv_grad_t = attend_back(
-        qkv_img, qkv_txt, attn_0, attn_text, after(attn_g0, out_o, text_o, up_b0), attn_g1, log_0, log_1
-    )
-    out_b0 = add_partner(out_o, by_row(half(attn_0, parity), proj_g0))
-    out_h0 = reduce_block(out_b0)
-    text_b = (text_m + partner(text_o, dps).astype(F32)).astype(BF)
-    text_b = text_b.reshape(2, share // 2, rows, wr).transpose(0, 2, 1, 3)
-    text_h = lax.all_to_all(text_b, "row", 1, 1)
-    qkv_o = product_left(halves(full1_0, 1 - parity), qkv_grad_0)
-    qkv_o = qkv_o.reshape(rows, -1, 3 * wc).astype(BF)
+    qkv_p = product_left(full1_0, qkv_grad_0).astype(BF).reshape(rows, wr, 3 * wc)
+    out_p = by_row(attn_0, proj_g0).astype(BF)
+    parts = [qkv_p[:, :, :wc], qkv_p[:, :, wc : 2 * wc], qkv_p[:, :, 2 * wc :], out_p]
+    first_pairs = [
+        sum_pair(jnp.stack([parts[i], parts[2 + i]]).reshape(2, -1, wc), dps) for i in range(2)
+    ]
 
     def column_sums(values):
         return jnp.sum(values, axis=0, dtype=F32)
@@ -869,8 +1592,8 @@
             column_sums(proj_g0),
             column_sums(branch_g1) * first,
             (place * column_sums(proj_g1)[None]).reshape(-1),
-            column_sums(pre_g0),
-            (place * column_sums(pre_g1)[None]).reshape(-1),
+            pre_s0[0],
+            (place * pre_s1).reshape(-1),
             qkv_s0[:wc],
             qkv_s0[2 * wc :],
             qkv_s1[:wc],
@@ -878,29 +1601,32 @@
         ]
     ).reshape(-1, wc)
     pad_rows = -vectors.shape[0] % 8
-    qkv_grad_1, mixed1_g0, vectors = exchange(
+    qkv_grad_1, mixed1_g0, vectors, *sums = exchange(
         16,
-        35,
+        51,
         AllGatherRow(qkv_grad_t),
-        ReduceScatterCol(after(product_right(qkv_grad_0, qkv_0).astype(BF), qkv_o), 4),
+        ReduceScatterCol(product_right(qkv_grad_0, qkv_0).astype(BF), 4),
         AllGatherRow(jnp.pad(vectors, ((0, pad_rows), (0, 0)))),
-    )
-    qkv_b0 = add_partner(
-        qkv_o, product_left(halves(full1_0, parity), qkv_grad_0).reshape(rows, -1, 3 * wc)
-    )
+        ReduceScatterCol(branch_p1, 2),
+        first_pairs[0][0],
+        first_pairs[1][0],
+    )
+    wide_1, sums = sums[0], sums[1:]
+    first_ha = reduce_row(first_pairs[0][1](sums))
+    first_hb = reduce_row(first_pairs[1][1](sums[1:]))
     qkv_g1 = product_left(full1_1, qkv_grad_1)
     image_grad = resid_g0 + norm_local_back(mixed1_g0 * (1.0 + mod_0[1]), norm1_0, inv1_0)
-    mixed1_g1, branch_1, vectors, image_grad, image_out = exchange(
+    branch_1, down_b0, mixed1_g1, text_b, vectors, image_grad = exchange(
         17,
         37,
+        ReduceScatterRow(stack(wide_1.astype(BF), rows)),
+        AllGatherDp(jnp.concatenate([down_ha, down_hb]), dps),
         ReduceScatterCol(product_right(qkv_grad_1, qkv_1).astype(BF)),
-        ReduceScatterRow(stack(after(wide_1, out_b0, down_h0).astype(BF), rows)),
+        AllGatherDp(text_h, dps),
         AllGatherDp(jnp.sum(vectors.reshape(rows, -1, wc), axis=0), dps),
         FromSequence(image_grad.astype(BF)),
-        FromSequence((resid_0 + mod_0[5] * branch_0).astype(BF)),
     )
     vectors = jnp.sum(vectors.reshape(dps, -1, wc), axis=0).reshape(-1)
-    qkv_h0 = reduce_block(qkv_b0)
     branch_1 = branch_1 + down_b[1].astype(F32)
     text_out = (resid_1 + mod_1[5] * branch_1).astype(BF)[:TXT]
     norm1_g1 = mixed1_g1 * (1.0 + mod_1[1])
@@ -931,16 +1657,22 @@
             )
         ]
     )
-    stats, cols_0, cols_1 = exchange(
+    up_b0, stats, cols_0, cols_1 = exchange(
         18,
-        10,
+        15,
+        AllGatherDp(jnp.concatenate([up_ha, up_hb]), dps),
         AllGatherRow(row_stats(norm1_g1, norm1_g1 * norm1_1)),
         AllGatherCol(jnp.pad(sums_0, ((0, 2), (0, 0)))),
         AllGatherCol(jnp.pad(sums_1, ((0, 2), (0, 0)))),
     )
     image_grad = image_grad.astype(F32)
     text_grad = resid_g1 + norm_row_back(norm1_g1, norm1_1, inv1_1, stats)
-    rows_0 = exchange(19, 8, AllGatherRow(jnp.sum(cols_0.reshape(cols, 8, rows * wr), axis=0)))
+    qkv_b1, rows_0 = exchange(
+        19,
+        19,
+        AllGatherDp(qkv_g1.astype(BF), dps),
+        AllGatherRow(jnp.sum(cols_0.reshape(cols, 8, rows * wr), axis=0)),
+    )
     rows_0 = lax.dynamic_index_in_dim(
         rows_0.reshape(seqs, 8, rows, wr)[:, :6], row, 2, keepdims=False
     )
@@ -949,9 +1681,11 @@
     silu_part = product_right(mods_low[0], ada_w[0].reshape(wc, 6 * wr)) + product_right(
         mods_low[1], ada_w[1].reshape(wc, 6 * wr)
     )
-    mods_all, silu_all, silu_part = exchange(
+    firsts, out_b1, mods_all, silu_all, silu_part = exchange(
         20,
-        9,
+        20,
+        AllGatherDp(jnp.concatenate([first_ha, first_hb]), dps),
+        AllGatherDp(out_g1.astype(BF), dps),
         AllGatherDp(mods_low.reshape(2 * seqs, 6 * wr).astype(F32), dps),
         AllGatherDp(jnp.pad(silu_low.astype(F32), ((0, 8 - seqs), (0, 0))), dps),
         AllGatherRow(jnp.pad(silu_part, ((0, 8 - seqs), (0, 0)))),
@@ -972,15 +1706,17 @@
     up_gb = rest[: 2 * wf].reshape(2, wf)
     qkv_gb = rest[2 * wf :].reshape(2, 2, wc)
 
-    def finish(half_sum, second_part):
-        first_part = join_over_dp(half_sum, dps, parity)
-        return jnp.stack([first_part, sum_over_dp(second_part.astype(BF), dps)])
-
-    text_h = text_h.transpose(2, 0, 1, 3)
-    text_g = join_over_dp(text_h[None], dps, parity)
-    text_g = text_g.reshape(2, share // 2, 2, rows, wr).transpose(2, 3, 0, 1, 4).reshape(2, wf, wr)
-    up_g = jnp.stack([join_over_dp(up_h0, dps, parity), text_g[0].T])
-    down_g = jnp.stack([join_over_dp(down_h0, dps, parity), text_g[1]])
+    up_g, down_g = finish(
+        finish_feed_kernel, "finish_feed", [(2, wr, wf), (2, wf, wr)], up_b0, down_b0, text_b
+    )
+    qkv_g, out_g = finish(
+        functools.partial(finish_rest_kernel, dps),
+        "finish_rest",
+        [(2, wr, 3 * wc), (2, wc, wr)],
+        firsts,
+        qkv_b1,
+        out_b1,
+    )
 
     return (
         image_out,
@@ -990,9 +1726,9 @@
         condition_grad,
         ada_gw,
         ada_gb,
-        finish(qkv_h0, qkv_g1).reshape(2, wr, 3, wc),
+        qkv_g.reshape(2, wr, 3, wc),
         qkv_gb,
-        finish(out_h0, out_g1),
+        out_g,
         row_sums[:, 1],
         up_g,
         up_gb,

time: 1160 us -> 970 us (0.84)
  Pallas kernels: 612 us -> 768 us
  waiting for transfers between devices: 108 us -> 1.44 us
  matrix products: 139 us -> 34.8 us
  local copies, waits for them, and re-layouts: 138 us -> 69 us
  other arithmetic: 108 us -> 70 us
  starting transfers between devices: 28.7 us -> 1.17 us
    pallas_call x2 -> x5, Pallas kernels: 51.1 us -> 291 us  [the longest x1 146 us: back(): pl.pallas_call(kernel, in_specs=[vmem] * 19 + [hbm] * len(fars), out_spec...]
    pallas_call x19 -> x12, Pallas kernels: 561 us -> 477 us  [exchange(): pl.pallas_call(functools.partial(exchange_kernel, ops), in_specs=[pl.Bloc...]
    ppermute x16 -> x0, waiting for transfers between devices: 59.5 us -> none  [the longest x7 31.5 us: shifted(): lax.ppermute(values, 'dp', [(i, (i + step) % count) for i in range(count)])]
    all_to_all x2 -> x0, waiting for transfers between devices: 42.2 us -> none  [the longest x1 42.2 us: shards(): text_w = lax.all_to_all(text_w, 'row', 1, 1)]
    dot_general x10 -> x4, matrix products: 46.7 us -> 10 us  [product_right(): lax.dot_general(left, right, (((1,), (1,)), ((), ())), preferred_element_...]
    dot_general x10 -> x5, matrix products: 44.5 us -> 10.1 us  [product(): return jnp.dot(left, right, preferred_element_type=F32)]
    dot_general x16 -> x6, matrix products: 47.4 us -> 14.7 us  [product_left(): lax.dot_general(left, right, (((0,), (0,)), ((), ())), preferred_element_...]
    another operation x23 -> x3, other arithmetic: 36.8 us -> 4.63 us  [the longest x2 3.34 us: shards(): jnp.stack([parts[i], parts[2 + i]]).reshape(2, -1, wc)]
  transfers between devices with their start and end apart: 25 -> 12, of which waited for: 7 -> 0; matrix products, arithmetic and copies ran while one was open for 27% -> 13% of each run, Pallas kernels for 53% -> 41%
where the time goes in v2:
time: 970 us; the launch traced here: 961 us
  Pallas kernels  768 us (79%)
  other arithmetic  70 us (7%)
  local copies, waits for them, and re-layouts  69 us (7%)
  matrix products  34.8 us (4%)
  between operations  15.8 us (2%)
    pallas_call x12, Pallas kernels, exchange(): pl.pallas_call(functools.partial(exchange_kernel, ops), in_specs=[pl.Bloc...  477 us
    pallas_call x1, Pallas kernels, back(): pl.pallas_call(kernel, in_specs=[vmem] * 19 + [hbm] * len(fars), out_spec...  146 us
    pallas_call x1, Pallas kernels, feed(): pl.pallas_call(kernel, in_specs=[vmem] * 11 + [hbm] * 3, out_specs=[vmem]...  123 us
  transfers between devices with their start and end apart: 12, of which 0 were waited for; matrix products, arithmetic and copies ran while one was open for 13% of the time, Pallas kernels for 41%

profile of v2, /device:TPU:0, one launch (start us, length us, event | category | flops | bytes accessed | tf_op | source)
XLA Modules:
  0.0 960.7 jit_solution(13634113813960658828)
XLA Ops:
  7.2 1.9 slice_bitcast_fusion.3
  9.2 2.5 fusion.71
  11.7 2.1 copy.81
  13.8 2.4 copy.64
  16.2 2.6 fusion.32
  18.9 2.2 fusion.68
  21.7 2.9 copy.60
  24.6 2.3 copy.61
  29.7 8.5 exchange1.1
  40.7 50.9 %exchange2.1 = (bf16[256,1536]{1,0:T(8,128)(2,1)}, f32[128,384]{1,0:T(8,128)}, f32[32,160]{1,0:T(8,128)}) custom-call(bf16[1024,384]{1,0:T(8,128)(2,1)} %refs_0_.1, f32[32,384]{1,0:T(8,128)} %maximum_bitcast_fusion.refs_1_, f32[8,160]{1,0:T(8,128)} %select_maximum_fusion.2.refs_2_), custom_call_target="tpu_custom_call" | custom-call | bytes 105000000 | tf_op jit(solution)/shard_map/exchange2/pallas_call | solution.py:727
  91.7 1.6 convert_reduce_fusion.4
  98.3 2.1 copy.82
  100.5 41.1 %exchange3.1 = (bf16[640,384]{1,0:T(8,128)(2,1)}, bf16[1024,1536]{1,0:T(8,128)(2,1)}, bf16[256,1536]{1,0:T(8,128)(2,1)}) custom-call(bf16[160,384]{1,0:T(8,128)(2,1)} %add_convert_fusion.3.refs_0_, bf16[256,1536]{1,0:T(8,128)(2,1)} %fusion.12.refs_1_, bf16[1024,384]{1,0:T(8,128)(2,1)} %refs_2_.1), custom_call_target="tpu_custom_call" | custom-call | bytes 94500000 | tf_op jit(solution)/shard_map/exchange3/pallas_call | solution.py:727
  141.5 1.8 fusion.70
  145.1 2.1 convolution_convert_fusion.3.refs_4_
  148.2 64.4 %exchange4.1 = (bf16[3072,384]{1,0:T(8,128)(2,1)}, bf16[3072,384]{1,0:T(8,128)(2,1)}, f32[160,1152]{1,0:T(8,128)}, bf16[640,384]{1,0:T(8,128)(2,1)}, bf16[1024,1536]{1,0:T(8,128)(2,1)}) custom-call(bf16[1536,384]{1,0:T(8,128)(2,1)} %all-gather.7.cloned.1.call-done.refs_0_, bf16[384,384]{1,0:T(8,128)(2,1)} %get-tuple-element.289.refs_1_, ...), custom_call_target="tpu_custom_call" | custom-call | bytes 157500000 | tf_op jit(solution)/shard_map/exchange4/pallas_call | solution.py:727
  214.1 1.9 fusion.69
  219.0 2.4 copy.67
  225.2 1.4 constant_dynamic-slice_fusion.9
  231.4 11.1 %input_product.1 = (bf16[1024,1152]{1,0:T(8,128)(2,1)}, bf16[1536,1152]{1,0:T(8,128)(2,1)}, bf16[384,1536]{1,0:T(8,128)(2,1)}) custom-call(bf16[1024,1536]{1,0:T(8,128)(2,1)} %get-tuple-element.104.x, bf16[3072,384]{1,0:T(8,128)(2,1)} %get-tuple-element.105.part_a, bf16[3072,384]{1,0:T(8,128)(2,1)} %get-tuple-element.106.part_b, f32[1,1152]{1,0:T(1,128)} %bitcast.274), custom_call_target="tpu_custom_call" | custom-call | bytes 28000000 | tf_op jit(solution)/shard_map/input_product/pallas_call | solution.py:797
  242.6 42.0 %attend5.1 = (bf16[1024,384]{1,0:T(8,128)(2,1)}, bf16[160,384]{1,0:T(8,128)(2,1)}, f32[3,8,1024]{2,1,0:T(8,128)}, f32[3,8,160]{2,1,0:T(8,128)}, bf16[1536,384]{1,0:T(8,128)(2,1)}) custom-call(bf16[1024,1152]{1,0:T(8,128)(2,1)} %get-tuple-element.107.refs_0_.refs_12_, bf16[160,1152]{1,0:T(8,128)(2,1)} %add_convert_fusion.2.refs_1_.refs_13_, ...), custom_call_target="tpu_custom_call" | custom-call | bytes 91000000 | tf_op jit(solution)/shard_map/attend5/pallas_call | solution.py:727
  284.6 4.6 convolution_convert_fusion.1.refs_5_
  289.2 36.8 %exchange6.1 = (bf16[3072,384]{1,0:T(8,128)(2,1)}, bf16[640,384]{1,0:T(8,128)(2,1)}, bf16[640,1536]{1,0:T(8,128)(2,1)}) custom-call(bf16[1536,384]{1,0:T(8,128)(2,1)} %all-gather.13.cloned.1.call-done.refs_0_, bf16[384,384]{1,0:T(8,128)(2,1)} %get-tuple-element.283.refs_1_, bf16[160,384]{1,0:T(8,128)(2,1)} %get-tuple-element.110.refs_2_.refs_15_, ...), custom_call_target="tpu_custom_call" | custom-call | bytes 70000000 | tf_op jit(solution)/shard_map/exchange6/pallas_call | solution.py:727
  326.0 2.3 convolution_convert_fusion.6.refs_4_
  328.2 46.4 %exchange7.1 = (bf16[3072,384]{1,0:T(8,128)(2,1)}, bf16[3072,384]{1,0:T(8,128)(2,1)}, f32[160,384]{1,0:T(8,128)}, f32[256,1536]{1,0:T(8,128)}) custom-call(bf16[1536,384]{1,0:T(8,128)(2,1)} %all-gather.11.cloned.1.call-done.refs_0_, bf16[384,384]{1,0:T(8,128)(2,1)} %get-tuple-element.285.refs_1_, bf16[1536,384]{1,0:T(8,128)(2,1)} %get-tuple-element.108.refs_2_, ...), custom_call_target="tpu_custom_call" | custom-call | bytes 112000000 | tf_op jit(solution)/shard_map/exchange7/pallas_call | solution.py:727
  374.7 1.9 fusion.64
  378.7 122.8 %feed.1 = (f32[256,1536]{1,0:T(8,128)}, f32[160,1536]{1,0:T(8,128)}, f32[32,160]{1,0:T(8,128)}, f32[1,1536]{1,0:T(1,128)}, f32[1,384]{1,0:T(1,128)}, /*index=5*/...) custom-call(bf16[256,1536]{1,0:T(8,128)(2,1)} %add_convert_fusion.1., ...), custom_call_target="tpu_custom_call" | custom-call | bytes 315000000 | tf_op jit(solution)/shard_map/feed/pallas_call | solution.py:1082
  501.5 1.4 convert_element_type.207
  503.7 1.6 copy.70
  505.3 1.6 copy-done.13
  506.9 5.7 fusion.66
  512.7 1.7 fusion.5
  514.3 146.0 %back.1 = (f32[256,1536]{1,0:T(8,128)}, bf16[1024,1536]{1,0:T(8,128)(2,1)}, f32[160,384]{1,0:T(8,128)}, f32[160,384]{1,0:T(8,128)}, bf16[640,384]{1,0:T(8,128)(2...) custom-call(f32[256,1536]{1,0:T(8,128)} %get-tuple-element.124.refs_, ...), custom_call_target="tpu_custom_call" | custom-call | bytes 455000000 | tf_op jit(solution)/shard_map/back/pallas_call | solution.py:1304
  662.7 2.5 convert_reduce_fusion.1
  665.8 2.4 convert_reduce_fusion
  669.6 2.1 convert_reduce_fusion.2
  671.7 2.9 convolution_convert_fusion.5
  674.6 5.7 convolution_convert_fusion
  683.0 2.4 slice_bitcast_fusion
  685.5 1.7 pad_maximum_fusion.2
  687.1 1.7 pad_maximum_fusion.1
  690.1 5.6 convolution_convert_fusion.2.refs_1_
  695.7 65.2 %exchange16.1 = (bf16[640,1152]{1,0:T(8,128)(2,1)}, f32[256,1536]{1,0:T(8,128)}, f32[128,384]{1,0:T(8,128)}, f32[160,1536]{1,0:T(8,128)}, bf16[1536,384]{1,0:T(8,128)(2,1)}, /*index=5*/bf16[1536,384]{1,0:T(8,128)(2,1)}) custom-call(bf16[160,1152]{1,0:T(8,128)(2,1)} %get-tuple-element.134.refs_0_, bf16[1024,1536]{1,0:T(8,128)(2,1)} %convolution_convert_fusion.2.refs_1_, ...), custom_call_target="tpu_custom_call" | custom-call | bytes 178500000 | tf_op jit(solution)/shard_map/exchange16/pallas_call | solution.py:727
  764.1 2.1 fusion.18
  766.3 3.7 multiply_reduce_fusion.1
  770.7 2.2 convolution_convert_fusion.8.refs_1_
  772.9 3.2 convolution_convert_fusion.7.refs_2_
  776.2 1.8 convolution_convert_fusion.4.refs_0_
  778.1 1.9 pad_maximum_fusion.3.refs_1_
  780.0 46.6 %exchange17.1 = (f32[160,384]{1,0:T(8,128)}, bf16[1536,384]{1,0:T(8,128)(2,1)}, f32[160,384]{1,0:T(8,128)}, bf16[3072,384]{1,0:T(8,128)(2,1)}, f32[64,384]{1,0:T(8,128)}, /*index=5*/bf16[1024,384]{1,0:T(8,128)(2,1)}) custom-call(bf16[640,384]{1,0:T(8,128)(2,1)} %bitcast.238, bf16[768,384]{1,0:T(8,128)(2,1)} %pad_maximum_fusion.3.refs_1_, ...), custom_call_target="tpu_custom_call" | custom-call | bytes 129500000 | tf_op jit(solution)/shard_map/exchange17/pallas_call | solution.py:727
  827.6 1.7 multiply_reduce_fusion.4
  831.7 1.8 fusion.65
  834.7 2.1 pad_maximum_fusion.4.refs_0_
  836.8 23.6 %exchange18.1 = (bf16[1536,384]{1,0:T(8,128)(2,1)}, f32[32,160]{1,0:T(8,128)}, f32[32,1536]{1,0:T(8,128)}, f32[32,384]{1,0:T(8,128)}) custom-call(bf16[768,384]{1,0:T(8,128)(2,1)} %pad_maximum_fusion.4.refs_0_, f32[8,160]{1,0:T(8,128)} %select_maximum_fusion.1.refs_1_, f32[8,1536]{1,0:T(8,128)} %pad.56.refs_2_, f32[8,384]{1,0:T(8,128)} %pad.57.refs_3_), custom_call_target="tpu_custom_call" | custom-call | bytes 52500000 | tf_op jit(solution)/shard_map/exchange18/pallas_call | solution.py:727
  861.3 1.6 bitcast_reduce_fusion.refs_1_
  862.8 26.0 %exchange19.1 = (bf16[768,1152]{1,0:T(8,128)(2,1)}, f32[32,1536]{1,0:T(8,128)}) custom-call(bf16[384,1152]{1,0:T(8,128)(2,1)} %convolution_convert_fusion.4.refs_0_, f32[8,1536]{1,0:T(8,128)} %bitcast_reduce_fusion.refs_1_), custom_call_target="tpu_custom_call" | custom-call | bytes 66500000 | tf_op jit(solution)/shard_map/exchange19/pallas_call | solution.py:727
  894.4 2.0 pad_maximum_fusion.5.refs_0_
  896.4 25.7 %exchange20.1 = (bf16[1536,384]{1,0:T(8,128)(2,1)}, bf16[768,384]{1,0:T(8,128)(2,1)}, f32[16,2304]{1,0:T(8,128)}, f32[16,384]{1,0:T(8,128)}, f32[32,384]{1,0:T(8,128)}) custom-call(bf16[768,384]{1,0:T(8,128)(2,1)} %pad_maximum_fusion.5.refs_0_, bf16[384,384]{1,0:T(8,128)(2,1)} %convolution_convert_fusion.8.refs_1_, f32[8,2304]{1,0:T(8,128)} %bitcast.261, ...), custom_call_target="tpu_custom_call" | custom-call | bytes 70000000 | tf_op jit(solution)/shard_map/exchange20/pallas_call | solution.py:727
  928.5 4.5 finish_rest.1
  933.0 3.3 copy.76
  936.3 2.9 copy.77
  939.3 1.4 convolution_bitcast_fusion
  941.4 3.5 pad_maximum_fusion
  944.9 6.7 finish_feed.1
  (323 shorter events, 61.3 us)
Async XLA Ops:
  7.2 141.1 %all-gather.7.cloned.1.call-start = ((), (), s32[]{:S(2)}) async-start(), calls=%async_computation.6 | async-start | bytes 1474560 | tf_op jit(solution)/shard_map/all_gather | solution.py:67
  13.8 5.0 copy-start.3
  18.8 2.3 copy-start.55
  18.8 129.4 %all-gather.9.cloned.1.call-start = ((), (), s32[]{:S(2)}) async-start(), calls=%async_computation.7 | async-start | bytes 1474560 | tf_op jit(solution)/shard_map/all_gather | solution.py:67
  21.7 2.9 copy-start.8
  24.6 2.3 copy-start.48
  28.4 10.8 %copy-start.22 = (bf16[154,384]{1,0:T(8,128)(2,1)S(1)}, bf16[154,384]{1,0:T(8,128)(2,1)}, u32[]{:S(2)}) copy-start(bf16[154,384]{1,0:T(8,128)(2,1)} %param.16) | copy-start | bytes 354820
  28.4 11.0 %copy-start.58 = (bf16[2,384]{1,0:T(2,128)(2,1)S(1)}, bf16[2,384]{1,0:T(2,128)(2,1)}, u32[]{:S(2)}) copy-start(bf16[2,384]{1,0:T(2,128)(2,1)} %param.23) | copy-start | bytes 4612
  28.4 11.0 %copy-start.59 = (bf16[2,384]{1,0:T(2,128)(2,1)S(1)}, bf16[2,384]{1,0:T(2,128)(2,1)}, u32[]{:S(2)}) copy-start(bf16[2,384]{1,0:T(2,128)(2,1)} %param.27) | copy-start | bytes 4612
  28.4 11.6 %copy-start.47 = (f32[2,6,384]{2,1,0:T(8,128)S(1)}, f32[2,6,384]{2,1,0:T(8,128)}, u32[]{:S(2)}) copy-start(f32[2,6,384]{2,1,0:T(8,128)} %copy.62) | copy-start | bytes 55300
  91.6 3.5 copy-start.1
  91.6 6.7 copy-start.14
  91.7 197.5 %all-gather.13.cloned.1.call-start = ((), (), s32[]{:S(2)}) async-start(), calls=%async_computation.9 | async-start | bytes 1474560 | tf_op jit(solution)/shard_map/all_gather | solution.py:67
  95.1 5.3 copy-start.50
  95.1 5.3 copy-start.52
  144.4 2.8 copy-start.6
  212.7 115.6 %all-gather.11.cloned.1.call-start = ((), (), s32[]{:S(2)}) async-start(), calls=%async_computation.8 | async-start | bytes 1474560 | tf_op jit(solution)/shard_map/all_gather | solution.py:67
  213.2 165.5 %all-gather.15.cloned.1.call-start = ((), (), s32[]{:S(2)}) async-start(), calls=%async_computation.10 | async-start | bytes 1474560 | tf_op jit(solution)/shard_map/all_gather | solution.py:67
  217.2 161.5 %all-gather.17.cloned.1.call-start = ((), (), s32[]{:S(2)}) async-start(), calls=%async_computation.11 | async-start | bytes 1474560 | tf_op jit(solution)/shard_map/all_gather | solution.py:67
  218.4 3.7 copy-start.49
  218.4 4.8 copy-start.62
  228.1 2.2 copy-start.39
  231.1 546.9 %reduce-scatter.7.cloned.1.call-start = ((), (), s32[]{:S(2)}) async-start(), calls=%async_computation.12 | async-start | bytes 1474560 | tf_op jit(solution)/shard_map/reduce_scatter | solution.py:78
  242.6 42.0 %copy-start.26 = (bf16[384,1536]{1,0:T(8,128)(2,1)S(1)}, bf16[384,1536]{1,0:T(8,128)(2,1)}, u32[]{:S(2)}) copy-start(bf16[384,1536]{1,0:T(8,128)(2,1)} %get-tuple-element.114.refs_9_) | copy-start | bytes 3538948
  289.2 36.8 %copy-start.24 = (bf16[2,384,384]{2,1,0:T(8,128)(2,1)S(1)}, bf16[2,384,384]{2,1,0:T(8,128)(2,1)}, u32[]{:S(2)}) copy-start(bf16[2,384,384]{2,1,0:T(8,128)(2,1)} %param.22) | copy-start | bytes 1769476
  374.7 1.9 copy-start.31
  374.7 1.9 copy-start.56
  376.6 136.1 %copy-start = (f32[256,1536]{1,0:T(8,128)}, f32[256,1536]{1,0:T(8,128)S(1)}, u32[]{:S(2)}) copy-start(f32[256,1536]{1,0:T(8,128)S(1)} %get-tuple-element.257.refs_2_) | copy-start | bytes 4718596
  501.5 2.3 copy-start.21
  503.7 3.2 copy-start.13
  506.9 5.7 copy-start.7
  506.9 5.7 copy-start.11
  506.9 5.7 copy-start.23
  660.4 117.7 %reduce-scatter.9.cloned.1.call-start = ((), (), s32[]{:S(2)}) async-start(), calls=%async_computation.13 | async-start | bytes 1474560 | tf_op jit(solution)/shard_map/reduce_scatter | solution.py:78
  661.1 173.6 %reduce-scatter.11.cloned.1.call-start = ((), (), s32[]{:S(2)}) async-start(), calls=%async_computation.14 | async-start | bytes 1474560 | tf_op jit(solution)/shard_map/reduce_scatter | solution.py:78
  662.6 2.6 copy-start.64
  662.6 2.6 copy-start.61
  662.7 2.6 copy-start.43
  662.7 2.8 copy-start.5
  668.2 3.4 copy-start.18
  668.2 166.5 %reduce-scatter.13.cloned.1.call-start = ((), (), s32[]{:S(2)}) async-start(), calls=%async_computation.15 | async-start | bytes 1474560 | tf_op jit(solution)/shard_map/reduce_scatter | solution.py:78
  668.3 3.4 copy-start.36
  671.7 2.9 copy-start.17
  671.7 2.9 copy-start.19
  680.3 214.1 %reduce-scatter.15.cloned.1.call-start = ((), (), s32[]{:S(2)}) async-start(), calls=%async_computation.16 | async-start | bytes 1474560 | tf_op jit(solution)/shard_map/reduce_scatter | solution.py:78
  685.5 3.4 copy-start.65
  687.1 3.0 copy-start.20
  695.7 66.5 %copy-start.29 = (f32[160,384]{1,0:T(8,128)S(1)}, f32[160,384]{1,0:T(8,128)}, u32[]{:S(2)}) copy-start(f32[160,384]{1,0:T(8,128)} %get-tuple-element.152) | copy-start | bytes 737284
  695.7 66.5 %copy-start.32 = (f32[160,384]{1,0:T(8,128)S(1)}, f32[160,384]{1,0:T(8,128)}, u32[]{:S(2)}) copy-start(f32[160,384]{1,0:T(8,128)} %get-tuple-element.116) | copy-start | bytes 737284
  761.9 132.5 %reduce-scatter.17.cloned.1.call-start = ((), (), s32[]{:S(2)}) async-start(), calls=%async_computation.17 | async-start | bytes 1474560 | tf_op jit(solution)/shard_map/reduce_scatter | solution.py:78
  763.5 2.8 copy-start.10
  766.3 4.4 copy-start.42
  770.0 2.9 copy-start.16
  772.9 3.3 copy-start.41
  772.9 3.3 copy-start.66
  780.0 47.5 %copy-start.57 = (f32[384]{0:T(512)S(1)}, f32[384]{0:T(512)}, u32[]{:S(2)}) copy-start(f32[384]{0:T(512)} %convert_reduce_fusion.9) | copy-start | bytes 4612
  834.7 55.2 %copy-start.4 = (bf16[2,384,6,384]{3,1,2,0:T(8,128)(2,1)S(1)}, bf16[2,384,6,384]{3,1,2,0:T(8,128)(2,1)}, u32[]{:S(2)}) copy-start(bf16[2,384,6,384]{3,1,2,0:T(8,128)(2,1)} %param.18) | copy-start | bytes 10616836
  889.9 3.8 copy-start.33
  894.4 32.9 %copy-start.38 = (bf16[1024,384]{1,0:T(8,128)(2,1)S(1)}, bf16[1024,384]{1,0:T(8,128)(2,1)}, u32[]{:S(2)}) copy-start(bf16[1024,384]{1,0:T(8,128)(2,1)} %get-tuple-element.151) | copy-start | bytes 2359300
  944.9 6.8 copy-start.30
  944.9 6.8 copy-start.34
  944.9 6.8 copy-start.35
  944.9 6.8 copy-start.63
  944.9 7.6 copy-start.37
  (15 other events, 22.4 us)
Sparse Core Ops, SparseCore 0:
  18.9 55.1 all-gather.6
  91.8 54.2 all-gather.8
  212.8 31.7 all-gather.12
  246.0 45.2 all-gather.10
  292.7 38.8 all-gather.14
  333.0 32.5 all-gather.16
  660.5 30.9 reduce-scatter.6
  693.8 46.8 reduce-scatter.8
  743.0 36.6 reduce-scatter.10
  781.9 43.5 reduce-scatter.12
  827.8 32.8 reduce-scatter.14
  862.8 29.1 reduce-scatter.16

commit v3 on v2

--- a/solution.py
+++ b/solution.py
@@ -819,10 +819,10 @@
 
 
 def feed_kernel(ops, me, refs):
-    gather_0, sums_t, gather_r, gather_t, scatter_0, scatter_t, scatter_b, *swaps = ops
+    gather_0, sums_t, gather_r, gather_t, scatter_0, scatter_t, scatter_b, swap = ops
     ins, outs, scratch = refs
     (mixed_0, resid_t, mod_t, grad_0, grad_t, bias_0, bias_t) = ins[:7]
-    (down_a, own_a, down_b, own_b, up_a, up_b, text_p) = ins[7:]
+    (down_b, own_b, down_a, up_a, up_b, text_p) = ins[7:]
     (mixed_g0, wide_g1, stats_out, sum_0, sum_t, branch_0) = outs[:6]
     (gup, gdown, gtext, branch_t) = outs[6:]
     (full_0, up, down, hidden, pre_g, part_0, stage, text_w) = scratch[:8]
@@ -837,21 +837,18 @@
     refs_s0 = ((part_0,), (mixed_g0,), rest[8:14])
     refs_s1 = ((part_t,), (wide_g1,), rest[14:20])
     refs_sb = ((part_b,), (branch_0,), rest[20:26])
-    refs_sd = [
-        ((down_a, own_a), (down_all.at[0],), rest[26:28]),
-        ((down_b, own_b), (down_all.at[1],), rest[28:30]),
-    ]
-
-    for i, swap in enumerate(swaps):
-        swap.start(refs_sd[i], me)
+    refs_sd = ((down_b, own_b), (down_all,), rest[26:28])
+
+    swap.start(refs_sd, me)
     copies = block_copies(up, (up_a, up_b), w_sems, 0, False)
+    copies += block_copies(down, (down_a,), w_sems, 16, True)
     parity = lax.rem(dp, 2)
     for k in range(2):
         for r in range(4):
             for w in range(2):
                 at = text_w.at[w, pl.ds(k * 192, 192), pl.ds(r * 384, 384)]
                 source = text_p.at[pl.ds((k * 4 + r) * 384 + w * 192, 192)]
-                copies.append(pltpu.make_async_copy(source, at, w_sems.at[16 + 8 * k + 2 * r + w]))
+                copies.append(pltpu.make_async_copy(source, at, w_sems.at[24 + 8 * k + 2 * r + w]))
     for copy in copies:
         copy.start()
     gather_0.start(refs_g0, me)
@@ -874,12 +871,11 @@
     gather_r.start(refs_gr, me)
     for copy in copies:
         copy.wait()
-    for i, swap in enumerate(swaps):
-        swap.finish(refs_sd[i], me)
-        for k in range(2):
-            for r in range(4):
-                place = down.at[pl.ds((2 * k + i) * 384, 384), pl.ds(r * 384, 384)]
-                place[...] = down_all[i, pl.ds((k * 4 + r) * 384, 384), :]
+    swap.finish(refs_sd, me)
+    for k in range(2):
+        for r in range(4):
+            place = down.at[pl.ds((2 * k + 1) * 384, 384), pl.ds(r * 384, 384)]
+            place[...] = down_all[pl.ds((k * 4 + r) * 384, 384), :]
     sum_0[...] = jnp.zeros_like(sum_0)
     sum_t[...] = jnp.zeros_like(sum_t)
 
@@ -1054,7 +1050,6 @@
         ReduceScatterCol(shape(640, 1536), 2),
         ReduceScatterCol(shape(1024, 1536), 4),
         SwapBlocks(weights[0], weights[1]),
-        SwapBlocks(weights[2], weights[3]),
     )
 
     def kernel(*refs):
@@ -1064,7 +1059,7 @@
         for device in peers:
             pl.semaphore_signal(barrier, 1, device_id=device, device_id_type=MESH)
         pl.semaphore_wait(barrier, len(peers))
-        feed_kernel(ops, me, (refs[:14], refs[14:24], refs[24:]))
+        feed_kernel(ops, me, (refs[:13], refs[13:23], refs[23:]))
 
     outs = [
         shape(256, 1536, dtype=F32),
@@ -1081,7 +1076,7 @@
     vmem, hbm = pl.BlockSpec(memory_space=pltpu.VMEM), pl.BlockSpec(memory_space=pl.ANY)
     return pl.pallas_call(
         kernel,
-        in_specs=[vmem] * 11 + [hbm] * 3,
+        in_specs=[vmem] * 9 + [hbm] * 4,
         out_specs=[vmem] * 6 + [hbm] * 4,
         out_shape=outs,
         scratch_shapes=[
@@ -1104,7 +1099,7 @@
             pltpu.SemaphoreType.DMA((40,)),
             pltpu.SemaphoreType.DMA((2, 4)),
             pltpu.VMEM((1024, 1536), BF),
-            pltpu.VMEM((2, 3072, 384), BF),
+            pltpu.VMEM((3072, 384), BF),
         ]
         + [item for op in ops for item in op.scratch],
         compiler_params=pltpu.CompilerParams(
@@ -1466,26 +1461,27 @@
         for half in (parity, 1 - parity)
     )
     text_own = lax.dynamic_index_in_dim(text_own, row, 0, False).reshape(-1, wr)
-    attn_0, attn_text, log_0, log_1, text_w = exchange(
+    attn_0, attn_text, log_0, log_1, up_a, text_w = exchange(
         5,
         26,
         attend(qkv_img, qkv_txt),
+        up_0.swap(0, up_a),
         AllToAllRow(text_w.reshape(-1, wr)),
         name="attend",
     )
-    up_a, attn_1, branch_g1 = exchange(
+    up_b0, text_w, attn_1, branch_g1 = exchange(
         6,
-        20,
-        up_0.swap(0, up_a),
-        AllGatherRow(attn_text),
-        AllGatherCol(side(wide_g1, rows), 2),
-    )
-
-    up_b0, text_w, proj_1, proj_0 = exchange(
-        7,
         32,
         up_0.swap(1, up_b0),
         SwapBlocks(text_w, text_own),
+        AllGatherRow(attn_text),
+        AllGatherCol(side(wide_g1, rows), 2),
+    )
+
+    down_a, proj_1, proj_0 = exchange(
+        7,
+        27,
+        down_0.swap(0, down_a),
         ReduceScatterCol(product(attn_1, out_w[1]).astype(BF)),
         ReduceScatterCol(product(attn_0, out_0).astype(BF), 4),
     )
@@ -1508,10 +1504,9 @@
         branch_g1,
         up_b[:1].astype(F32),
         up_bias_1[None],
-        down_a,
-        down_0.other(0),
         down_b0,
         down_0.other(1),
+        down_a,
         up_a,
         up_b0,
         text_w,

time: 970 us -> 949 us (0.978)
  Pallas kernels: 768 us -> 740 us
    pallas_call x1, Pallas kernels: 123 us -> 98.5 us  [feed(): pl.pallas_call(kernel, in_specs=[vmem] * 9 + [hbm] * 4, out_specs=[vmem]...]
  transfers between devices with their start and end apart: 12 -> 12, of which waited for: 0 -> 2; matrix products, arithmetic and copies ran while one was open for 13% -> 13% of each run, Pallas kernels for 41% -> 42%
where the time goes in v3:
time: 949 us; the launch traced here: 940 us
  Pallas kernels  740 us (78%)
  other arithmetic  70.3 us (7%)
  local copies, waits for them, and re-layouts  68.9 us (7%)
  matrix products  34.8 us (4%)
  between operations  15.8 us (2%)
    pallas_call x12, Pallas kernels, exchange(): pl.pallas_call(functools.partial(exchange_kernel, ops), in_specs=[pl.Bloc...  472 us
    pallas_call x1, Pallas kernels, back(): pl.pallas_call(kernel, in_specs=[vmem] * 19 + [hbm] * len(fars), out_spec...  147 us
    pallas_call x1, Pallas kernels, feed(): pl.pallas_call(kernel, in_specs=[vmem] * 9 + [hbm] * 4, out_specs=[vmem]...  98.5 us
  transfers between devices with their start and end apart: 12, of which 2 were waited for; matrix products, arithmetic and copies ran while one was open for 13% of the time, Pallas kernels for 42%

profile of v3, /device:TPU:0, one launch (start us, length us, event | category | flops | bytes accessed | tf_op | source)
XLA Modules:
  0.0 939.9 jit_solution(703021227918976002)
XLA Ops:
  7.2 1.9 slice_bitcast_fusion.3
  9.2 2.5 fusion.71
  11.7 2.1 copy.81
  13.8 2.4 copy.64
  16.2 2.6 fusion.32
  18.9 2.2 fusion.68
  21.7 2.9 copy.60
  24.6 2.3 copy.61
  29.6 8.5 exchange1.1
  40.7 50.9 %exchange2.1 = (bf16[256,1536]{1,0:T(8,128)(2,1)}, f32[128,384]{1,0:T(8,128)}, f32[32,160]{1,0:T(8,128)}) custom-call(bf16[1024,384]{1,0:T(8,128)(2,1)} %refs_0_.1, f32[32,384]{1,0:T(8,128)} %maximum_bitcast_fusion.refs_1_, f32[8,160]{1,0:T(8,128)} %select_maximum_fusion.2.refs_2_), custom_call_target="tpu_custom_call" | custom-call | bytes 105000000 | tf_op jit(solution)/shard_map/exchange2/pallas_call | solution.py:727
  91.7 1.6 convert_reduce_fusion.4
  98.3 2.1 copy.82
  100.4 41.1 %exchange3.1 = (bf16[640,384]{1,0:T(8,128)(2,1)}, bf16[1024,1536]{1,0:T(8,128)(2,1)}, bf16[256,1536]{1,0:T(8,128)(2,1)}) custom-call(bf16[160,384]{1,0:T(8,128)(2,1)} %add_convert_fusion.3.refs_0_, bf16[256,1536]{1,0:T(8,128)(2,1)} %fusion.12.refs_1_, bf16[1024,384]{1,0:T(8,128)(2,1)} %refs_2_.1), custom_call_target="tpu_custom_call" | custom-call | bytes 94500000 | tf_op jit(solution)/shard_map/exchange3/pallas_call | solution.py:727
  141.5 1.8 fusion.70
  145.1 2.1 convolution_convert_fusion.3.refs_4_
  148.2 64.5 %exchange4.1 = (bf16[3072,384]{1,0:T(8,128)(2,1)}, bf16[3072,384]{1,0:T(8,128)(2,1)}, f32[160,1152]{1,0:T(8,128)}, bf16[640,384]{1,0:T(8,128)(2,1)}, bf16[1024,1536]{1,0:T(8,128)(2,1)}) custom-call(bf16[1536,384]{1,0:T(8,128)(2,1)} %all-gather.7.cloned.1.call-done.refs_0_, bf16[384,384]{1,0:T(8,128)(2,1)} %get-tuple-element.291.refs_1_, ...), custom_call_target="tpu_custom_call" | custom-call | bytes 157500000 | tf_op jit(solution)/shard_map/exchange4/pallas_call | solution.py:727
  214.2 1.9 fusion.69
  219.1 2.4 copy.67
  231.6 11.1 %input_product.1 = (bf16[1024,1152]{1,0:T(8,128)(2,1)}, bf16[1536,1152]{1,0:T(8,128)(2,1)}, bf16[384,1536]{1,0:T(8,128)(2,1)}) custom-call(bf16[1024,1536]{1,0:T(8,128)(2,1)} %get-tuple-element.106.x, bf16[3072,384]{1,0:T(8,128)(2,1)} %get-tuple-element.107.part_a, bf16[3072,384]{1,0:T(8,128)(2,1)} %get-tuple-element.108.part_b, f32[1,1152]{1,0:T(1,128)} %bitcast.274), custom_call_target="tpu_custom_call" | custom-call | bytes 28000000 | tf_op jit(solution)/shard_map/input_product/pallas_call | solution.py:797
  242.7 1.9 all-gather.15.cloned.1.call-done.refs_2_
  244.6 42.0 %attend5.1 = (bf16[1024,384]{1,0:T(8,128)(2,1)}, bf16[160,384]{1,0:T(8,128)(2,1)}, f32[3,8,1024]{2,1,0:T(8,128)}, f32[3,8,160]{2,1,0:T(8,128)}, bf16[3072,384]{1,0:T(8,128)(2,1)}, /*index=5*/bf16[1536,384]{1,0:T(8,128)(2,1)}) custom-call(bf16[1024,1152]{1,0:T(8,128)(2,1)} %get-tuple-element.109.refs_0_.refs_12_, ...), custom_call_target="tpu_custom_call" | custom-call | bytes 91000000 | tf_op jit(solution)/shard_map/attend5/pallas_call | solution.py:727
  286.7 5.7 all-gather.13.cloned.1.call-done.refs_0_
  292.4 50.6 %exchange6.1 = (bf16[3072,384]{1,0:T(8,128)(2,1)}, bf16[3072,384]{1,0:T(8,128)(2,1)}, bf16[640,384]{1,0:T(8,128)(2,1)}, bf16[640,1536]{1,0:T(8,128)(2,1)}) custom-call(bf16[1536,384]{1,0:T(8,128)(2,1)} %all-gather.13.cloned.1.call-done.refs_0_, bf16[384,384]{1,0:T(8,128)(2,1)} %get-tuple-element.287.refs_1_, bf16[1536,384]{1,0:T(8,128)(2,1)} %get-tuple-element.111.refs_2_, ...), custom_call_target="tpu_custom_call" | custom-call | bytes 112000000 | tf_op jit(solution)/shard_map/exchange6/pallas_call | solution.py:727
  343.0 2.3 convolution_convert_fusion.6.refs_2_
  345.3 4.6 convolution_convert_fusion.1.refs_3_
  349.9 28.8 %exchange7.1 = (bf16[3072,384]{1,0:T(8,128)(2,1)}, f32[160,384]{1,0:T(8,128)}, f32[256,1536]{1,0:T(8,128)}) custom-call(bf16[1536,384]{1,0:T(8,128)(2,1)} %all-gather.11.cloned.1.call-done.refs_0_, bf16[384,384]{1,0:T(8,128)(2,1)} %get-tuple-element.283.refs_1_, bf16[640,384]{1,0:T(8,128)(2,1)} %convolution_convert_fusion.6.refs_2_, ...), custom_call_target="tpu_custom_call" | custom-call | bytes 94500000 | tf_op jit(solution)/shard_map/exchange7/pallas_call | solution.py:727
  378.7 1.9 fusion.64
  382.7 98.5 %feed.1 = (f32[256,1536]{1,0:T(8,128)}, f32[160,1536]{1,0:T(8,128)}, f32[32,160]{1,0:T(8,128)}, f32[1,1536]{1,0:T(1,128)}, f32[1,384]{1,0:T(1,128)}, /*index=5*/...) custom-call(bf16[256,1536]{1,0:T(8,128)(2,1)} %add_convert_fusion.1., ...), custom_call_target="tpu_custom_call" | custom-call | bytes 315000000 | tf_op jit(solution)/shard_map/feed/pallas_call | solution.py:1077
  483.6 1.6 copy.70
  485.1 1.6 copy-done.13
  486.8 5.7 fusion.66
  492.5 1.7 fusion.5
  494.2 146.6 %back.1 = (f32[256,1536]{1,0:T(8,128)}, bf16[1024,1536]{1,0:T(8,128)(2,1)}, f32[160,384]{1,0:T(8,128)}, f32[160,384]{1,0:T(8,128)}, bf16[640,384]{1,0:T(8,128)(2...) custom-call(f32[256,1536]{1,0:T(8,128)} %get-tuple-element.126.refs_, ...), custom_call_target="tpu_custom_call" | custom-call | bytes 455000000 | tf_op jit(solution)/shard_map/back/pallas_call | solution.py:1299
  643.1 2.5 convert_reduce_fusion.1
  646.3 2.6 convert_reduce_fusion
  650.2 2.1 convert_reduce_fusion.2
  652.3 2.9 convolution_convert_fusion.5
  655.2 5.7 convolution_convert_fusion
  663.7 2.4 slice_bitcast_fusion
  666.1 1.7 pad_maximum_fusion.2
  667.8 1.7 pad_maximum_fusion.1
  670.8 5.6 convolution_convert_fusion.2.refs_1_
  676.4 63.9 %exchange16.1 = (bf16[640,1152]{1,0:T(8,128)(2,1)}, f32[256,1536]{1,0:T(8,128)}, f32[128,384]{1,0:T(8,128)}, f32[160,1536]{1,0:T(8,128)}, bf16[1536,384]{1,0:T(8,128)(2,1)}, /*index=5*/bf16[1536,384]{1,0:T(8,128)(2,1)}) custom-call(bf16[160,1152]{1,0:T(8,128)(2,1)} %get-tuple-element.136.refs_0_, bf16[1024,1536]{1,0:T(8,128)(2,1)} %convolution_convert_fusion.2.refs_1_, ...), custom_call_target="tpu_custom_call" | custom-call | bytes 178500000 | tf_op jit(solution)/shard_map/exchange16/pallas_call | solution.py:727
  743.5 2.1 fusion.18
  745.6 3.7 multiply_reduce_fusion.1
  750.0 2.2 convolution_convert_fusion.8.refs_1_
  752.3 3.2 convolution_convert_fusion.7.refs_2_
  755.5 1.8 convolution_convert_fusion.4.refs_0_
  757.4 1.9 pad_maximum_fusion.3.refs_1_
  759.4 47.0 %exchange17.1 = (f32[160,384]{1,0:T(8,128)}, bf16[1536,384]{1,0:T(8,128)(2,1)}, f32[160,384]{1,0:T(8,128)}, bf16[3072,384]{1,0:T(8,128)(2,1)}, f32[64,384]{1,0:T(8,128)}, /*index=5*/bf16[1024,384]{1,0:T(8,128)(2,1)}) custom-call(bf16[640,384]{1,0:T(8,128)(2,1)} %bitcast.238, bf16[768,384]{1,0:T(8,128)(2,1)} %pad_maximum_fusion.3.refs_1_, ...), custom_call_target="tpu_custom_call" | custom-call | bytes 129500000 | tf_op jit(solution)/shard_map/exchange17/pallas_call | solution.py:727
  807.4 1.7 multiply_reduce_fusion.4
  811.5 1.8 fusion.65
  814.6 2.1 pad_maximum_fusion.4.refs_0_
  816.6 23.3 %exchange18.1 = (bf16[1536,384]{1,0:T(8,128)(2,1)}, f32[32,160]{1,0:T(8,128)}, f32[32,1536]{1,0:T(8,128)}, f32[32,384]{1,0:T(8,128)}) custom-call(bf16[768,384]{1,0:T(8,128)(2,1)} %pad_maximum_fusion.4.refs_0_, f32[8,160]{1,0:T(8,128)} %select_maximum_fusion.1.refs_1_, f32[8,1536]{1,0:T(8,128)} %pad.56.refs_2_, f32[8,384]{1,0:T(8,128)} %pad.57.refs_3_), custom_call_target="tpu_custom_call" | custom-call | bytes 52500000 | tf_op jit(solution)/shard_map/exchange18/pallas_call | solution.py:727
  840.7 1.6 bitcast_reduce_fusion.refs_1_
  842.3 26.1 %exchange19.1 = (bf16[768,1152]{1,0:T(8,128)(2,1)}, f32[32,1536]{1,0:T(8,128)}) custom-call(bf16[384,1152]{1,0:T(8,128)(2,1)} %convolution_convert_fusion.4.refs_0_, f32[8,1536]{1,0:T(8,128)} %bitcast_reduce_fusion.refs_1_), custom_call_target="tpu_custom_call" | custom-call | bytes 66500000 | tf_op jit(solution)/shard_map/exchange19/pallas_call | solution.py:727
  873.9 2.0 pad_maximum_fusion.5.refs_0_
  875.9 25.6 %exchange20.1 = (bf16[1536,384]{1,0:T(8,128)(2,1)}, bf16[768,384]{1,0:T(8,128)(2,1)}, f32[16,2304]{1,0:T(8,128)}, f32[16,384]{1,0:T(8,128)}, f32[32,384]{1,0:T(8,128)}) custom-call(bf16[768,384]{1,0:T(8,128)(2,1)} %pad_maximum_fusion.5.refs_0_, bf16[384,384]{1,0:T(8,128)(2,1)} %convolution_convert_fusion.8.refs_1_, f32[8,2304]{1,0:T(8,128)} %bitcast.261, ...), custom_call_target="tpu_custom_call" | custom-call | bytes 70000000 | tf_op jit(solution)/shard_map/exchange20/pallas_call | solution.py:727
  907.8 4.4 finish_rest.1
  912.3 3.3 copy.76
  915.6 2.9 copy.77
  918.5 1.4 convolution_bitcast_fusion
  920.7 3.5 pad_maximum_fusion
  924.2 6.7 finish_feed.1
  (323 shorter events, 64.1 us)
Async XLA Ops:
  7.2 141.0 %all-gather.7.cloned.1.call-start = ((), (), s32[]{:S(2)}) async-start(), calls=%async_computation.6 | async-start | bytes 1474560 | tf_op jit(solution)/shard_map/all_gather | solution.py:67
  13.8 5.0 copy-start.3
  18.8 2.3 copy-start.55
  18.8 129.4 %all-gather.9.cloned.1.call-start = ((), (), s32[]{:S(2)}) async-start(), calls=%async_computation.7 | async-start | bytes 1474560 | tf_op jit(solution)/shard_map/all_gather | solution.py:67
  21.7 2.9 copy-start.8
  24.6 2.3 copy-start.48
  28.4 10.8 %copy-start.22 = (bf16[154,384]{1,0:T(8,128)(2,1)S(1)}, bf16[154,384]{1,0:T(8,128)(2,1)}, u32[]{:S(2)}) copy-start(bf16[154,384]{1,0:T(8,128)(2,1)} %param.16) | copy-start | bytes 354820
  28.4 10.9 %copy-start.58 = (bf16[2,384]{1,0:T(2,128)(2,1)S(1)}, bf16[2,384]{1,0:T(2,128)(2,1)}, u32[]{:S(2)}) copy-start(bf16[2,384]{1,0:T(2,128)(2,1)} %param.23) | copy-start | bytes 4612
  28.4 11.0 %copy-start.59 = (bf16[2,384]{1,0:T(2,128)(2,1)S(1)}, bf16[2,384]{1,0:T(2,128)(2,1)}, u32[]{:S(2)}) copy-start(bf16[2,384]{1,0:T(2,128)(2,1)} %param.27) | copy-start | bytes 4612
  28.4 11.6 %copy-start.47 = (f32[2,6,384]{2,1,0:T(8,128)S(1)}, f32[2,6,384]{2,1,0:T(8,128)}, u32[]{:S(2)}) copy-start(f32[2,6,384]{2,1,0:T(8,128)} %copy.62) | copy-start | bytes 55300
  91.6 3.5 copy-start.1
  91.6 6.7 copy-start.14
  91.6 153.0 %all-gather.15.cloned.1.call-start = ((), (), s32[]{:S(2)}) async-start(), calls=%async_computation.10 | async-start | bytes 1474560 | tf_op jit(solution)/shard_map/all_gather | solution.py:67
  95.1 5.3 copy-start.50
  95.1 5.3 copy-start.52
  144.4 2.8 copy-start.6
  212.7 79.6 %all-gather.13.cloned.1.call-start = ((), (), s32[]{:S(2)}) async-start(), calls=%async_computation.9 | async-start | bytes 1474560 | tf_op jit(solution)/shard_map/all_gather | solution.py:67
  213.3 136.5 %all-gather.11.cloned.1.call-start = ((), (), s32[]{:S(2)}) async-start(), calls=%async_computation.8 | async-start | bytes 1474560 | tf_op jit(solution)/shard_map/all_gather | solution.py:67
  217.3 165.5 %all-gather.17.cloned.1.call-start = ((), (), s32[]{:S(2)}) async-start(), calls=%async_computation.11 | async-start | bytes 1474560 | tf_op jit(solution)/shard_map/all_gather | solution.py:67
  218.5 3.7 copy-start.49
  218.5 4.9 copy-start.62
  228.3 2.2 copy-start.39
  231.3 526.1 %reduce-scatter.7.cloned.1.call-start = ((), (), s32[]{:S(2)}) async-start(), calls=%async_computation.12 | async-start | bytes 1474560 | tf_op jit(solution)/shard_map/reduce_scatter | solution.py:78
  292.4 50.6 %copy-start.24 = (bf16[2,384,384]{2,1,0:T(8,128)(2,1)S(1)}, bf16[2,384,384]{2,1,0:T(8,128)(2,1)}, u32[]{:S(2)}) copy-start(bf16[2,384,384]{2,1,0:T(8,128)(2,1)} %param.22) | copy-start | bytes 1769476
  292.4 52.9 %copy-start.26 = (bf16[384,1536]{1,0:T(8,128)(2,1)S(1)}, bf16[384,1536]{1,0:T(8,128)(2,1)}, u32[]{:S(2)}) copy-start(bf16[384,1536]{1,0:T(8,128)(2,1)} %get-tuple-element.116.refs_9_) | copy-start | bytes 3538948
  378.7 1.9 copy-start.31
  378.7 1.9 copy-start.56
  380.6 111.9 %copy-start = (f32[256,1536]{1,0:T(8,128)}, f32[256,1536]{1,0:T(8,128)S(1)}, u32[]{:S(2)}) copy-start(f32[256,1536]{1,0:T(8,128)S(1)} %get-tuple-element.259.refs_2_) | copy-start | bytes 4718596
  481.3 2.3 copy-start.21
  483.6 3.2 copy-start.13
  486.7 5.7 copy-start.7
  486.8 5.7 copy-start.11
  486.8 5.7 copy-start.23
  640.9 116.6 %reduce-scatter.9.cloned.1.call-start = ((), (), s32[]{:S(2)}) async-start(), calls=%async_computation.13 | async-start | bytes 1474560 | tf_op jit(solution)/shard_map/reduce_scatter | solution.py:78
  641.6 172.9 %reduce-scatter.11.cloned.1.call-start = ((), (), s32[]{:S(2)}) async-start(), calls=%async_computation.14 | async-start | bytes 1474560 | tf_op jit(solution)/shard_map/reduce_scatter | solution.py:78
  643.1 2.6 copy-start.64
  643.1 2.6 copy-start.61
  643.1 2.6 copy-start.43
  643.1 2.8 copy-start.5
  648.9 3.4 copy-start.18
  648.9 165.7 %reduce-scatter.13.cloned.1.call-start = ((), (), s32[]{:S(2)}) async-start(), calls=%async_computation.15 | async-start | bytes 1474560 | tf_op jit(solution)/shard_map/reduce_scatter | solution.py:78
  648.9 3.4 copy-start.36
  652.3 2.9 copy-start.17
  652.3 2.9 copy-start.19
  661.0 212.9 %reduce-scatter.15.cloned.1.call-start = ((), (), s32[]{:S(2)}) async-start(), calls=%async_computation.16 | async-start | bytes 1474560 | tf_op jit(solution)/shard_map/reduce_scatter | solution.py:78
  666.1 3.4 copy-start.65
  667.8 3.0 copy-start.20
  676.4 65.2 %copy-start.29 = (f32[160,384]{1,0:T(8,128)S(1)}, f32[160,384]{1,0:T(8,128)}, u32[]{:S(2)}) copy-start(f32[160,384]{1,0:T(8,128)} %get-tuple-element.154) | copy-start | bytes 737284
  676.4 65.2 %copy-start.32 = (f32[160,384]{1,0:T(8,128)S(1)}, f32[160,384]{1,0:T(8,128)}, u32[]{:S(2)}) copy-start(f32[160,384]{1,0:T(8,128)} %get-tuple-element.118) | copy-start | bytes 737284
  741.3 132.7 %reduce-scatter.17.cloned.1.call-start = ((), (), s32[]{:S(2)}) async-start(), calls=%async_computation.17 | async-start | bytes 1474560 | tf_op jit(solution)/shard_map/reduce_scatter | solution.py:78
  742.8 2.8 copy-start.10
  745.6 4.4 copy-start.42
  749.3 2.9 copy-start.16
  752.2 3.3 copy-start.41
  752.3 3.3 copy-start.66
  759.4 48.0 %copy-start.57 = (f32[384]{0:T(512)S(1)}, f32[384]{0:T(512)}, u32[]{:S(2)}) copy-start(f32[384]{0:T(512)} %convert_reduce_fusion.9) | copy-start | bytes 4612
  814.6 54.9 %copy-start.4 = (bf16[2,384,6,384]{3,1,2,0:T(8,128)(2,1)S(1)}, bf16[2,384,6,384]{3,1,2,0:T(8,128)(2,1)}, u32[]{:S(2)}) copy-start(bf16[2,384,6,384]{3,1,2,0:T(8,128)(2,1)} %param.18) | copy-start | bytes 10616836
  869.5 3.8 copy-start.33
  873.9 32.7 %copy-start.38 = (bf16[1024,384]{1,0:T(8,128)(2,1)S(1)}, bf16[1024,384]{1,0:T(8,128)(2,1)}, u32[]{:S(2)}) copy-start(bf16[1024,384]{1,0:T(8,128)(2,1)} %get-tuple-element.153) | copy-start | bytes 2359300
  924.1 6.8 copy-start.30
  924.2 6.8 copy-start.34
  924.2 6.8 copy-start.35
  924.2 6.8 copy-start.63
  924.2 7.6 copy-start.37
  (15 other events, 22.4 us)
Sparse Core Ops, SparseCore 0:
  18.9 55.1 all-gather.6
  91.8 54.2 all-gather.8
  212.9 31.7 all-gather.14
  246.0 46.2 all-gather.12
  293.8 36.3 all-gather.10
  331.6 31.6 all-gather.16
  641.0 29.9 reduce-scatter.6
  673.3 44.9 reduce-scatter.8
  720.6 38.6 reduce-scatter.10
  761.4 43.4 reduce-scatter.12
  807.2 32.7 reduce-scatter.14
  842.2 29.2 reduce-scatter.16
